TPU v7x, 512 devices: a whole 4x8x8 slice. The times are simulated.
512 devices in a mesh: items: 32 (over x, y), users: 16 (over z, core).
Axes of the slice: x: 4, y: 8, z: 8, core: 2. Of those that a mesh axis runs over, the one named last changes fastest.
Arguments:
- user_vectors: float32 [8192, 256], P('users'), may hold values from -64 to 64
- item_vectors: float32 [16384, 256], P(('items', 'users')), may hold values from -1 to 1
- item_counts: int32 [16384], P(('items', 'users')), may hold values from 0 to 1048575
- positive_ids: int32 [8192], P('users'), may hold values from 0 to 16383
Outputs:
- user_loss: float32 [8192], P('users')
- user_grad: float32 [8192, 256], P('users')
- item_grad: float32 [16384, 256], P(('items', 'users'))
All inputs are finite; a program needn't handle non-finite values.
Results may differ from a plain program's by a relative error of at most 0.0025.
Values sent between devices are 32-bit elements; how exact they have to be, the bound alone decides.
No kernel may reach another device: no remote copies, remote signals or barrier semaphores. Data moves between devices by JAX's collectives and lax.ppermute only.
A program may use at most 128 MiB of HBM per device.

v0:
```python
import math

import jax
import jax.numpy as jnp
from jax import lax
from jax.sharding import PartitionSpec as P

HIGH = lax.Precision.HIGHEST


def block_size(piece_rows):
    return math.gcd(piece_rows, 256)


def per_device(user_vectors, item_vectors, item_counts, positive_ids):
    user_rows = user_vectors.shape[0]
    embed_width = user_vectors.shape[1]
    own_items = item_vectors.shape[0]
    slab_items = own_items * lax.axis_size("users")
    group_base = lax.axis_index("items") * slab_items
    priors = jnp.log1p(item_counts.astype(jnp.float32))
    zero_rows = jnp.zeros((user_rows,), jnp.float32)
    zero_block = jnp.zeros((user_rows, embed_width), jnp.float32)
    starting = (
        jnp.full((user_rows,), -jnp.inf, jnp.float32),
        zero_rows,
        zero_block,
        zero_rows,
        zero_block,
    )
    item_piece = lax.all_gather(item_vectors, "users", axis=0, tiled=True)
    prior_piece = lax.all_gather(priors, "users", axis=0, tiled=True)
    block_rows = block_size(item_piece.shape[0])
    count_blocks = item_piece.shape[0] // block_rows

    def fold_one_block(block_index, state):
        highest, exp_total, weighted, positive_score, positive_row = state
        offset = block_index * block_rows
        item_block = lax.dynamic_slice_in_dim(item_piece, offset, block_rows, 0)
        prior_block = lax.dynamic_slice_in_dim(prior_piece, offset, block_rows, 0)
        scores = (
            jnp.dot(user_vectors, item_block.T, precision=HIGH, preferred_element_type=jnp.float32)
            - prior_block[None, :]
        )
        new_highest = jnp.maximum(highest, jnp.max(scores, axis=1))
        factor = jnp.exp(highest - new_highest)
        exponent_terms = jnp.exp(scores - new_highest[:, None])
        exp_total = exp_total * factor + jnp.sum(exponent_terms, axis=1)
        weighted = weighted * factor[:, None] + jnp.dot(
            exponent_terms, item_block, precision=HIGH, preferred_element_type=jnp.float32
        )
        local_ids = positive_ids - (group_base + offset)
        inside = (local_ids >= 0) & (local_ids < block_rows)
        clipped = jnp.clip(local_ids, 0, block_rows - 1)
        picked = jnp.take_along_axis(scores, clipped[:, None], axis=1)[:, 0]
        positive_score = positive_score + jnp.where(inside, picked, 0.0)
        positive_row = positive_row + jnp.where(
            inside[:, None], jnp.take(item_block, clipped, axis=0), 0.0
        )
        return (new_highest, exp_total, weighted, positive_score, positive_row)

    highest, exp_total, weighted, positive_score, positive_row = lax.fori_loop(
        0, count_blocks, fold_one_block, starting
    )
    global_max = lax.pmax(highest, "items")
    factor = jnp.exp(highest - global_max)
    exp_total, weighted, positive_score, positive_row = lax.psum(
        (exp_total * factor, weighted * factor[:, None], positive_score, positive_row), "items"
    )
    highest = global_max
    log_total = highest + jnp.log(exp_total)
    user_loss = log_total - positive_score
    user_grad = weighted / exp_total[:, None] - positive_row
    slab_item_piece, slab_prior_piece = lax.all_gather(
        (item_vectors, priors), "users", axis=0, tiled=True
    )
    piece_rows = slab_item_piece.shape[0]
    slab_block_rows = block_size(piece_rows)
    count_blocks = piece_rows // slab_block_rows
    items_blocked = slab_item_piece.reshape(count_blocks, slab_block_rows, embed_width)
    priors_blocked = slab_prior_piece.reshape(count_blocks, slab_block_rows)
    firsts = group_base + jnp.arange(count_blocks, dtype=jnp.int32) * slab_block_rows

    def slab_one_block(inputs):
        item_block, prior_block, block_first = inputs
        scores = (
            jnp.dot(user_vectors, item_block.T, precision=HIGH, preferred_element_type=jnp.float32)
            - prior_block[None, :]
        )
        probability = jnp.exp(scores - log_total[:, None])
        item_ids = block_first + jnp.arange(slab_block_rows, dtype=jnp.int32)
        target = (positive_ids[:, None] == item_ids[None, :]).astype(jnp.float32)
        return jnp.dot(
            (probability - target).T,
            user_vectors,
            precision=HIGH,
            preferred_element_type=jnp.float32,
        )

    gradient_terms = lax.map(slab_one_block, (items_blocked, priors_blocked, firsts)).reshape(
        piece_rows, embed_width
    )
    item_grad = lax.psum_scatter(gradient_terms, "users", scatter_dimension=0, tiled=True)
    return (user_loss, user_grad, item_grad)


def solution(mesh):
    placed = (P("users", None), P(("items", "users"), None), P(("items", "users")), P("users"))
    return jax.shard_map(
        per_device,
        mesh=mesh,
        in_specs=placed,
        out_specs=(P("users"), P("users", None), P(("items", "users"), None)),
        check_vma=False,
    )
```

profile of v0, /device:TPU:64, one launch (start us, length us, event | category | flops | bytes accessed | tf_op | source)
XLA Modules:
  0.0 312.8 jit_solution(10760638850874669612)
XLA Ops:
  8.1 21.9 %all_gather.8 = f32[512,256]{1,0:T(8,128)S(1)} all-gather(f32[32,256]{1,0:T(8,128)} %param.9), channel_id=1, replica_groups=mesh['items'=32,'users'=16] {'users'}, dimensions={0}, use_global_device_ids=true | all-gather | bytes 557056 | tf_op jit(solution)/shard_map/all_gather | solution.py:31
  30.0 1.3 dynamic-slice
  32.0 0.6 copy-done.4
  32.7 23.1 %all-reduce = f32[512]{0:T(512)S(1)} all-reduce(f32[512]{0:T(512)S(1)} %log-plus-one_dynamic-update-slice_fusion), channel_id=1, replica_groups=mesh['items'=32,'users'=16] {'users'}, use_global_device_ids=true, to_apply=%add | all-reduce | flops 512 | bytes 4096
  55.8 0.7 copy-done.3
  56.5 17.1 %while.33 = (s32[]{:T(128)}, f32[512]{0:T(512)S(1)}, f32[512]{0:T(512)S(1)}, f32[512,256]{1,0:T(8,128)S(1)}, f32[512]{0:T(512)S(1)}, /*index=5*/f32[512,256]{1,0...) while((s32[]{:T(128)}, f32[512]{0:T(512)S(1)}, ...), condition=%wide.region_3.0_spmd.clone, body=%wide.region_0.3_spmd.clone.sunk | while | flops 806898176 | bytes 6907116 | solution.py:62
  56.6 0.6 fusion.45
  57.3 4.5 %gather_fusion = f32[512]{0:T(512)S(1)} fusion(f32[512,256]{0,1:T(8,128)S(1)} %bitcast.73, s32[512]{0:T(512)S(1)} %bitcast.72), kind=kCustom, calls=%fused_computation.1.clone.clone.1 | custom fusion | bytes 8192 | tf_op jit(solution)/shard_map/while/body/eval_jaxpr/jit(take_along_axis)/gather | solution.py:55
  62.0 1.1 convolution_add_fusion.2
  63.2 1.6 gather_fusion.1
  65.1 0.6 fusion.45
  65.8 4.5 %gather_fusion = f32[512]{0:T(512)S(1)} fusion(f32[512,256]{0,1:T(8,128)S(1)} %bitcast.73, s32[512]{0:T(512)S(1)} %bitcast.72), kind=kCustom, calls=%fused_computation.1.clone.clone.1 | custom fusion | bytes 8192 | tf_op jit(solution)/shard_map/while/body/eval_jaxpr/jit(take_along_axis)/gather | solution.py:55
  70.6 1.1 convolution_add_fusion.2
  71.7 1.6 gather_fusion.1
  73.6 75.3 %pmax.7 = f32[512]{0:T(512)S(1)} all-reduce(f32[512]{0:T(512)S(1)} %get-tuple-element.233), channel_id=1, replica_groups=mesh['items'=32,'users'=16] {'items'}, use_global_device_ids=true, to_apply=%region_4.5 | all-reduce | flops 512 | bytes 4096 | tf_op jit(solution)/shard_map/pmax | solution.py:65
  148.9 1.0 broadcast_multiply_fusion
  149.9 69.8 %all-reduce.1 = (f32[512]{0:T(512)S(1)}, f32[512]{0:T(512)S(1)}) all-reduce(f32[512]{0:T(512)S(1)} %get-tuple-element.324, f32[512]{0:T(512)S(1)} %get-tuple-element.235), channel_id=1, replica_groups=mesh['items'=32,'users'=16] {'items'}, use_global_device_ids=true, to_apply=%region_5.6 | all-reduce | flops 1024 | bytes 8192 | tf_op jit(solution)/shard_map/psum | solution.py:67
  220.3 5.2 %while.32 = (s32[]{:T(128)}, f32[2,256,256]{2,1,0:T(8,128)S(1)}, f32[2,256,256]{2,1,0:T(8,128)S(1)}, f32[512,256]{1,0:T(8,128)S(1)}, f32[2,256]{1,0:T(2,128)S(1)...) while((s32[]{:T(128)}, f32[2,256,256]{2,1,0:T(8,128)S(1)}, ...), condition=%wide.region_10.11_spmd, body=%wide.region_9.10_spmd.sunk | while | flops 805961984 | bytes 2630785 | solution.py:100
  221.5 0.7 fusion.40
  222.9 0.6 dynamic_slice.41
  224.1 0.7 fusion.40
  225.5 0.8 copy-done.2
  226.3 76.9 %all-reduce.5.cloned.1.call-done = (f32[512,256]{1,0:T(8,128)}, f32[512,256]{1,0:T(8,128)}) async-done(((f32[512,256]{1,0:T(8,128)}, f32[512,256]{1,0:T(8,128)}), (f32[512,256]{1,0:T(8,128)}, f32[512,256]{1,0:T(8,128)})) %all-reduce.5.cloned.1.call-update) | async-done | bytes 1048592 | tf_op jit(solution)/shard_map/psum | solution.py:67
  303.2 2.1 divide_subtract_fusion
  (59 shorter events, 4.9 us)
Async XLA Ops:
  8.0 47.8 %copy-start = (f32[512,256]{1,0:T(8,128)S(1)}, f32[512,256]{1,0:T(8,128)}, u32[]{:S(2)}) copy-start(f32[512,256]{1,0:T(8,128)} %param.8) | copy-start | bytes 1572868
  8.0 295.2 %all-reduce.5.cloned.1.call-start = ((), (), s32[]{:S(2)}) async-start(), calls=%async_computation.2 | async-start | bytes 2097152 | tf_op jit(solution)/shard_map/psum | solution.py:67
  31.9 0.7 copy-start.4
  55.8 0.7 copy-start.3
  73.6 76.3 %copy-start.1 = (f32[512,256]{1,0:T(8,128)}, f32[512,256]{1,0:T(8,128)S(1)}, u32[]{:S(2)}) copy-start(f32[512,256]{1,0:T(8,128)S(1)} %get-tuple-element.237) | copy-start | bytes 1572868
  149.8 155.5 %reduce-scatter.2.cloned.1.call-start = ((), (), s32[]{:S(2)}) async-start(), calls=%async_computation.1 | async-start | bytes 557056 | tf_op jit(solution)/shard_map/reduce_scatter | solution.py:103
  225.5 0.8 copy-start.2
Sparse Core Ops, SparseCore 0:
  150.0 153.2 all-reduce.4
Sparse Core Ops, SparseCore 1:
  226.4 51.4 reduce-scatter.1
where the time goes:
time: 313 us
  blocking collectives  190 us (61%)
  waiting for transfers between devices  77 us (25%)
  local copies, waits for them, and re-layouts  17.1 us (5%)
  between operations  16.3 us (5%)
  matrix products  6.16 us (2%)
  other arithmetic  5.85 us (2%)
    psum x1, waiting for transfers between devices, per_device(): lax.psum((exp_total * factor, weighted * factor[:, None], positive_score,...  76.9 us
    pmax x1, blocking collectives, per_device(): global_max = lax.pmax(highest, 'items')  75.3 us
    psum x1, blocking collectives, per_device(): lax.psum((exp_total * factor, weighted * factor[:, None], positive_score,...  69.8 us
    unnamed x1, blocking collectives  23.1 us
    all_gather x1, blocking collectives, per_device(): item_piece = lax.all_gather(item_vectors, 'users', axis=0, tiled=True)  21.9 us
    gather x2, local copies, waits for them, and re-layouts, fold_one_block(): picked = jnp.take_along_axis(scores, clipped[:, None], axis=1)[:, 0]  9.1 us
  transfers between devices with their start and end apart: 2, of which 1 were waited for; matrix products, arithmetic and copies ran while one was open for 3% of the time, Pallas kernels for 0%

commit v1 on v0

v1 whole, which is shorter than its diff:
```python
import functools

import jax
import jax.numpy as jnp
from jax import lax
from jax.experimental import pallas as pl
from jax.experimental.pallas import tpu as pltpu
from jax.sharding import PartitionSpec as P

HIGH = lax.Precision.HIGHEST
GROUPS, MEMBERS = 32, 16
Z, CORES = 8, 2
E = 256
OWN = 32
PACK = OWN + 8
SLAB = MEMBERS * OWN
HALF = SLAB // CORES
ROWS = 512
SHARE = ROWS // GROUPS
SENT = 4 * SHARE + 8
VMEM_LIMIT = 48 * 1024 * 1024


def vmem():
    return pl.BlockSpec(memory_space=pltpu.VMEM)


def smem():
    return pl.BlockSpec(memory_space=pltpu.SMEM)


def f32(*shape):
    return jax.ShapeDtypeStruct(shape, jnp.float32)


def call(body, out_shape, operands, scalars=0, scratch=(), flops=0):
    single = not isinstance(out_shape, (tuple, list))
    outs = [out_shape] if single else list(out_shape)
    size = sum(o.size * 4 for o in operands) + sum(4 * s.size for s in outs)
    result = pl.pallas_call(
        body,
        out_shape=outs,
        in_specs=[smem()] * scalars + [vmem()] * (len(operands) - scalars),
        out_specs=[vmem()] * len(outs),
        scratch_shapes=list(scratch),
        compiler_params=pltpu.CompilerParams(vmem_limit_bytes=VMEM_LIMIT),
        cost_estimate=pl.CostEstimate(flops=flops, bytes_accessed=size, transcendentals=0),
    )(*operands)
    return result[0] if single else result


def dot(a, b, contract_a, contract_b):
    return lax.dot_general(
        a, b, (((contract_a,), (contract_b,)), ((), ())),
        precision=HIGH, preferred_element_type=jnp.float32,
    )


def pack_body(items, counts, out):
    out[0:OWN, :] = items[...]
    priors = jnp.log(1.0 + counts[...].astype(jnp.float32))
    out[OWN:PACK, :] = jnp.zeros((PACK - OWN, E), jnp.float32)
    out[OWN:OWN + 1, 0:OWN] = priors


def column_of(row):
    size = row.shape[1]
    eye = lax.broadcasted_iota(jnp.int32, (size, size), 0) == lax.broadcasted_iota(
        jnp.int32, (size, size), 1
    )
    return jnp.sum(jnp.where(eye, jnp.broadcast_to(row, (size, size)), 0.0), axis=1, keepdims=True)


def member_of(place, k):
    core = place[2] if k < Z else 1 - place[2]
    return k % Z * CORES + core


def hits(place, positive, k):
    rows = lax.broadcasted_iota(jnp.int32, (OWN, ROWS), 0)
    return rows == positive - (place[0] * SLAB + member_of(place, k) * OWN)


def score_body(place, users, packed, positive, items, scores, sent, share, target):
    priors = []
    for k in range(MEMBERS):
        first = pl.multiple_of(member_of(place, k) * PACK, 8)
        items[OWN * k:OWN * (k + 1), :] = packed[pl.ds(first, OWN), :]
        priors.append(column_of(packed[pl.ds(first + OWN, 8), :][0:1, 0:OWN]))
    raw = dot(items[...], users[...], 1, 1)
    wanted = positive[...]
    highest = None
    picked = jnp.zeros((OWN, ROWS), jnp.float32)
    for k in range(MEMBERS):
        at = slice(OWN * k, OWN * (k + 1))
        block = raw[at, :] - priors[k]
        scores[at, :] = block
        top = jnp.max(block, axis=0, keepdims=True)
        highest = top if k == 0 else jnp.maximum(highest, top)
        hit = hits(place, wanted, k)
        picked = picked + jnp.where(hit, block, 0.0)
        target[at, :] = jnp.where(hit, 1.0, 0.0).astype(jnp.bfloat16)
    total = jnp.sum(jnp.exp(scores[...] - highest), axis=0, keepdims=True)
    level = highest + jnp.log(total)
    picked = jnp.sum(picked, axis=0, keepdims=True)
    share[...] = jnp.exp(scores[...] - level)
    weighted = dot(share[...], items[...], 0, 0)
    rest, chosen = items[...], None
    for term in range(3):
        piece = rest.astype(jnp.bfloat16)
        rest = rest - piece.astype(jnp.float32)
        product = lax.dot_general(
            target[...], piece, (((0,), (0,)), ((), ())), preferred_element_type=jnp.float32
        )
        chosen = product if term == 0 else chosen + product
    for d in range(GROUPS):
        rows = slice(SHARE * d, SHARE * (d + 1))
        for part, value in enumerate((weighted, chosen)):
            for half in range(2):
                at = (2 * part + half) * SHARE
                sent[d, at:at + SHARE, :] = value[rows, 128 * half:128 * (half + 1)]
        for k in range(4):
            lanes = slice(128 * k, 128 * (k + 1))
            sent[d, 4 * SHARE + k:4 * SHARE + k + 1, :] = level[:, lanes]
            sent[d, 4 * SHARE + 4 + k:4 * SHARE + 5 + k, :] = picked[:, lanes]


def combine_body(place, got, loss, level, out, own):
    low = slice(4 * SHARE, 4 * SHARE + 4)
    highest = got[0, low, :]
    for d in range(1, GROUPS):
        highest = jnp.maximum(highest, got[d, low, :])
    total = jnp.zeros((4, 128), jnp.float32)
    picked = jnp.zeros((4, 128), jnp.float32)
    for d in range(GROUPS):
        total = total + jnp.exp(got[d, low, :] - highest)
        picked = picked + got[d, 4 * SHARE + 4:SENT, :]
    log_total = highest + jnp.log(total)
    loss[...] = log_total - picked
    level[...] = log_total
    row = place[0] * SHARE // 128
    lane = lax.rem(place[0] * SHARE, 128)
    here = lax.broadcasted_iota(jnp.int32, (SHARE, 128), 1) == (
        lax.broadcasted_iota(jnp.int32, (SHARE, 128), 0) + lane
    )
    own[0:4, :] = log_total
    base = own[pl.ds(row, 1), :]
    left = jnp.zeros((SHARE, 128), jnp.float32)
    right = jnp.zeros((SHARE, 128), jnp.float32)
    for d in range(GROUPS):
        part = jnp.exp(got[d, pl.ds(4 * SHARE + row, 1), :] - base)
        part = jnp.sum(jnp.where(here, part, 0.0), axis=1, keepdims=True)
        left = left + (part * got[d, 0:SHARE, :] - got[d, 2 * SHARE:3 * SHARE, :])
        right = right + (part * got[d, SHARE:2 * SHARE, :] - got[d, 3 * SHARE:4 * SHARE, :])
    for d in range(GROUPS):
        out[d, :, 0:128] = left
        out[d, :, 128:256] = right


def item_body(place, users, positive, scores, level, mine, theirs, grad):
    level = jnp.concatenate([level[k:k + 1, :] for k in range(4)], axis=1)
    wanted = positive[...]
    for k in range(MEMBERS):
        at = slice(OWN * k, OWN * (k + 1))
        hit = hits(place, wanted, k)
        grad[at, :] = jnp.exp(scores[at, :] - level) - jnp.where(hit, 1.0, 0.0)
    theirs[...] = dot(grad[HALF:SLAB, :], users[...], 1, 0)
    mine[...] = dot(grad[0:HALF, :], users[...], 1, 0)


def halve_body(shift, place, a, b, keep, send, both):
    both[...] = a[...] + b[...]
    bit = lax.rem(lax.shift_right_logical(place[1], shift), 2)
    for k in range(keep.shape[0] // OWN):
        at = slice(OWN * k, OWN * (k + 1))
        keep[at, :] = both[pl.ds(pl.multiple_of((2 * k + bit) * OWN, OWN), OWN), :]
        send[at, :] = both[pl.ds(pl.multiple_of((2 * k + 1 - bit) * OWN, OWN), OWN), :]


def sum_body(a, b, out):
    out[...] = a[...] + b[...]


def exchange(value, axis):
    return lax.all_to_all(value, axis, split_axis=0, concat_axis=0, tiled=True)


def swap(value, flip_z, flip_core):
    pairs = [
        (z * CORES + c, (z ^ flip_z) * CORES + (c ^ flip_core))
        for z in range(Z)
        for c in range(CORES)
    ]
    return lax.ppermute(value, "users", pairs)


def per_device(user_vectors, item_vectors, item_counts, positive_ids):
    member = lax.axis_index("users")
    place = jnp.stack([lax.axis_index("items"), member // CORES, member % CORES]).astype(jnp.int32)
    positive = positive_ids.reshape(1, ROWS)
    product = 2 * ROWS * SLAB * E

    packed = call(pack_body, f32(PACK, E), (item_vectors, item_counts.reshape(1, OWN)))
    packed = lax.all_gather(packed, "users", axis=0, tiled=True)
    items, scores, sent = call(
        score_body, (f32(SLAB, E), f32(SLAB, ROWS), f32(GROUPS, SENT, 128)),
        (place, user_vectors, packed, positive), scalars=1, flops=3 * product,
        scratch=[pltpu.VMEM((SLAB, ROWS), jnp.float32), pltpu.VMEM((SLAB, ROWS), jnp.bfloat16)],
    )
    got = exchange(sent, "items")
    loss, level, spread = call(
        combine_body, (f32(4, 128), f32(4, 128), f32(GROUPS, SHARE, E)), (place, got),
        scalars=1, scratch=[pltpu.VMEM((8, 128), jnp.float32)],
    )
    user_grad = exchange(spread, "items").reshape(ROWS, E)
    mine, theirs = call(
        item_body, (f32(HALF, E), f32(HALF, E)), (place, user_vectors, positive, scores, level),
        scalars=1, scratch=[pltpu.VMEM((SLAB, ROWS), jnp.float32)], flops=product,
    )
    arrived = swap(theirs, 0, 1)
    for shift in range(3):
        size = HALF >> (shift + 1)
        mine, theirs = call(
            functools.partial(halve_body, shift), (f32(size, E), f32(size, E)),
            (place, mine, arrived), scalars=1, scratch=[pltpu.VMEM((2 * size, E), jnp.float32)],
        )
        arrived = swap(theirs, 1 << shift, 0)
    item_grad = call(sum_body, f32(OWN, E), (mine, arrived))
    return (loss.reshape(ROWS), user_grad, item_grad)


def solution(mesh):
    placed = (P("users", None), P(("items", "users"), None), P(("items", "users")), P("users"))
    return jax.shard_map(
        per_device,
        mesh=mesh,
        in_specs=placed,
        out_specs=(P("users"), P("users", None), P(("items", "users"), None)),
        check_vma=False,
    )
```

time: 313 us -> 115 us (0.37)
  the two profiles are of different devices: /device:TPU:64 before, /device:TPU:2 now
where the time goes in v1:
time: 115 us
  blocking collectives  66.8 us (58%)
  waiting for transfers between devices  18.4 us (16%)
  starting transfers between devices  14.8 us (13%)
  Pallas kernels  9.86 us (9%)
  local copies, waits for them, and re-layouts  3.93 us (3%)
    all_to_all x1, blocking collectives, exchange(): return lax.all_to_all(value, axis, split_axis=0, concat_axis=0, tiled=True)  41.8 us
    all_gather x1, blocking collectives, per_device(): packed = lax.all_gather(packed, 'users', axis=0, tiled=True)  24.9 us
    ppermute x4, waiting for transfers between devices, swap(): return lax.ppermute(value, 'users', pairs)  18.4 us
    pallas_call x8, Pallas kernels, call(): pl.pallas_call(body, out_shape=outs, in_specs=[smem()] * scalars + [vmem(...  9.86 us
    ppermute x4, starting transfers between devices, swap(): return lax.ppermute(value, 'users', pairs)  9.6 us
    all_to_all x1, starting transfers between devices, exchange(): return lax.all_to_all(value, axis, split_axis=0, concat_axis=0, tiled=True)  5.24 us
    unnamed x13, local copies, waits for them, and re-layouts  3.93 us
  transfers between devices with their start and end apart: 5, of which 4 were waited for; matrix products, arithmetic and copies ran while one was open for 0% of the time, Pallas kernels for 4%

profile of v1, /device:TPU:2, one launch (start us, length us, event | category | flops | bytes accessed | tf_op | source)
XLA Modules:
  0.0 114.7 jit_solution(529288385291077275)
XLA Ops:
  0.7 0.7 copy-done.2
  1.4 0.7 copy-done.5
  2.1 24.9 %all_gather.3.packed = f32[640,256]{1,0:T(8,128)S(1)} all-gather(f32[40,256]{1,0:T(8,128)S(1)} %shard_map.67), channel_id=1, replica_groups=mesh['items'=32,'users'=16] {'users'}, dimensions={0}, use_global_device_ids=true | all-gather | bytes 696320 | tf_op jit(solution)/shard_map/all_gather | solution.py:204
  27.0 0.1 pad_add_fusion.place
  27.1 1.0 copy-done
  28.1 0.7 copy-done.3
  28.8 4.1 %shard_map.68 = (f32[512,256]{1,0:T(8,128)}, f32[512,512]{1,0:T(8,128)S(1)}, f32[32,72,128]{2,1,0:T(8,128)S(1)}) custom-call(s32[3]{0:T(128)S(1)} %pad_add_fusion.place, f32[512,256]{1,0:T(8,128)S(1)} %copy-done, f32[640,256]{1,0:T(8,128)S(1)} %all_gather.3.packed, s32[1,512]{1,0:T(1,128)S(1)} %bitcast.7), custom_call_target="tpu_custom_call" | custom-call | flops 402653184 | bytes 3934220 | tf_op jit(solution)/shard_map/pallas_call | solution.py:40
  32.9 41.8 %all_to_all.10.got = f32[32,72,128]{2,1,0:T(8,128)S(1)} all-to-all(f32[32,72,128]{2,1,0:T(8,128)S(1)} %get-tuple-element.16), channel_id=1, replica_groups=mesh['items'=32,'users'=16] {'items'}, dimensions={0} | all-to-all | bytes 2359296 | tf_op jit(solution)/shard_map/all_to_all | solution.py:185
  74.8 1.6 %shard_map.69 = (f32[4,128]{1,0:T(4,128)}, f32[4,128]{1,0:T(4,128)S(1)}, f32[32,16,256]{2,1,0:T(8,128)}) custom-call(s32[3]{0:T(128)S(1)} %pad_add_fusion.place, f32[32,72,128]{2,1,0:T(8,128)S(1)} %all_to_all.10.got), custom_call_target="tpu_custom_call" | custom-call | bytes 1708044 | tf_op jit(solution)/shard_map/pallas_call | solution.py:40
  76.4 5.2 %all-to-all-start.1 = ((f32[32,16,256]{2,1,0:T(8,128)}), f32[32,16,256]{2,1,0:T(8,128)S(1)}, u32[]{:S(2)}, u32[]{:S(2)}) async-start(f32[32,16,256]{2,1,0:T(8,128)} %get-tuple-element.18), calls=%async_computation.1 | async-start | bytes 1048576 | tf_op jit(solution)/shard_map/all_to_all | solution.py:185
  81.7 1.8 %shard_map.70 = (f32[256,256]{1,0:T(8,128)S(1)}, f32[256,256]{1,0:T(8,128)S(1)}) custom-call(s32[3]{0:T(128)S(1)} %pad_add_fusion.place, f32[512,256]{1,0:T(8,128)S(1)} %copy-done.1, s32[1,512]{1,0:T(1,128)S(1)} %bitcast.8, f32[512,512]{1,0:T(8,128)S(1)} %get-tuple-element.19.scores, f32[4,128]{1,0:T(4,128)S(1)} %get-tuple-element.20.level), custom_call_target="tpu_custom_call" | custom-call | flops 134217728 | bytes 2101260 | tf_op jit(solution)/shard_map/pallas_call | solution.py:40
  83.5 1.9 %collective-permute-start = (f32[256,256]{1,0:T(8,128)S(1)}, f32[256,256]{1,0:T(8,128)S(1)}, u32[]{:S(2)}, u32[]{:S(2)}) collective-permute-start(f32[256,256]{1,0:T(8,128)S(1)} %get-tuple-element.22), channel_id=1, source_target_pairs={{0,1},{1,0},{2,3},{3,2},{4,5},{5,4},{6,7},{7,6},{8,9},{9,8},{10,11... | collective-permute-start | bytes 786440 | tf_op jit(solution)/shard_map/ppermute | solution.py:194
  85.4 1.5 %collective-permute-done.b = f32[256,256]{1,0:T(8,128)S(1)} collective-permute-done((f32[256,256]{1,0:T(8,128)S(1)}, f32[256,256]{1,0:T(8,128)S(1)}, u32[]{:S(2)}, u32[]{:S(2)}) %collective-permute-start) | collective-permute-done | bytes 262176 | tf_op jit(solution)/shard_map/ppermute | solution.py:194
  86.9 0.6 shard_map.71
  87.5 1.9 %collective-permute-start.1 = (f32[128,256]{1,0:T(8,128)S(1)}, f32[128,256]{1,0:T(8,128)S(1)}, u32[]{:S(2)}, u32[]{:S(2)}) collective-permute-start(f32[128,256]{1,0:T(8,128)S(1)} %get-tuple-element.24), channel_id=1, source_target_pairs={{0,2},{1,3},{2,0},{3,1},{4,6},{5,7},{6,4},{7,5},{8,10},{9,11},{10,... | collective-permute-start | bytes 393224 | tf_op jit(solution)/shard_map/ppermute | solution.py:194
  89.4 5.5 %collective-permute-done.1.b = f32[128,256]{1,0:T(8,128)S(1)} collective-permute-done((f32[128,256]{1,0:T(8,128)S(1)}, f32[128,256]{1,0:T(8,128)S(1)}, u32[]{:S(2)}, u32[]{:S(2)}) %collective-permute-start.1) | collective-permute-done | bytes 131104 | tf_op jit(solution)/shard_map/ppermute | solution.py:194
  94.9 0.6 shard_map.72
  95.5 2.2 %collective-permute-start.2 = (f32[64,256]{1,0:T(8,128)S(1)}, f32[64,256]{1,0:T(8,128)S(1)}, u32[]{:S(2)}, u32[]{:S(2)}) collective-permute-start(f32[64,256]{1,0:T(8,128)S(1)} %get-tuple-element.26), channel_id=1, source_target_pairs={{0,4},{1,5},{2,6},{3,7},{4,0},{5,1},{6,2},{7,3},{8,12},{9,13},{10,... | collective-permute-start | bytes 196616 | tf_op jit(solution)/shard_map/ppermute | solution.py:194
  97.7 5.3 %collective-permute-done.2.b = f32[64,256]{1,0:T(8,128)S(1)} collective-permute-done((f32[64,256]{1,0:T(8,128)S(1)}, f32[64,256]{1,0:T(8,128)S(1)}, u32[]{:S(2)}, u32[]{:S(2)}) %collective-permute-start.2) | collective-permute-done | bytes 65568 | tf_op jit(solution)/shard_map/ppermute | solution.py:194
  103.0 0.6 shard_map.73
  103.6 3.6 %collective-permute-start.3 = (f32[32,256]{1,0:T(8,128)S(1)}, f32[32,256]{1,0:T(8,128)S(1)}, u32[]{:S(2)}, u32[]{:S(2)}) collective-permute-start(f32[32,256]{1,0:T(8,128)S(1)} %get-tuple-element.28), channel_id=1, source_target_pairs={{0,8},{1,9},{2,10},{3,11},{4,12},{5,13},{6,14},{7,15},{8,0},{9,1},... | collective-permute-start | bytes 98312 | tf_op jit(solution)/shard_map/ppermute | solution.py:194
  107.2 6.1 %collective-permute-done.3.b = f32[32,256]{1,0:T(8,128)S(1)} collective-permute-done((f32[32,256]{1,0:T(8,128)S(1)}, f32[32,256]{1,0:T(8,128)S(1)}, u32[]{:S(2)}, u32[]{:S(2)}) %collective-permute-start.3) | collective-permute-done | bytes 32800 | tf_op jit(solution)/shard_map/ppermute | solution.py:194
  113.3 0.6 shard_map.74
  113.9 0.8 copy.8
  (10 shorter events, 0.0 us)
Async XLA Ops:
  0.6 0.8 copy-start.2
  1.4 0.7 copy-start.5
  27.1 1.0 copy-start
  28.1 0.7 copy-start.3
  74.8 6.9 %copy-start.1 = (f32[512,256]{1,0:T(8,128)S(1)}, f32[512,256]{1,0:T(8,128)}, u32[]{:S(2)}) copy-start(f32[512,256]{1,0:T(8,128)} %users.3) | copy-start | bytes 1572868
  74.8 6.9 %copy-start.4 = (s32[512]{0:T(512)S(1)}, s32[512]{0:T(512)}, u32[]{:S(2)}) copy-start(s32[512]{0:T(512)} %param.7) | copy-start | bytes 6148
  76.4 37.5 %all-to-all-start.1 = ((f32[32,16,256]{2,1,0:T(8,128)}), f32[32,16,256]{2,1,0:T(8,128)S(1)}, u32[]{:S(2)}, u32[]{:S(2)}) async-start(f32[32,16,256]{2,1,0:T(8,128)} %get-tuple-element.18), calls=%async_computation.1 | async-start | bytes 1048576 | tf_op jit(solution)/shard_map/all_to_all | solution.py:185
  83.5 3.4 %collective-permute-start = (f32[256,256]{1,0:T(8,128)S(1)}, f32[256,256]{1,0:T(8,128)S(1)}, u32[]{:S(2)}, u32[]{:S(2)}) collective-permute-start(f32[256,256]{1,0:T(8,128)S(1)} %get-tuple-element.22), channel_id=1, source_target_pairs={{0,1},{1,0},{2,3},{3,2},{4,5},{5,4},{6,7},{7,6},{8,9},{9,8},{10,11... | collective-permute-start | bytes 786440 | tf_op jit(solution)/shard_map/ppermute | solution.py:194
  87.5 7.4 %collective-permute-start.1 = (f32[128,256]{1,0:T(8,128)S(1)}, f32[128,256]{1,0:T(8,128)S(1)}, u32[]{:S(2)}, u32[]{:S(2)}) collective-permute-start(f32[128,256]{1,0:T(8,128)S(1)} %get-tuple-element.24), channel_id=1, source_target_pairs={{0,2},{1,3},{2,0},{3,1},{4,6},{5,7},{6,4},{7,5},{8,10},{9,11},{10,... | collective-permute-start | bytes 393224 | tf_op jit(solution)/shard_map/ppermute | solution.py:194
  95.5 7.5 %collective-permute-start.2 = (f32[64,256]{1,0:T(8,128)S(1)}, f32[64,256]{1,0:T(8,128)S(1)}, u32[]{:S(2)}, u32[]{:S(2)}) collective-permute-start(f32[64,256]{1,0:T(8,128)S(1)} %get-tuple-element.26), channel_id=1, source_target_pairs={{0,4},{1,5},{2,6},{3,7},{4,0},{5,1},{6,2},{7,3},{8,12},{9,13},{10,... | collective-permute-start | bytes 196616 | tf_op jit(solution)/shard_map/ppermute | solution.py:194
  103.6 9.7 %collective-permute-start.3 = (f32[32,256]{1,0:T(8,128)S(1)}, f32[32,256]{1,0:T(8,128)S(1)}, u32[]{:S(2)}, u32[]{:S(2)}) collective-permute-start(f32[32,256]{1,0:T(8,128)S(1)} %get-tuple-element.28), channel_id=1, source_target_pairs={{0,8},{1,9},{2,10},{3,11},{4,12},{5,13},{6,14},{7,15},{8,0},{9,1},... | collective-permute-start | bytes 98312 | tf_op jit(solution)/shard_map/ppermute | solution.py:194

commit v2 on v1

v2 whole, which is shorter than its diff:
```python
import functools

import jax
import jax.numpy as jnp
from jax import lax
from jax.experimental import pallas as pl
from jax.experimental.pallas import tpu as pltpu
from jax.sharding import PartitionSpec as P

HIGH = lax.Precision.HIGHEST
GROUPS, MEMBERS = 32, 16
Z, CORES = 8, 2
E = 256
OWN = 32
PACK = OWN + 8
SLAB = MEMBERS * OWN
HALF = SLAB // CORES
ROWS = 512
SHARE = ROWS // GROUPS
VMEM_LIMIT = 48 * 1024 * 1024


def vmem():
    return pl.BlockSpec(memory_space=pltpu.VMEM)


def smem():
    return pl.BlockSpec(memory_space=pltpu.SMEM)


def f32(*shape):
    return jax.ShapeDtypeStruct(shape, jnp.float32)


def call(body, out_shape, operands, scalars=0, scratch=(), flops=0, after=()):
    single = not isinstance(out_shape, (tuple, list))
    outs = [out_shape] if single else list(out_shape)
    size = sum(o.size * 4 for o in operands) + sum(4 * s.size for s in outs)
    last = len(operands)
    result = pl.pallas_call(
        (lambda *refs: body(*refs[:last], *refs[last + len(after):])) if after else body,
        out_shape=outs,
        in_specs=[smem()] * scalars + [vmem()] * (len(operands) - scalars)
        + [pl.BlockSpec(memory_space=pl.ANY)] * len(after),
        out_specs=[vmem()] * len(outs),
        scratch_shapes=list(scratch),
        compiler_params=pltpu.CompilerParams(vmem_limit_bytes=VMEM_LIMIT),
        cost_estimate=pl.CostEstimate(flops=flops, bytes_accessed=size, transcendentals=0),
    )(*operands, *after)
    return result[0] if single else result


def dot(a, b, contract_a, contract_b):
    return lax.dot_general(
        a, b, (((contract_a,), (contract_b,)), ((), ())),
        precision=HIGH, preferred_element_type=jnp.float32,
    )


def pack_body(items, counts, out):
    out[0:OWN, :] = items[...]
    priors = jnp.log(1.0 + counts[...].astype(jnp.float32))
    out[OWN:PACK, :] = jnp.zeros((PACK - OWN, E), jnp.float32)
    out[OWN:OWN + 1, 0:OWN] = priors


def column_of(row):
    size = row.shape[1]
    eye = lax.broadcasted_iota(jnp.int32, (size, size), 0) == lax.broadcasted_iota(
        jnp.int32, (size, size), 1
    )
    return jnp.sum(jnp.where(eye, jnp.broadcast_to(row, (size, size)), 0.0), axis=1, keepdims=True)


def member_of(place, k):
    core = place[2] if k < Z else 1 - place[2]
    return k % Z * CORES + core


def hits(place, positive, k):
    rows = lax.broadcasted_iota(jnp.int32, (OWN, ROWS), 0)
    return rows == positive - (place[0] * SLAB + member_of(place, k) * OWN)


def score_body(place, users, packed, positive, items, scores, stats):
    priors = []
    for k in range(MEMBERS):
        first = pl.multiple_of(member_of(place, k) * PACK, 8)
        items[OWN * k:OWN * (k + 1), :] = packed[pl.ds(first, OWN), :]
        priors.append(column_of(packed[pl.ds(first + OWN, 8), :][0:1, 0:OWN]))
    raw = dot(items[...], users[...], 1, 1)
    wanted = positive[...]
    highest = None
    picked = jnp.zeros((OWN, ROWS), jnp.float32)
    for k in range(MEMBERS):
        at = slice(OWN * k, OWN * (k + 1))
        block = raw[at, :] - priors[k]
        scores[at, :] = block
        top = jnp.max(block, axis=0, keepdims=True)
        highest = top if k == 0 else jnp.maximum(highest, top)
        picked = picked + jnp.where(hits(place, wanted, k), block, 0.0)
    total = jnp.sum(jnp.exp(scores[...] - highest), axis=0, keepdims=True)
    level = highest + jnp.log(total)
    picked = jnp.sum(picked, axis=0, keepdims=True)
    for k in range(4):
        lanes = slice(128 * k, 128 * (k + 1))
        stats[0, k:k + 1, :] = level[:, lanes]
        stats[0, 4 + k:5 + k, :] = picked[:, lanes]
    one = stats[0, :, :]
    for d in range(1, GROUPS):
        stats[d, :, :] = one


def user_body(place, items, positive, scores, stats, loss, grad, user_part):
    highest = stats[0, 0:4, :]
    for d in range(1, GROUPS):
        highest = jnp.maximum(highest, stats[d, 0:4, :])
    total = jnp.zeros((4, 128), jnp.float32)
    picked = jnp.zeros((4, 128), jnp.float32)
    for d in range(GROUPS):
        total = total + jnp.exp(stats[d, 0:4, :] - highest)
        picked = picked + stats[d, 4:8, :]
    log_total = highest + jnp.log(total)
    loss[...] = log_total - picked
    level = jnp.concatenate([log_total[k:k + 1, :] for k in range(4)], axis=1)
    wanted = positive[...]
    for k in range(MEMBERS):
        at = slice(OWN * k, OWN * (k + 1))
        hit = hits(place, wanted, k)
        grad[at, :] = jnp.exp(scores[at, :] - level) - jnp.where(hit, 1.0, 0.0)
    user_part[...] = dot(grad[...], items[...], 0, 0)


def item_body(users, grad, mine, theirs):
    theirs[...] = dot(grad[HALF:SLAB, :], users[...], 1, 0)
    mine[...] = dot(grad[0:HALF, :], users[...], 1, 0)


def add_spread_body(parts, out):
    total = parts[0]
    for r in range(1, parts.shape[0]):
        total = total + parts[r]
    for r in range(out.shape[0]):
        out[r] = total


def halve_body(shift, place, a, b, keep, send, both):
    both[...] = a[...] + b[...]
    bit = lax.rem(lax.shift_right_logical(place[1], shift), 2)
    for k in range(keep.shape[0] // OWN):
        at = slice(OWN * k, OWN * (k + 1))
        keep[at, :] = both[pl.ds(pl.multiple_of((2 * k + bit) * OWN, OWN), OWN), :]
        send[at, :] = both[pl.ds(pl.multiple_of((2 * k + 1 - bit) * OWN, OWN), OWN), :]


def sum_body(a, b, out):
    out[...] = a[...] + b[...]


def exchange(value, axis):
    return lax.all_to_all(value, axis, split_axis=0, concat_axis=0, tiled=True)


def swap(value, flip_z, flip_core):
    pairs = [
        (z * CORES + c, (z ^ flip_z) * CORES + (c ^ flip_core))
        for z in range(Z)
        for c in range(CORES)
    ]
    return lax.ppermute(value, "users", pairs)


def per_device(user_vectors, item_vectors, item_counts, positive_ids):
    member = lax.axis_index("users")
    place = jnp.stack([lax.axis_index("items"), member // CORES, member % CORES]).astype(jnp.int32)
    positive = positive_ids.reshape(1, ROWS)
    product = 2 * ROWS * SLAB * E

    packed = call(pack_body, f32(PACK, E), (item_vectors, item_counts.reshape(1, OWN)))
    packed = lax.all_gather(packed, "users", axis=0, tiled=True)
    items, scores, stats = call(
        score_body, (f32(SLAB, E), f32(SLAB, ROWS), f32(GROUPS, 8, 128)),
        (place, user_vectors, packed, positive), scalars=1, flops=product,
    )
    stats = exchange(stats, "items")
    loss, grad, user_part = call(
        user_body, (f32(4, 128), f32(SLAB, ROWS), f32(ROWS, E)),
        (place, items, positive, scores, stats), scalars=1, flops=product,
    )
    parts = exchange(user_part.reshape(GROUPS, SHARE, E), "items")
    mine, theirs = call(item_body, (f32(HALF, E), f32(HALF, E)), (user_vectors, grad), flops=product)
    arrived = swap(theirs, 0, 1)
    for shift in range(3):
        size = HALF >> (shift + 1)
        mine, theirs = call(
            functools.partial(halve_body, shift), (f32(size, E), f32(size, E)),
            (place, mine, arrived), scalars=1, scratch=[pltpu.VMEM((2 * size, E), jnp.float32)],
        )
        arrived = swap(theirs, 1 << shift, 0)
        if shift == 0:
            spread = call(add_spread_body, f32(GROUPS, SHARE, E), (parts,), after=(arrived,))
            user_grad = exchange(spread, "items").reshape(ROWS, E)
    item_grad = call(sum_body, f32(OWN, E), (mine, arrived))
    return (loss.reshape(ROWS), user_grad, item_grad)


def solution(mesh):
    placed = (P("users", None), P(("items", "users"), None), P(("items", "users")), P("users"))
    return jax.shard_map(
        per_device,
        mesh=mesh,
        in_specs=placed,
        out_specs=(P("users"), P("users", None), P(("items", "users"), None)),
        check_vma=False,
    )
```

time: 115 us -> 101 us (0.88)
  blocking collectives: 66.8 us -> 44.6 us
  starting transfers between devices: 14.8 us -> 22 us
  waiting for transfers between devices: 18.4 us -> 20.9 us
  local copies, waits for them, and re-layouts: 3.93 us -> 2.78 us
    all_to_all x1, blocking collectives: 41.8 us -> 19.7 us  [exchange(): return lax.all_to_all(value, axis, split_axis=0, concat_axis=0, tiled=True)]
    all_to_all x1 -> x2, starting transfers between devices: 5.24 us -> 12.4 us  [exchange(): return lax.all_to_all(value, axis, split_axis=0, concat_axis=0, tiled=True)]
    all_to_all x1 -> x2, waiting for transfers between devices: 0.01 us -> 2.49 us  [exchange(): return lax.all_to_all(value, axis, split_axis=0, concat_axis=0, tiled=True)]
    unnamed x13 -> x9, local copies, waits for them, and re-layouts: 3.93 us -> 2.78 us
    pallas_call x8 -> x9, Pallas kernels: 9.86 us -> 8.93 us  [call(): pl.pallas_call((lambda *refs: body(*refs[:last], *refs[last + len(after):...]
  transfers between devices with their start and end apart: 5 -> 6, of which waited for: 4 -> 5; matrix products, arithmetic and copies ran while one was open for 0% -> 0% of each run, Pallas kernels for 4% -> 3%
where the time goes in v2:
time: 101 us; the launch traced here: 100 us
  blocking collectives  44.6 us (44%)
  starting transfers between devices  22 us (22%)
  waiting for transfers between devices  20.9 us (21%)
  Pallas kernels  8.93 us (9%)
  local copies, waits for them, and re-layouts  2.78 us (3%)
    all_gather x1, blocking collectives, per_device(): packed = lax.all_gather(packed, 'users', axis=0, tiled=True)  24.9 us
    all_to_all x1, blocking collectives, exchange(): return lax.all_to_all(value, axis, split_axis=0, concat_axis=0, tiled=True)  19.7 us
    ppermute x4, waiting for transfers between devices, swap(): return lax.ppermute(value, 'users', pairs)  18.4 us
    all_to_all x2, starting transfers between devices, exchange(): return lax.all_to_all(value, axis, split_axis=0, concat_axis=0, tiled=True)  12.4 us
    ppermute x4, starting transfers between devices, swap(): return lax.ppermute(value, 'users', pairs)  9.62 us
    pallas_call x9, Pallas kernels, call(): pl.pallas_call((lambda *refs: body(*refs[:last], *refs[last + len(after):...  8.93 us
    unnamed x9, local copies, waits for them, and re-layouts  2.78 us
    all_to_all x2, waiting for transfers between devices, exchange(): return lax.all_to_all(value, axis, split_axis=0, concat_axis=0, tiled=True)  2.49 us
  transfers between devices with their start and end apart: 6, of which 5 were waited for; matrix products, arithmetic and copies ran while one was open for 0% of the time, Pallas kernels for 3%

profile of v2, /device:TPU:2, one launch (start us, length us, event | category | flops | bytes accessed | tf_op | source)
XLA Modules:
  0.0 100.1 jit_solution(8960725582805456492)
XLA Ops:
  0.7 0.7 copy-done.1
  1.4 0.7 copy-done.3
  2.1 24.9 %all_gather.3.packed = f32[640,256]{1,0:T(8,128)S(1)} all-gather(f32[40,256]{1,0:T(8,128)S(1)} %shard_map.67), channel_id=1, replica_groups=mesh['items'=32,'users'=16] {'users'}, dimensions={0}, use_global_device_ids=true | all-gather | bytes 696320 | tf_op jit(solution)/shard_map/all_gather | solution.py:180
  27.1 0.6 copy-done.2
  27.7 1.9 %shard_map.68 = (f32[512,256]{1,0:T(8,128)S(1)}, f32[512,512]{1,0:T(8,128)S(1)}, f32[32,8,128]{2,1,0:T(8,128)S(1)}) custom-call(s32[3]{0:T(128)S(1)} %pad_add_fusion.place, f32[512,256]{1,0:T(8,128)S(1)} %copy-done, f32[640,256]{1,0:T(8,128)S(1)} %all_gather.3.packed, s32[1,512]{1,0:T(1,128)S(1)} %bitcast.8), custom_call_target="tpu_custom_call" | custom-call | flops 134217728 | bytes 2885644 | tf_op jit(solution)/shard_map/pallas_call | solution.py:40
  29.6 19.7 %all_to_all.15.stats = f32[32,8,128]{2,1,0:T(8,128)S(1)} all-to-all(f32[32,8,128]{2,1,0:T(8,128)S(1)} %get-tuple-element.19), channel_id=1, replica_groups=mesh['items'=32,'users'=16] {'items'}, dimensions={0} | all-to-all | bytes 262144 | tf_op jit(solution)/shard_map/all_to_all | solution.py:161
  49.3 2.8 %shard_map.69 = (f32[4,128]{1,0:T(4,128)}, f32[512,512]{1,0:T(8,128)S(1)}, f32[512,256]{1,0:T(8,128)}) custom-call(s32[3]{0:T(128)S(1)} %pad_add_fusion.place, f32[512,256]{1,0:T(8,128)S(1)} %get-tuple-element.17.items, s32[1,512]{1,0:T(1,128)S(1)} %bitcast.9, f32[512,512]{1,0:T(8,128)S(1)} %get-tuple-element.18.scores, f32[32,8,128]{2,1,0:T(8,128)S(1)} %all_to_all.15.stats), custom_call_target="tpu_custom_call" | custom-call | flops 134217728 | bytes 3280908 | tf_op jit(solution)/shard_map/pallas_call | solution.py:40
  52.1 5.0 %all-to-all-start.1 = ((f32[32,16,256]{2,1,0:T(8,128)}), f32[32,16,256]{2,1,0:T(8,128)S(1)}, u32[]{:S(2)}, u32[]{:S(2)}) async-start(f32[32,16,256]{2,1,0:T(8,128)} %bitcast.6), calls=%async_computation.1 | async-start | bytes 1048576 | tf_op jit(solution)/shard_map/all_to_all | solution.py:161
  57.1 1.0 %shard_map.70 = (f32[256,256]{1,0:T(8,128)S(1)}, f32[256,256]{1,0:T(8,128)S(1)}) custom-call(f32[512,256]{1,0:T(8,128)S(1)} %copy-done, f32[512,512]{1,0:T(8,128)S(1)} %get-tuple-element.22.grad), custom_call_target="tpu_custom_call" | custom-call | flops 134217728 | bytes 2097152 | tf_op jit(solution)/shard_map/pallas_call | solution.py:40
  58.1 1.9 %collective-permute-start = (f32[256,256]{1,0:T(8,128)S(1)}, f32[256,256]{1,0:T(8,128)S(1)}, u32[]{:S(2)}, u32[]{:S(2)}) collective-permute-start(f32[256,256]{1,0:T(8,128)S(1)} %get-tuple-element.24), channel_id=1, source_target_pairs={{0,1},{1,0},{2,3},{3,2},{4,5},{5,4},{6,7},{7,6},{8,9},{9,8},{10,11... | collective-permute-start | bytes 786440 | tf_op jit(solution)/shard_map/ppermute | solution.py:170
  60.0 1.5 %collective-permute-done.b = f32[256,256]{1,0:T(8,128)S(1)} collective-permute-done((f32[256,256]{1,0:T(8,128)S(1)}, f32[256,256]{1,0:T(8,128)S(1)}, u32[]{:S(2)}, u32[]{:S(2)}) %collective-permute-start) | collective-permute-done | bytes 262176 | tf_op jit(solution)/shard_map/ppermute | solution.py:170
  61.5 0.6 shard_map.71
  62.1 1.9 %collective-permute-start.1 = (f32[128,256]{1,0:T(8,128)S(1)}, f32[128,256]{1,0:T(8,128)S(1)}, u32[]{:S(2)}, u32[]{:S(2)}) collective-permute-start(f32[128,256]{1,0:T(8,128)S(1)} %get-tuple-element.25), channel_id=1, source_target_pairs={{0,2},{1,3},{2,0},{3,1},{4,6},{5,7},{6,4},{7,5},{8,10},{9,11},{10,... | collective-permute-start | bytes 393224 | tf_op jit(solution)/shard_map/ppermute | solution.py:170
  64.0 5.5 %collective-permute-done.1.refs_1_.b = f32[128,256]{1,0:T(8,128)S(1)} collective-permute-done((f32[128,256]{1,0:T(8,128)S(1)}, f32[128,256]{1,0:T(8,128)S(1)}, u32[]{:S(2)}, u32[]{:S(2)}) %collective-permute-start.1) | collective-permute-done | bytes 131104 | tf_op jit(solution)/shard_map/ppermute | solution.py:170
  69.5 2.5 %all-to-all-done.1.refs_0_ = f32[32,16,256]{2,1,0:T(8,128)S(1)} async-done(((f32[32,16,256]{2,1,0:T(8,128)}), f32[32,16,256]{2,1,0:T(8,128)S(1)}, u32[]{:S(2)}, u32[]{:S(2)}) %all-to-all-start.1) | async-done | bytes 524320 | tf_op jit(solution)/shard_map/all_to_all | solution.py:161
  72.0 0.9 shard_map.72
  72.9 7.4 %all-to-all-start.2 = ((f32[32,16,256]{2,1,0:T(8,128)}), f32[32,16,256]{2,1,0:T(8,128)S(1)}, u32[]{:S(2)}, u32[]{:S(2)}) async-start(f32[32,16,256]{2,1,0:T(8,128)} %shard_map.72), calls=%async_computation.2 | async-start | bytes 1048576 | tf_op jit(solution)/shard_map/all_to_all | solution.py:161
  80.3 0.6 shard_map.73
  80.9 2.2 %collective-permute-start.2 = (f32[64,256]{1,0:T(8,128)S(1)}, f32[64,256]{1,0:T(8,128)S(1)}, u32[]{:S(2)}, u32[]{:S(2)}) collective-permute-start(f32[64,256]{1,0:T(8,128)S(1)} %get-tuple-element.28), channel_id=1, source_target_pairs={{0,4},{1,5},{2,6},{3,7},{4,0},{5,1},{6,2},{7,3},{8,12},{9,13},{10,... | collective-permute-start | bytes 196616 | tf_op jit(solution)/shard_map/ppermute | solution.py:170
  83.0 5.3 %collective-permute-done.2.b = f32[64,256]{1,0:T(8,128)S(1)} collective-permute-done((f32[64,256]{1,0:T(8,128)S(1)}, f32[64,256]{1,0:T(8,128)S(1)}, u32[]{:S(2)}, u32[]{:S(2)}) %collective-permute-start.2) | collective-permute-done | bytes 65568 | tf_op jit(solution)/shard_map/ppermute | solution.py:170
  88.9 3.6 %collective-permute-start.3 = (f32[32,256]{1,0:T(8,128)S(1)}, f32[32,256]{1,0:T(8,128)S(1)}, u32[]{:S(2)}, u32[]{:S(2)}) collective-permute-start(f32[32,256]{1,0:T(8,128)S(1)} %get-tuple-element.30), channel_id=1, source_target_pairs={{0,8},{1,9},{2,10},{3,11},{4,12},{5,13},{6,14},{7,15},{8,0},{9,1},... | collective-permute-start | bytes 98312 | tf_op jit(solution)/shard_map/ppermute | solution.py:170
  92.5 6.1 %collective-permute-done.3.b = f32[32,256]{1,0:T(8,128)S(1)} collective-permute-done((f32[32,256]{1,0:T(8,128)S(1)}, f32[32,256]{1,0:T(8,128)S(1)}, u32[]{:S(2)}, u32[]{:S(2)}) %collective-permute-start.3) | collective-permute-done | bytes 32800 | tf_op jit(solution)/shard_map/ppermute | solution.py:170
  98.6 0.6 shard_map.75
  99.3 0.8 copy.8
  (9 shorter events, 0.7 us)
Async XLA Ops:
  0.6 0.8 copy-start.1
  0.6 26.4 %copy-start = (f32[512,256]{1,0:T(8,128)S(1)}, f32[512,256]{1,0:T(8,128)}, u32[]{:S(2)}) copy-start(f32[512,256]{1,0:T(8,128)} %users.3) | copy-start | bytes 1572868
  1.4 0.7 copy-start.3
  27.0 0.7 copy-start.2
  52.1 20.0 %all-to-all-start.1 = ((f32[32,16,256]{2,1,0:T(8,128)}), f32[32,16,256]{2,1,0:T(8,128)S(1)}, u32[]{:S(2)}, u32[]{:S(2)}) async-start(f32[32,16,256]{2,1,0:T(8,128)} %bitcast.6), calls=%async_computation.1 | async-start | bytes 1048576 | tf_op jit(solution)/shard_map/all_to_all | solution.py:161
  58.1 3.4 %collective-permute-start = (f32[256,256]{1,0:T(8,128)S(1)}, f32[256,256]{1,0:T(8,128)S(1)}, u32[]{:S(2)}, u32[]{:S(2)}) collective-permute-start(f32[256,256]{1,0:T(8,128)S(1)} %get-tuple-element.24), channel_id=1, source_target_pairs={{0,1},{1,0},{2,3},{3,2},{4,5},{5,4},{6,7},{7,6},{8,9},{9,8},{10,11... | collective-permute-start | bytes 786440 | tf_op jit(solution)/shard_map/ppermute | solution.py:170
  62.1 7.4 %collective-permute-start.1 = (f32[128,256]{1,0:T(8,128)S(1)}, f32[128,256]{1,0:T(8,128)S(1)}, u32[]{:S(2)}, u32[]{:S(2)}) collective-permute-start(f32[128,256]{1,0:T(8,128)S(1)} %get-tuple-element.25), channel_id=1, source_target_pairs={{0,2},{1,3},{2,0},{3,1},{4,6},{5,7},{6,4},{7,5},{8,10},{9,11},{10,... | collective-permute-start | bytes 393224 | tf_op jit(solution)/shard_map/ppermute | solution.py:170
  72.9 26.3 %all-to-all-start.2 = ((f32[32,16,256]{2,1,0:T(8,128)}), f32[32,16,256]{2,1,0:T(8,128)S(1)}, u32[]{:S(2)}, u32[]{:S(2)}) async-start(f32[32,16,256]{2,1,0:T(8,128)} %shard_map.72), calls=%async_computation.2 | async-start | bytes 1048576 | tf_op jit(solution)/shard_map/all_to_all | solution.py:161
  80.9 7.5 %collective-permute-start.2 = (f32[64,256]{1,0:T(8,128)S(1)}, f32[64,256]{1,0:T(8,128)S(1)}, u32[]{:S(2)}, u32[]{:S(2)}) collective-permute-start(f32[64,256]{1,0:T(8,128)S(1)} %get-tuple-element.28), channel_id=1, source_target_pairs={{0,4},{1,5},{2,6},{3,7},{4,0},{5,1},{6,2},{7,3},{8,12},{9,13},{10,... | collective-permute-start | bytes 196616 | tf_op jit(solution)/shard_map/ppermute | solution.py:170
  88.9 9.7 %collective-permute-start.3 = (f32[32,256]{1,0:T(8,128)S(1)}, f32[32,256]{1,0:T(8,128)S(1)}, u32[]{:S(2)}, u32[]{:S(2)}) collective-permute-start(f32[32,256]{1,0:T(8,128)S(1)} %get-tuple-element.30), channel_id=1, source_target_pairs={{0,8},{1,9},{2,10},{3,11},{4,12},{5,13},{6,14},{7,15},{8,0},{9,1},... | collective-permute-start | bytes 98312 | tf_op jit(solution)/shard_map/ppermute | solution.py:170

commit v3 on v2

--- a/solution.py
+++ b/solution.py
@@ -111,7 +111,25 @@
         stats[d, :, :] = one
 
 
-def user_body(place, items, positive, scores, stats, loss, grad, user_part):
+def weigh_body(place, items, positive, scores, stats, share, weighted, chosen, target):
+    level = jnp.concatenate([stats[0, k:k + 1, :] for k in range(4)], axis=1)
+    wanted = positive[...]
+    for k in range(MEMBERS):
+        at = slice(OWN * k, OWN * (k + 1))
+        share[at, :] = jnp.exp(scores[at, :] - level)
+        target[at, :] = jnp.where(hits(place, wanted, k), 1.0, 0.0).astype(jnp.bfloat16)
+    weighted[...] = dot(share[...], items[...], 0, 0)
+    rest = items[...]
+    for term in range(3):
+        piece = rest.astype(jnp.bfloat16)
+        rest = rest - piece.astype(jnp.float32)
+        product = lax.dot_general(
+            target[...], piece, (((0,), (0,)), ((), ())), preferred_element_type=jnp.float32
+        )
+        chosen[...] = product if term == 0 else chosen[...] + product
+
+
+def user_body(own, stats, weighted, chosen, loss, factor, user_part):
     highest = stats[0, 0:4, :]
     for d in range(1, GROUPS):
         highest = jnp.maximum(highest, stats[d, 0:4, :])
@@ -122,16 +140,19 @@
         picked = picked + stats[d, 4:8, :]
     log_total = highest + jnp.log(total)
     loss[...] = log_total - picked
-    level = jnp.concatenate([log_total[k:k + 1, :] for k in range(4)], axis=1)
+    factor[...] = jnp.exp(own[0, 0:4, :] - log_total)
+    for k in range(4):
+        at = slice(128 * k, 128 * (k + 1))
+        user_part[at, :] = column_of(factor[k:k + 1, :]) * weighted[at, :] - chosen[at, :]
+
+
+def item_body(place, users, positive, share, factor, mine, theirs, grad):
+    scale = jnp.concatenate([factor[k:k + 1, :] for k in range(4)], axis=1)
     wanted = positive[...]
-    for k in range(MEMBERS):
-        at = slice(OWN * k, OWN * (k + 1))
-        hit = hits(place, wanted, k)
-        grad[at, :] = jnp.exp(scores[at, :] - level) - jnp.where(hit, 1.0, 0.0)
-    user_part[...] = dot(grad[...], items[...], 0, 0)
-
-
-def item_body(users, grad, mine, theirs):
+    for k in list(range(Z, MEMBERS)) + list(range(Z)):
+        at = slice(OWN * k, OWN * (k + 1))
+        hit = jnp.where(hits(place, wanted, k), 1.0, 0.0)
+        grad[at, :] = share[at, :] * scale - hit
     theirs[...] = dot(grad[HALF:SLAB, :], users[...], 1, 0)
     mine[...] = dot(grad[0:HALF, :], users[...], 1, 0)
 
@@ -173,22 +194,28 @@
 def per_device(user_vectors, item_vectors, item_counts, positive_ids):
     member = lax.axis_index("users")
     place = jnp.stack([lax.axis_index("items"), member // CORES, member % CORES]).astype(jnp.int32)
-    positive = positive_ids.reshape(1, ROWS)
     product = 2 * ROWS * SLAB * E
-
+    users, positive = user_vectors, positive_ids.reshape(1, ROWS)
     packed = call(pack_body, f32(PACK, E), (item_vectors, item_counts.reshape(1, OWN)))
     packed = lax.all_gather(packed, "users", axis=0, tiled=True)
-    items, scores, stats = call(
+    items, scores, own = call(
         score_body, (f32(SLAB, E), f32(SLAB, ROWS), f32(GROUPS, 8, 128)),
-        (place, user_vectors, packed, positive), scalars=1, flops=product,
-    )
-    stats = exchange(stats, "items")
-    loss, grad, user_part = call(
-        user_body, (f32(4, 128), f32(SLAB, ROWS), f32(ROWS, E)),
-        (place, items, positive, scores, stats), scalars=1, flops=product,
+        (place, users, packed, positive), scalars=1, flops=product,
+    )
+    stats = exchange(own, "items")
+    share, weighted, chosen = call(
+        weigh_body, (f32(SLAB, ROWS), f32(ROWS, E), f32(ROWS, E)),
+        (place, items, positive, scores, own), scalars=1, flops=2 * product,
+        scratch=[pltpu.VMEM((SLAB, ROWS), jnp.bfloat16)],
+    )
+    loss, factor, user_part = call(
+        user_body, (f32(4, 128), f32(4, 128), f32(ROWS, E)), (own, stats, weighted, chosen),
     )
     parts = exchange(user_part.reshape(GROUPS, SHARE, E), "items")
-    mine, theirs = call(item_body, (f32(HALF, E), f32(HALF, E)), (user_vectors, grad), flops=product)
+    mine, theirs = call(
+        item_body, (f32(HALF, E), f32(HALF, E)), (place, users, positive, share, factor),
+        scalars=1, flops=product, scratch=[pltpu.VMEM((SLAB, ROWS), jnp.float32)],
+    )
     arrived = swap(theirs, 0, 1)
     for shift in range(3):
         size = HALF >> (shift + 1)
@@ -196,10 +223,10 @@
             functools.partial(halve_body, shift), (f32(size, E), f32(size, E)),
             (place, mine, arrived), scalars=1, scratch=[pltpu.VMEM((2 * size, E), jnp.float32)],
         )
+        if shift == 1:
+            spread = call(add_spread_body, f32(GROUPS, SHARE, E), (parts,), after=(theirs,))
+            user_grad = exchange(spread, "items").reshape(ROWS, E)
         arrived = swap(theirs, 1 << shift, 0)
-        if shift == 0:
-            spread = call(add_spread_body, f32(GROUPS, SHARE, E), (parts,), after=(arrived,))
-            user_grad = exchange(spread, "items").reshape(ROWS, E)
     item_grad = call(sum_body, f32(OWN, E), (mine, arrived))
     return (loss.reshape(ROWS), user_grad, item_grad)
 

time: 101 us -> 103 us (1.020)
  blocking collectives: 44.6 us -> 24.9 us
  starting transfers between devices: 22 us -> 33.5 us
  waiting for transfers between devices: 20.9 us -> 25 us
  local copies, waits for them, and re-layouts: 2.78 us -> 6.44 us
  Pallas kernels: 8.93 us -> 11.9 us
    all_to_all x1 -> x0, blocking collectives: 19.7 us -> none  [exchange(): return lax.all_to_all(value, axis, split_axis=0, concat_axis=0, tiled=True)]
    all_to_all x2 -> x3, starting transfers between devices: 12.4 us -> 23.9 us  [exchange(): return lax.all_to_all(value, axis, split_axis=0, concat_axis=0, tiled=True)]
    all_to_all x2 -> x3, waiting for transfers between devices: 2.49 us -> 6.55 us  [exchange(): return lax.all_to_all(value, axis, split_axis=0, concat_axis=0, tiled=True)]
    unnamed x9 -> x17, local copies, waits for them, and re-layouts: 2.78 us -> 6.44 us
    pallas_call x9 -> x10, Pallas kernels: 8.93 us -> 11.9 us  [call(): pl.pallas_call((lambda *refs: body(*refs[:last], *refs[last + len(after):...]
  transfers between devices with their start and end apart: 6 -> 7, of which waited for: 5 -> 6; matrix products, arithmetic and copies ran while one was open for 0% -> 0% of each run, Pallas kernels for 3% -> 6%
where the time goes in v3:
time: 103 us
  starting transfers between devices  33.5 us (33%)
  waiting for transfers between devices  25 us (24%)
  blocking collectives  24.9 us (24%)
  Pallas kernels  11.9 us (12%)
  local copies, waits for them, and re-layouts  6.44 us (6%)
    all_gather x1, blocking collectives, per_device(): packed = lax.all_gather(packed, 'users', axis=0, tiled=True)  24.9 us
    all_to_all x3, starting transfers between devices, exchange(): return lax.all_to_all(value, axis, split_axis=0, concat_axis=0, tiled=True)  23.9 us
    ppermute x4, waiting for transfers between devices, swap(): return lax.ppermute(value, 'users', pairs)  18.4 us
    pallas_call x10, Pallas kernels, call(): pl.pallas_call((lambda *refs: body(*refs[:last], *refs[last + len(after):...  11.9 us
    ppermute x4, starting transfers between devices, swap(): return lax.ppermute(value, 'users', pairs)  9.62 us
    all_to_all x3, waiting for transfers between devices, exchange(): return lax.all_to_all(value, axis, split_axis=0, concat_axis=0, tiled=True)  6.55 us
    unnamed x17, local copies, waits for them, and re-layouts  6.44 us
  transfers between devices with their start and end apart: 7, of which 6 were waited for; matrix products, arithmetic and copies ran while one was open for 0% of the time, Pallas kernels for 6%

profile of v3, /device:TPU:2, one launch (start us, length us, event | category | flops | bytes accessed | tf_op | source)
XLA Modules:
  0.0 102.6 jit_solution(2823406779332244246)
XLA Ops:
  2.1 24.9 %all_gather.3.packed = f32[640,256]{1,0:T(8,128)S(1)} all-gather(f32[40,256]{1,0:T(8,128)S(1)} %shard_map.67), channel_id=1, replica_groups=mesh['items'=32,'users'=16] {'users'}, dimensions={0}, use_global_device_ids=true | all-gather | bytes 696320 | tf_op jit(solution)/shard_map/all_gather | solution.py:200
  27.7 2.6 %shard_map.68 = (f32[512,256]{1,0:T(8,128)S(1)}, f32[512,512]{1,0:T(8,128)S(1)}, f32[32,8,128]{2,1,0:T(8,128)}) custom-call(s32[3]{0:T(128)S(1)} %pad_add_fusion.place, f32[512,256]{1,0:T(8,128)S(1)} %copy-done, f32[640,256]{1,0:T(8,128)S(1)} %all_gather.3.packed, s32[1,512]{1,0:T(1,128)S(1)} %bitcast.8), custom_call_target="tpu_custom_call" | custom-call | flops 134217728 | bytes 2885644 | tf_op jit(solution)/shard_map/pallas_call | solution.py:40
  30.2 0.8 copy-done.1
  31.0 10.3 %all-to-all-start = ((f32[32,8,128]{2,1,0:T(8,128)}), f32[32,8,128]{2,1,0:T(8,128)S(1)}, u32[]{:S(2)}, u32[]{:S(2)}) async-start(f32[32,8,128]{2,1,0:T(8,128)} %get-tuple-element.20.stats.own), calls=%async_computation | async-start | bytes 262144 | tf_op jit(solution)/shard_map/all_to_all | solution.py:182
  41.3 1.0 %copy-done.2 = f32[512,256]{1,0:T(8,128)S(1)} copy-done((f32[512,256]{1,0:T(8,128)S(1)}, f32[512,256]{1,0:T(8,128)}, u32[]{:S(2)}) %copy-start.2) | copy-done | bytes 524312
  42.3 2.5 %shard_map.69 = (f32[512,512]{1,0:T(8,128)S(1)}, f32[512,256]{1,0:T(8,128)S(1)}, f32[512,256]{1,0:T(8,128)S(1)}) custom-call(s32[3]{0:T(128)S(1)} %pad_add_fusion.place, f32[512,256]{1,0:T(8,128)S(1)} %copy-done.2, s32[1,512]{1,0:T(1,128)S(1)} %bitcast.9, f32[512,512]{1,0:T(8,128)S(1)} %get-tuple-element.22.scores, f32[32,8,128]{2,1,0:T(8,128)} %get-tuple-element.20.stats.own), custom_call_target="tpu_custom_call" | custom-call | flops 268435456 | bytes 3803148 | tf_op jit(solution)/shard_map/pallas_call | solution.py:40
  44.8 0.8 copy-done.3
  45.6 5.3 %all-to-all-done.stats = f32[32,8,128]{2,1,0:T(8,128)S(1)} async-done(((f32[32,8,128]{2,1,0:T(8,128)}), f32[32,8,128]{2,1,0:T(8,128)S(1)}, u32[]{:S(2)}, u32[]{:S(2)}) %all-to-all-start) | async-done | bytes 131104 | tf_op jit(solution)/shard_map/all_to_all | solution.py:182
  50.9 1.0 %copy-done.4 = f32[512,256]{1,0:T(8,128)S(1)} copy-done((f32[512,256]{1,0:T(8,128)S(1)}, f32[512,256]{1,0:T(8,128)}, u32[]{:S(2)}) %copy-start.4) | copy-done | bytes 524312
  52.0 1.9 %shard_map.70 = (f32[4,128]{1,0:T(4,128)}, f32[4,128]{1,0:T(4,128)S(1)}, f32[512,256]{1,0:T(8,128)}) custom-call(f32[32,8,128]{2,1,0:T(8,128)} %get-tuple-element.20.stats.own, f32[32,8,128]{2,1,0:T(8,128)S(1)} %all-to-all-done.stats, f32[512,256]{1,0:T(8,128)S(1)} %get-tuple-element.23.weighted, f32[512,256]{1,0:T(8,128)S(1)} %copy-done.4), custom_call_target="tpu_custom_call" | custom-call | bytes 1839104 | tf_op jit(solution)/shard_map/pallas_call | solution.py:40
  53.9 5.0 %all-to-all-start.1 = ((f32[32,16,256]{2,1,0:T(8,128)}), f32[32,16,256]{2,1,0:T(8,128)S(1)}, u32[]{:S(2)}, u32[]{:S(2)}) async-start(f32[32,16,256]{2,1,0:T(8,128)} %bitcast.6), calls=%async_computation.1 | async-start | bytes 1048576 | tf_op jit(solution)/shard_map/all_to_all | solution.py:182
  58.9 1.7 %shard_map.71 = (f32[256,256]{1,0:T(8,128)S(1)}, f32[256,256]{1,0:T(8,128)S(1)}) custom-call(s32[3]{0:T(128)S(1)} %pad_add_fusion.place, f32[512,256]{1,0:T(8,128)S(1)} %copy-done, s32[1,512]{1,0:T(1,128)S(1)} %bitcast.10, f32[512,512]{1,0:T(8,128)S(1)} %get-tuple-element.27.share, f32[4,128]{1,0:T(4,128)S(1)} %get-tuple-element.28.factor), custom_call_target="tpu_custom_call" | custom-call | flops 134217728 | bytes 2101260 | tf_op jit(solution)/shard_map/pallas_call | solution.py:40
  60.6 1.9 %collective-permute-start = (f32[256,256]{1,0:T(8,128)S(1)}, f32[256,256]{1,0:T(8,128)S(1)}, u32[]{:S(2)}, u32[]{:S(2)}) collective-permute-start(f32[256,256]{1,0:T(8,128)S(1)} %get-tuple-element.30), channel_id=1, source_target_pairs={{0,1},{1,0},{2,3},{3,2},{4,5},{5,4},{6,7},{7,6},{8,9},{9,8},{10,11... | collective-permute-start | bytes 786440 | tf_op jit(solution)/shard_map/ppermute | solution.py:191
  62.6 1.5 %collective-permute-done.b = f32[256,256]{1,0:T(8,128)S(1)} collective-permute-done((f32[256,256]{1,0:T(8,128)S(1)}, f32[256,256]{1,0:T(8,128)S(1)}, u32[]{:S(2)}, u32[]{:S(2)}) %collective-permute-start) | collective-permute-done | bytes 262176 | tf_op jit(solution)/shard_map/ppermute | solution.py:191
  64.7 1.9 %collective-permute-start.1 = (f32[128,256]{1,0:T(8,128)S(1)}, f32[128,256]{1,0:T(8,128)S(1)}, u32[]{:S(2)}, u32[]{:S(2)}) collective-permute-start(f32[128,256]{1,0:T(8,128)S(1)} %get-tuple-element.32), channel_id=1, source_target_pairs={{0,2},{1,3},{2,0},{3,1},{4,6},{5,7},{6,4},{7,5},{8,10},{9,11},{10,... | collective-permute-start | bytes 393224 | tf_op jit(solution)/shard_map/ppermute | solution.py:191
  66.6 5.5 %collective-permute-done.1.b = f32[128,256]{1,0:T(8,128)S(1)} collective-permute-done((f32[128,256]{1,0:T(8,128)S(1)}, f32[128,256]{1,0:T(8,128)S(1)}, u32[]{:S(2)}, u32[]{:S(2)}) %collective-permute-start.1) | collective-permute-done | bytes 131104 | tf_op jit(solution)/shard_map/ppermute | solution.py:191
  72.7 1.2 %all-to-all-done.1.refs_0_ = f32[32,16,256]{2,1,0:T(8,128)S(1)} async-done(((f32[32,16,256]{2,1,0:T(8,128)}), f32[32,16,256]{2,1,0:T(8,128)S(1)}, u32[]{:S(2)}, u32[]{:S(2)}) %all-to-all-start.1) | async-done | bytes 524320 | tf_op jit(solution)/shard_map/all_to_all | solution.py:182
  73.9 0.9 shard_map.74
  74.8 8.6 %all-to-all-start.2 = ((f32[32,16,256]{2,1,0:T(8,128)}), f32[32,16,256]{2,1,0:T(8,128)S(1)}, u32[]{:S(2)}, u32[]{:S(2)}) async-start(f32[32,16,256]{2,1,0:T(8,128)} %shard_map.74), calls=%async_computation.2 | async-start | bytes 1048576 | tf_op jit(solution)/shard_map/all_to_all | solution.py:182
  83.4 2.2 %collective-permute-start.2 = (f32[64,256]{1,0:T(8,128)S(1)}, f32[64,256]{1,0:T(8,128)S(1)}, u32[]{:S(2)}, u32[]{:S(2)}) collective-permute-start(f32[64,256]{1,0:T(8,128)S(1)} %get-tuple-element.33.refs_1_), channel_id=1, source_target_pairs={{0,4},{1,5},{2,6},{3,7},{4,0},{5,1},{6,2},{7,3},{8,12},{9,13},{10,... | collective-permute-start | bytes 196616 | tf_op jit(solution)/shard_map/ppermute | solution.py:191
  85.6 5.3 %collective-permute-done.2.b = f32[64,256]{1,0:T(8,128)S(1)} collective-permute-done((f32[64,256]{1,0:T(8,128)S(1)}, f32[64,256]{1,0:T(8,128)S(1)}, u32[]{:S(2)}, u32[]{:S(2)}) %collective-permute-start.2) | collective-permute-done | bytes 65568 | tf_op jit(solution)/shard_map/ppermute | solution.py:191
  91.5 3.6 %collective-permute-start.3 = (f32[32,256]{1,0:T(8,128)S(1)}, f32[32,256]{1,0:T(8,128)S(1)}, u32[]{:S(2)}, u32[]{:S(2)}) collective-permute-start(f32[32,256]{1,0:T(8,128)S(1)} %get-tuple-element.36), channel_id=1, source_target_pairs={{0,8},{1,9},{2,10},{3,11},{4,12},{5,13},{6,14},{7,15},{8,0},{9,1},... | collective-permute-start | bytes 98312 | tf_op jit(solution)/shard_map/ppermute | solution.py:191
  95.1 6.1 %collective-permute-done.3.b = f32[32,256]{1,0:T(8,128)S(1)} collective-permute-done((f32[32,256]{1,0:T(8,128)S(1)}, f32[32,256]{1,0:T(8,128)S(1)}, u32[]{:S(2)}, u32[]{:S(2)}) %collective-permute-start.3) | collective-permute-done | bytes 32800 | tf_op jit(solution)/shard_map/ppermute | solution.py:191
  101.8 0.8 copy.8
  (19 shorter events, 4.4 us)
Async XLA Ops:
  0.6 0.8 copy-start.5
  0.6 26.4 %copy-start = (f32[512,256]{1,0:T(8,128)S(1)}, f32[512,256]{1,0:T(8,128)}, u32[]{:S(2)}) copy-start(f32[512,256]{1,0:T(8,128)} %users.3) | copy-start | bytes 1572868
  1.4 0.7 copy-start.7
  27.0 0.7 copy-start.6
  30.2 0.8 copy-start.1
  31.0 19.9 %all-to-all-start = ((f32[32,8,128]{2,1,0:T(8,128)}), f32[32,8,128]{2,1,0:T(8,128)S(1)}, u32[]{:S(2)}, u32[]{:S(2)}) async-start(f32[32,8,128]{2,1,0:T(8,128)} %get-tuple-element.20.stats.own), calls=%async_computation | async-start | bytes 262144 | tf_op jit(solution)/shard_map/all_to_all | solution.py:182
  41.3 1.0 %copy-start.2 = (f32[512,256]{1,0:T(8,128)S(1)}, f32[512,256]{1,0:T(8,128)}, u32[]{:S(2)}) copy-start(f32[512,256]{1,0:T(8,128)} %copy-done.1) | copy-start | bytes 1572868
  44.8 0.8 copy-start.3
  50.9 1.0 %copy-start.4 = (f32[512,256]{1,0:T(8,128)S(1)}, f32[512,256]{1,0:T(8,128)}, u32[]{:S(2)}) copy-start(f32[512,256]{1,0:T(8,128)} %copy-done.3) | copy-start | bytes 1572868
  53.9 20.0 %all-to-all-start.1 = ((f32[32,16,256]{2,1,0:T(8,128)}), f32[32,16,256]{2,1,0:T(8,128)S(1)}, u32[]{:S(2)}, u32[]{:S(2)}) async-start(f32[32,16,256]{2,1,0:T(8,128)} %bitcast.6), calls=%async_computation.1 | async-start | bytes 1048576 | tf_op jit(solution)/shard_map/all_to_all | solution.py:182
  60.6 3.4 %collective-permute-start = (f32[256,256]{1,0:T(8,128)S(1)}, f32[256,256]{1,0:T(8,128)S(1)}, u32[]{:S(2)}, u32[]{:S(2)}) collective-permute-start(f32[256,256]{1,0:T(8,128)S(1)} %get-tuple-element.30), channel_id=1, source_target_pairs={{0,1},{1,0},{2,3},{3,2},{4,5},{5,4},{6,7},{7,6},{8,9},{9,8},{10,11... | collective-permute-start | bytes 786440 | tf_op jit(solution)/shard_map/ppermute | solution.py:191
  64.7 7.4 %collective-permute-start.1 = (f32[128,256]{1,0:T(8,128)S(1)}, f32[128,256]{1,0:T(8,128)S(1)}, u32[]{:S(2)}, u32[]{:S(2)}) collective-permute-start(f32[128,256]{1,0:T(8,128)S(1)} %get-tuple-element.32), channel_id=1, source_target_pairs={{0,2},{1,3},{2,0},{3,1},{4,6},{5,7},{6,4},{7,5},{8,10},{9,11},{10,... | collective-permute-start | bytes 393224 | tf_op jit(solution)/shard_map/ppermute | solution.py:191
  74.8 27.0 %all-to-all-start.2 = ((f32[32,16,256]{2,1,0:T(8,128)}), f32[32,16,256]{2,1,0:T(8,128)S(1)}, u32[]{:S(2)}, u32[]{:S(2)}) async-start(f32[32,16,256]{2,1,0:T(8,128)} %shard_map.74), calls=%async_computation.2 | async-start | bytes 1048576 | tf_op jit(solution)/shard_map/all_to_all | solution.py:182
  83.4 7.5 %collective-permute-start.2 = (f32[64,256]{1,0:T(8,128)S(1)}, f32[64,256]{1,0:T(8,128)S(1)}, u32[]{:S(2)}, u32[]{:S(2)}) collective-permute-start(f32[64,256]{1,0:T(8,128)S(1)} %get-tuple-element.33.refs_1_), channel_id=1, source_target_pairs={{0,4},{1,5},{2,6},{3,7},{4,0},{5,1},{6,2},{7,3},{8,12},{9,13},{10,... | collective-permute-start | bytes 196616 | tf_op jit(solution)/shard_map/ppermute | solution.py:191
  91.5 9.7 %collective-permute-start.3 = (f32[32,256]{1,0:T(8,128)S(1)}, f32[32,256]{1,0:T(8,128)S(1)}, u32[]{:S(2)}, u32[]{:S(2)}) collective-permute-start(f32[32,256]{1,0:T(8,128)S(1)} %get-tuple-element.36), channel_id=1, source_target_pairs={{0,8},{1,9},{2,10},{3,11},{4,12},{5,13},{6,14},{7,15},{8,0},{9,1},... | collective-permute-start | bytes 98312 | tf_op jit(solution)/shard_map/ppermute | solution.py:191

commit v4 on v2

--- a/solution.py
+++ b/solution.py
@@ -1,5 +1,3 @@
-import functools
-
 import jax
 import jax.numpy as jnp
 from jax import lax
@@ -55,6 +53,23 @@
         a, b, (((contract_a,), (contract_b,)), ((), ())),
         precision=HIGH, preferred_element_type=jnp.float32,
     )
+
+
+def split(a):
+    high = a.astype(jnp.bfloat16)
+    return high, (a - high.astype(jnp.float32)).astype(jnp.bfloat16)
+
+
+def dot_split(a, b, contract_a, contract_b):
+    (a_high, a_low), (b_high, b_low) = a, b
+
+    def product(left, right):
+        return lax.dot_general(
+            left, right, (((contract_a,), (contract_b,)), ((), ())),
+            preferred_element_type=jnp.float32,
+        )
+
+    return product(a_high, b_high) + (product(a_high, b_low) + product(a_low, b_high))
 
 
 def pack_body(items, counts, out):
@@ -128,12 +143,13 @@
         at = slice(OWN * k, OWN * (k + 1))
         hit = hits(place, wanted, k)
         grad[at, :] = jnp.exp(scores[at, :] - level) - jnp.where(hit, 1.0, 0.0)
-    user_part[...] = dot(grad[...], items[...], 0, 0)
+    user_part[...] = dot_split(split(grad[...]), split(items[...]), 0, 0)
 
 
 def item_body(users, grad, mine, theirs):
-    theirs[...] = dot(grad[HALF:SLAB, :], users[...], 1, 0)
-    mine[...] = dot(grad[0:HALF, :], users[...], 1, 0)
+    right = split(users[...])
+    theirs[...] = dot_split(split(grad[HALF:SLAB, :]), right, 1, 0)
+    mine[...] = dot_split(split(grad[0:HALF, :]), right, 1, 0)
 
 
 def add_spread_body(parts, out):
@@ -144,29 +160,40 @@
         out[r] = total
 
 
-def halve_body(shift, place, a, b, keep, send, both):
+def halve_body(place, a, b, keep, send, both):
     both[...] = a[...] + b[...]
-    bit = lax.rem(lax.shift_right_logical(place[1], shift), 2)
+    bit = lax.rem(place[1], 2)
     for k in range(keep.shape[0] // OWN):
         at = slice(OWN * k, OWN * (k + 1))
         keep[at, :] = both[pl.ds(pl.multiple_of((2 * k + bit) * OWN, OWN), OWN), :]
         send[at, :] = both[pl.ds(pl.multiple_of((2 * k + 1 - bit) * OWN, OWN), OWN), :]
 
 
-def sum_body(a, b, out):
-    out[...] = a[...] + b[...]
+def deal_body(place, a, b, *outs):
+    *outs, both = outs
+    both[...] = a[...] + b[...]
+    for r, out in enumerate(outs):
+        pair = lax.rem(lax.shift_right_logical(place[1], 1) + r, Z // 2)
+        out[...] = both[pl.ds(pl.multiple_of(pair * OWN, OWN), OWN), :]
+
+
+def sum_body(*refs):
+    total = refs[0][...]
+    for ref in refs[1:-1]:
+        total = total + ref[...]
+    refs[-1][...] = total
 
 
 def exchange(value, axis):
     return lax.all_to_all(value, axis, split_axis=0, concat_axis=0, tiled=True)
 
 
-def swap(value, flip_z, flip_core):
-    pairs = [
-        (z * CORES + c, (z ^ flip_z) * CORES + (c ^ flip_core))
-        for z in range(Z)
-        for c in range(CORES)
-    ]
+def move(value, target):
+    pairs = []
+    for z in range(Z):
+        for c in range(CORES):
+            z_to, c_to = target(z, c)
+            pairs.append((z * CORES + c, z_to % Z * CORES + c_to))
     return lax.ppermute(value, "users", pairs)
 
 
@@ -189,18 +216,22 @@
     )
     parts = exchange(user_part.reshape(GROUPS, SHARE, E), "items")
     mine, theirs = call(item_body, (f32(HALF, E), f32(HALF, E)), (user_vectors, grad), flops=product)
-    arrived = swap(theirs, 0, 1)
-    for shift in range(3):
-        size = HALF >> (shift + 1)
-        mine, theirs = call(
-            functools.partial(halve_body, shift), (f32(size, E), f32(size, E)),
-            (place, mine, arrived), scalars=1, scratch=[pltpu.VMEM((2 * size, E), jnp.float32)],
-        )
-        arrived = swap(theirs, 1 << shift, 0)
-        if shift == 0:
-            spread = call(add_spread_body, f32(GROUPS, SHARE, E), (parts,), after=(arrived,))
-            user_grad = exchange(spread, "items").reshape(ROWS, E)
-    item_grad = call(sum_body, f32(OWN, E), (mine, arrived))
+    arrived = move(theirs, lambda z, c: (z, 1 - c))
+    mine, theirs = call(
+        halve_body, [f32(HALF // 2, E)] * 2, (place, mine, arrived), scalars=1,
+        scratch=[pltpu.VMEM((HALF, E), jnp.float32)],
+    )
+    arrived = move(theirs, lambda z, c: (z ^ 1, c))
+    pieces = call(
+        deal_body, [f32(OWN, E)] * (Z // 2), (place, mine, arrived), scalars=1,
+        scratch=[pltpu.VMEM((HALF // 2, E), jnp.float32)],
+    )
+    spread = call(add_spread_body, f32(GROUPS, SHARE, E), (parts,), after=(pieces[0],))
+    user_grad = exchange(spread, "items").reshape(ROWS, E)
+    terms = [pieces[0]]
+    for r in (2, 1, 3):
+        terms.append(move(pieces[r], lambda z, c, r=r: (z + 2 * r, c)))
+    item_grad = call(sum_body, f32(OWN, E), terms)
     return (loss.reshape(ROWS), user_grad, item_grad)
 
 

time: 101 us -> 98.3 us (0.973)
  the two profiles are of different devices: /device:TPU:2 before, /device:TPU:8 now
where the time goes in v4:
time: 98.3 us; the launch traced here: 97.8 us
  blocking collectives  45.1 us (46%)
  starting transfers between devices  24.9 us (25%)
  waiting for transfers between devices  16.6 us (17%)
  Pallas kernels  7.46 us (8%)
  local copies, waits for them, and re-layouts  2.78 us (3%)
    all_gather x1, blocking collectives, per_device(): packed = lax.all_gather(packed, 'users', axis=0, tiled=True)  24.9 us
    all_to_all x1, blocking collectives, exchange(): return lax.all_to_all(value, axis, split_axis=0, concat_axis=0, tiled=True)  20.2 us
    ppermute x5, starting transfers between devices, move(): return lax.ppermute(value, 'users', pairs)  15.1 us
    ppermute x5, waiting for transfers between devices, move(): return lax.ppermute(value, 'users', pairs)  9.87 us
    all_to_all x2, starting transfers between devices, exchange(): return lax.all_to_all(value, axis, split_axis=0, concat_axis=0, tiled=True)  9.79 us
    pallas_call x8, Pallas kernels, call(): pl.pallas_call((lambda *refs: body(*refs[:last], *refs[last + len(after):...  7.46 us
    all_to_all x2, waiting for transfers between devices, exchange(): return lax.all_to_all(value, axis, split_axis=0, concat_axis=0, tiled=True)  6.76 us
    unnamed x9, local copies, waits for them, and re-layouts  2.78 us
  transfers between devices with their start and end apart: 7, of which 5 were waited for; matrix products, arithmetic and copies ran while one was open for 0% of the time, Pallas kernels for 2%

profile of v4, /device:TPU:8, one launch (start us, length us, event | category | flops | bytes accessed | tf_op | source)
XLA Modules:
  0.0 97.8 jit_solution(14157105409710070963)
XLA Ops:
  0.7 0.7 copy-done.1
  1.4 0.7 copy-done.3
  2.1 24.9 %all_gather.3.packed = f32[640,256]{1,0:T(8,128)S(1)} all-gather(f32[40,256]{1,0:T(8,128)S(1)} %shard_map.67), channel_id=1, replica_groups=mesh['items'=32,'users'=16] {'users'}, dimensions={0}, use_global_device_ids=true | all-gather | bytes 696320 | tf_op jit(solution)/shard_map/all_gather | solution.py:207
  27.1 0.6 copy-done.2
  27.7 1.9 %shard_map.68 = (f32[512,256]{1,0:T(8,128)S(1)}, f32[512,512]{1,0:T(8,128)S(1)}, f32[32,8,128]{2,1,0:T(8,128)S(1)}) custom-call(s32[3]{0:T(128)S(1)} %pad_add_fusion.place, f32[512,256]{1,0:T(8,128)S(1)} %copy-done, f32[640,256]{1,0:T(8,128)S(1)} %all_gather.3.packed, s32[1,512]{1,0:T(1,128)S(1)} %bitcast.8), custom_call_target="tpu_custom_call" | custom-call | flops 134217728 | bytes 2885644 | tf_op jit(solution)/shard_map/pallas_call | solution.py:38
  29.6 20.2 %all_to_all.15.stats = f32[32,8,128]{2,1,0:T(8,128)S(1)} all-to-all(f32[32,8,128]{2,1,0:T(8,128)S(1)} %get-tuple-element.19), channel_id=1, replica_groups=mesh['items'=32,'users'=16] {'items'}, dimensions={0} | all-to-all | bytes 262144 | tf_op jit(solution)/shard_map/all_to_all | solution.py:188
  49.8 2.3 %shard_map.69 = (f32[4,128]{1,0:T(4,128)}, f32[512,512]{1,0:T(8,128)S(1)}, f32[512,256]{1,0:T(8,128)}) custom-call(s32[3]{0:T(128)S(1)} %pad_add_fusion.place, f32[512,256]{1,0:T(8,128)S(1)} %get-tuple-element.17.items, s32[1,512]{1,0:T(1,128)S(1)} %bitcast.9, f32[512,512]{1,0:T(8,128)S(1)} %get-tuple-element.18.scores, f32[32,8,128]{2,1,0:T(8,128)S(1)} %all_to_all.15.stats), custom_call_target="tpu_custom_call" | custom-call | flops 134217728 | bytes 3280908 | tf_op jit(solution)/shard_map/pallas_call | solution.py:38
  52.1 4.4 %all-to-all-start.1 = ((f32[32,16,256]{2,1,0:T(8,128)}), f32[32,16,256]{2,1,0:T(8,128)S(1)}, u32[]{:S(2)}, u32[]{:S(2)}) async-start(f32[32,16,256]{2,1,0:T(8,128)} %bitcast.6), calls=%async_computation.1 | async-start | bytes 1048576 | tf_op jit(solution)/shard_map/all_to_all | solution.py:188
  56.5 0.6 shard_map.70
  57.1 1.9 %collective-permute-start = (f32[256,256]{1,0:T(8,128)S(1)}, f32[256,256]{1,0:T(8,128)S(1)}, u32[]{:S(2)}, u32[]{:S(2)}) collective-permute-start(f32[256,256]{1,0:T(8,128)S(1)} %get-tuple-element.24), channel_id=1, source_target_pairs={{0,1},{1,0},{2,3},{3,2},{4,5},{5,4},{6,7},{7,6},{8,9},{9,8},{10,11... | collective-permute-start | bytes 786440 | tf_op jit(solution)/shard_map/ppermute | solution.py:197
  59.0 1.5 %collective-permute-done.b = f32[256,256]{1,0:T(8,128)S(1)} collective-permute-done((f32[256,256]{1,0:T(8,128)S(1)}, f32[256,256]{1,0:T(8,128)S(1)}, u32[]{:S(2)}, u32[]{:S(2)}) %collective-permute-start) | collective-permute-done | bytes 262176 | tf_op jit(solution)/shard_map/ppermute | solution.py:197
  60.5 0.6 shard_map.71
  61.1 1.9 %collective-permute-start.1 = (f32[128,256]{1,0:T(8,128)S(1)}, f32[128,256]{1,0:T(8,128)S(1)}, u32[]{:S(2)}, u32[]{:S(2)}) collective-permute-start(f32[128,256]{1,0:T(8,128)S(1)} %get-tuple-element.26), channel_id=1, source_target_pairs={{0,2},{1,3},{2,0},{3,1},{4,6},{5,7},{6,4},{7,5},{8,10},{9,11},{10,... | collective-permute-start | bytes 393224 | tf_op jit(solution)/shard_map/ppermute | solution.py:197
  63.0 5.5 %collective-permute-done.1.b = f32[128,256]{1,0:T(8,128)S(1)} collective-permute-done((f32[128,256]{1,0:T(8,128)S(1)}, f32[128,256]{1,0:T(8,128)S(1)}, u32[]{:S(2)}, u32[]{:S(2)}) %collective-permute-start.1) | collective-permute-done | bytes 131104 | tf_op jit(solution)/shard_map/ppermute | solution.py:197
  69.1 4.5 %all-to-all-done.1.refs_0_ = f32[32,16,256]{2,1,0:T(8,128)S(1)} async-done(((f32[32,16,256]{2,1,0:T(8,128)}), f32[32,16,256]{2,1,0:T(8,128)S(1)}, u32[]{:S(2)}, u32[]{:S(2)}) %all-to-all-start.1) | async-done | bytes 524320 | tf_op jit(solution)/shard_map/all_to_all | solution.py:188
  73.6 0.9 shard_map.73
  74.5 5.4 %all-to-all-start.2 = ((f32[32,16,256]{2,1,0:T(8,128)}), f32[32,16,256]{2,1,0:T(8,128)S(1)}, u32[]{:S(2)}, u32[]{:S(2)}) async-start(f32[32,16,256]{2,1,0:T(8,128)} %shard_map.73), calls=%async_computation.2 | async-start | bytes 1048576 | tf_op jit(solution)/shard_map/all_to_all | solution.py:188
  79.9 3.4 %collective-permute-start.2 = (f32[32,256]{1,0:T(8,128)S(1)}, f32[32,256]{1,0:T(8,128)S(1)}, u32[]{:S(2)}, u32[]{:S(2)}) collective-permute-start(f32[32,256]{1,0:T(8,128)S(1)} %get-tuple-element.28), channel_id=1, source_target_pairs={{0,8},{1,9},{2,10},{3,11},{4,12},{5,13},{6,14},{7,15},{8,0},{9,1},... | collective-permute-start | bytes 98312 | tf_op jit(solution)/shard_map/ppermute | solution.py:197
  83.2 3.1 %collective-permute-start.3 = (f32[32,256]{1,0:T(8,128)S(1)}, f32[32,256]{1,0:T(8,128)S(1)}, u32[]{:S(2)}, u32[]{:S(2)}) collective-permute-start(f32[32,256]{1,0:T(8,128)S(1)} %get-tuple-element.29), channel_id=1, source_target_pairs={{0,4},{1,5},{2,6},{3,7},{4,8},{5,9},{6,10},{7,11},{8,12},{9,13},{1... | collective-permute-start | bytes 98312 | tf_op jit(solution)/shard_map/ppermute | solution.py:197
  86.3 4.9 %collective-permute-start.4 = (f32[32,256]{1,0:T(8,128)S(1)}, f32[32,256]{1,0:T(8,128)S(1)}, u32[]{:S(2)}, u32[]{:S(2)}) collective-permute-start(f32[32,256]{1,0:T(8,128)S(1)} %get-tuple-element.30), channel_id=1, source_target_pairs={{0,12},{1,13},{2,14},{3,15},{4,0},{5,1},{6,2},{7,3},{8,4},{9,5},{1... | collective-permute-start | bytes 98312 | tf_op jit(solution)/shard_map/ppermute | solution.py:197
  91.2 2.9 %collective-permute-done.4.refs_3_ = f32[32,256]{1,0:T(8,128)S(1)} collective-permute-done((f32[32,256]{1,0:T(8,128)S(1)}, f32[32,256]{1,0:T(8,128)S(1)}, u32[]{:S(2)}, u32[]{:S(2)}) %collective-permute-start.4) | collective-permute-done | bytes 32800 | tf_op jit(solution)/shard_map/ppermute | solution.py:197
  94.1 0.6 shard_map.74
  94.7 2.3 %all-to-all-done.2 = f32[32,16,256]{2,1,0:T(8,128)S(1)} async-done(((f32[32,16,256]{2,1,0:T(8,128)}), f32[32,16,256]{2,1,0:T(8,128)S(1)}, u32[]{:S(2)}, u32[]{:S(2)}) %all-to-all-start.2) | async-done | bytes 524320 | tf_op jit(solution)/shard_map/all_to_all | solution.py:188
  97.0 0.8 copy.8
  (10 shorter events, 0.7 us)
Async XLA Ops:
  0.6 0.8 copy-start.1
  0.6 26.4 %copy-start = (f32[512,256]{1,0:T(8,128)S(1)}, f32[512,256]{1,0:T(8,128)}, u32[]{:S(2)}) copy-start(f32[512,256]{1,0:T(8,128)} %users.3) | copy-start | bytes 1572868
  1.4 0.7 copy-start.3
  27.0 0.7 copy-start.2
  52.1 21.5 %all-to-all-start.1 = ((f32[32,16,256]{2,1,0:T(8,128)}), f32[32,16,256]{2,1,0:T(8,128)S(1)}, u32[]{:S(2)}, u32[]{:S(2)}) async-start(f32[32,16,256]{2,1,0:T(8,128)} %bitcast.6), calls=%async_computation.1 | async-start | bytes 1048576 | tf_op jit(solution)/shard_map/all_to_all | solution.py:188
  57.1 3.4 %collective-permute-start = (f32[256,256]{1,0:T(8,128)S(1)}, f32[256,256]{1,0:T(8,128)S(1)}, u32[]{:S(2)}, u32[]{:S(2)}) collective-permute-start(f32[256,256]{1,0:T(8,128)S(1)} %get-tuple-element.24), channel_id=1, source_target_pairs={{0,1},{1,0},{2,3},{3,2},{4,5},{5,4},{6,7},{7,6},{8,9},{9,8},{10,11... | collective-permute-start | bytes 786440 | tf_op jit(solution)/shard_map/ppermute | solution.py:197
  61.1 7.4 %collective-permute-start.1 = (f32[128,256]{1,0:T(8,128)S(1)}, f32[128,256]{1,0:T(8,128)S(1)}, u32[]{:S(2)}, u32[]{:S(2)}) collective-permute-start(f32[128,256]{1,0:T(8,128)S(1)} %get-tuple-element.26), channel_id=1, source_target_pairs={{0,2},{1,3},{2,0},{3,1},{4,6},{5,7},{6,4},{7,5},{8,10},{9,11},{10,... | collective-permute-start | bytes 393224 | tf_op jit(solution)/shard_map/ppermute | solution.py:197
  74.5 22.5 %all-to-all-start.2 = ((f32[32,16,256]{2,1,0:T(8,128)}), f32[32,16,256]{2,1,0:T(8,128)S(1)}, u32[]{:S(2)}, u32[]{:S(2)}) async-start(f32[32,16,256]{2,1,0:T(8,128)} %shard_map.73), calls=%async_computation.2 | async-start | bytes 1048576 | tf_op jit(solution)/shard_map/all_to_all | solution.py:188
  79.9 11.3 %collective-permute-start.2 = (f32[32,256]{1,0:T(8,128)S(1)}, f32[32,256]{1,0:T(8,128)S(1)}, u32[]{:S(2)}, u32[]{:S(2)}) collective-permute-start(f32[32,256]{1,0:T(8,128)S(1)} %get-tuple-element.28), channel_id=1, source_target_pairs={{0,8},{1,9},{2,10},{3,11},{4,12},{5,13},{6,14},{7,15},{8,0},{9,1},... | collective-permute-start | bytes 98312 | tf_op jit(solution)/shard_map/ppermute | solution.py:197
  83.2 8.0 %collective-permute-start.3 = (f32[32,256]{1,0:T(8,128)S(1)}, f32[32,256]{1,0:T(8,128)S(1)}, u32[]{:S(2)}, u32[]{:S(2)}) collective-permute-start(f32[32,256]{1,0:T(8,128)S(1)} %get-tuple-element.29), channel_id=1, source_target_pairs={{0,4},{1,5},{2,6},{3,7},{4,8},{5,9},{6,10},{7,11},{8,12},{9,13},{1... | collective-permute-start | bytes 98312 | tf_op jit(solution)/shard_map/ppermute | solution.py:197
  86.3 7.8 %collective-permute-start.4 = (f32[32,256]{1,0:T(8,128)S(1)}, f32[32,256]{1,0:T(8,128)S(1)}, u32[]{:S(2)}, u32[]{:S(2)}) collective-permute-start(f32[32,256]{1,0:T(8,128)S(1)} %get-tuple-element.30), channel_id=1, source_target_pairs={{0,12},{1,13},{2,14},{3,15},{4,0},{5,1},{6,2},{7,3},{8,4},{9,5},{1... | collective-permute-start | bytes 98312 | tf_op jit(solution)/shard_map/ppermute | solution.py:197

commit v5 on v4

--- a/solution.py
+++ b/solution.py
@@ -3,11 +3,13 @@
 from jax import lax
 from jax.experimental import pallas as pl
 from jax.experimental.pallas import tpu as pltpu
-from jax.sharding import PartitionSpec as P
+from jax.sharding import Mesh, PartitionSpec as P
 
 HIGH = lax.Precision.HIGHEST
-GROUPS, MEMBERS = 32, 16
-Z, CORES = 8, 2
+X, Y, Z, CORES = 4, 8, 8, 2
+GROUPS, MEMBERS = X * Y, Z * CORES
+PEERS = ("y", "x")
+USER_AXES = ("z", "core")
 E = 256
 OWN = 32
 PACK = OWN + 8
@@ -160,21 +162,21 @@
         out[r] = total
 
 
-def halve_body(place, a, b, keep, send, both):
-    both[...] = a[...] + b[...]
+def halve_body(place, a, b, keep, send):
     bit = lax.rem(place[1], 2)
     for k in range(keep.shape[0] // OWN):
         at = slice(OWN * k, OWN * (k + 1))
-        keep[at, :] = both[pl.ds(pl.multiple_of((2 * k + bit) * OWN, OWN), OWN), :]
-        send[at, :] = both[pl.ds(pl.multiple_of((2 * k + 1 - bit) * OWN, OWN), OWN), :]
+        here = pl.ds(pl.multiple_of((2 * k + bit) * OWN, OWN), OWN)
+        there = pl.ds(pl.multiple_of((2 * k + 1 - bit) * OWN, OWN), OWN)
+        send[at, :] = a[there, :] + b[there, :]
+        keep[at, :] = a[here, :] + b[here, :]
 
 
 def deal_body(place, a, b, *outs):
-    *outs, both = outs
-    both[...] = a[...] + b[...]
     for r, out in enumerate(outs):
         pair = lax.rem(lax.shift_right_logical(place[1], 1) + r, Z // 2)
-        out[...] = both[pl.ds(pl.multiple_of(pair * OWN, OWN), OWN), :]
+        rows = pl.ds(pl.multiple_of(pair * OWN, OWN), OWN)
+        out[...] = a[rows, :] + b[rows, :]
 
 
 def sum_body(*refs):
@@ -194,40 +196,38 @@
         for c in range(CORES):
             z_to, c_to = target(z, c)
             pairs.append((z * CORES + c, z_to % Z * CORES + c_to))
-    return lax.ppermute(value, "users", pairs)
+    return lax.ppermute(value, USER_AXES, pairs)
 
 
 def per_device(user_vectors, item_vectors, item_counts, positive_ids):
-    member = lax.axis_index("users")
-    place = jnp.stack([lax.axis_index("items"), member // CORES, member % CORES]).astype(jnp.int32)
+    place = jnp.stack([lax.axis_index(("x", "y")), lax.axis_index("z"), lax.axis_index("core")])
+    place = place.astype(jnp.int32)
     positive = positive_ids.reshape(1, ROWS)
     product = 2 * ROWS * SLAB * E
 
     packed = call(pack_body, f32(PACK, E), (item_vectors, item_counts.reshape(1, OWN)))
-    packed = lax.all_gather(packed, "users", axis=0, tiled=True)
+    packed = lax.all_gather(packed, USER_AXES, axis=0, tiled=True)
     items, scores, stats = call(
         score_body, (f32(SLAB, E), f32(SLAB, ROWS), f32(GROUPS, 8, 128)),
         (place, user_vectors, packed, positive), scalars=1, flops=product,
     )
-    stats = exchange(stats, "items")
+    stats = exchange(stats, PEERS)
     loss, grad, user_part = call(
         user_body, (f32(4, 128), f32(SLAB, ROWS), f32(ROWS, E)),
         (place, items, positive, scores, stats), scalars=1, flops=product,
     )
-    parts = exchange(user_part.reshape(GROUPS, SHARE, E), "items")
+    parts = exchange(user_part.reshape(GROUPS, SHARE, E), PEERS)
     mine, theirs = call(item_body, (f32(HALF, E), f32(HALF, E)), (user_vectors, grad), flops=product)
     arrived = move(theirs, lambda z, c: (z, 1 - c))
     mine, theirs = call(
         halve_body, [f32(HALF // 2, E)] * 2, (place, mine, arrived), scalars=1,
-        scratch=[pltpu.VMEM((HALF, E), jnp.float32)],
     )
     arrived = move(theirs, lambda z, c: (z ^ 1, c))
     pieces = call(
         deal_body, [f32(OWN, E)] * (Z // 2), (place, mine, arrived), scalars=1,
-        scratch=[pltpu.VMEM((HALF // 2, E), jnp.float32)],
     )
     spread = call(add_spread_body, f32(GROUPS, SHARE, E), (parts,), after=(pieces[0],))
-    user_grad = exchange(spread, "items").reshape(ROWS, E)
+    user_grad = exchange(spread, PEERS).reshape(ROWS, E)
     terms = [pieces[0]]
     for r in (2, 1, 3):
         terms.append(move(pieces[r], lambda z, c, r=r: (z + 2 * r, c)))
@@ -236,11 +236,12 @@
 
 
 def solution(mesh):
-    placed = (P("users", None), P(("items", "users"), None), P(("items", "users")), P("users"))
+    fine = Mesh(mesh.devices.reshape(X, Y, Z, CORES), ("x", "y") + USER_AXES)
+    users, everything = P(USER_AXES), P(("x", "y") + USER_AXES)
     return jax.shard_map(
         per_device,
-        mesh=mesh,
-        in_specs=placed,
-        out_specs=(P("users"), P("users", None), P(("items", "users"), None)),
+        mesh=fine,
+        in_specs=(users, everything, everything, users),
+        out_specs=(users, users, everything),
         check_vma=False,
     )

time: 98.3 us -> 98.2 us (level)
  no operation moved by 1% of the time
where the time goes in v5:
time: 98.2 us; the launch traced here: 97.6 us
  blocking collectives  45 us (46%)
  starting transfers between devices  25.6 us (26%)
  waiting for transfers between devices  15.9 us (16%)
  Pallas kernels  7.45 us (8%)
  local copies, waits for them, and re-layouts  2.86 us (3%)
    all_gather x1, blocking collectives, per_device(): packed = lax.all_gather(packed, USER_AXES, axis=0, tiled=True)  24.9 us
    all_to_all x1, blocking collectives, exchange(): return lax.all_to_all(value, axis, split_axis=0, concat_axis=0, tiled=True)  20.1 us
    ppermute x5, starting transfers between devices, move(): return lax.ppermute(value, USER_AXES, pairs)  15.1 us
    all_to_all x2, starting transfers between devices, exchange(): return lax.all_to_all(value, axis, split_axis=0, concat_axis=0, tiled=True)  10.4 us
    ppermute x5, waiting for transfers between devices, move(): return lax.ppermute(value, USER_AXES, pairs)  9.87 us
    pallas_call x8, Pallas kernels, call(): pl.pallas_call((lambda *refs: body(*refs[:last], *refs[last + len(after):...  7.45 us
    all_to_all x2, waiting for transfers between devices, exchange(): return lax.all_to_all(value, axis, split_axis=0, concat_axis=0, tiled=True)  5.99 us
    unnamed x9, local copies, waits for them, and re-layouts  2.86 us
  transfers between devices with their start and end apart: 7, of which 5 were waited for; matrix products, arithmetic and copies ran while one was open for 0% of the time, Pallas kernels for 2%

profile of v5, /device:TPU:8, one launch (start us, length us, event | category | flops | bytes accessed | tf_op | source)
XLA Modules:
  0.0 97.6 jit_solution(511377620521600805)
XLA Ops:
  0.7 0.8 copy-done.1
  1.5 0.7 copy-done.3
  2.1 24.9 %all_gather.3.packed = f32[640,256]{1,0:T(8,128)S(1)} all-gather(f32[40,256]{1,0:T(8,128)S(1)} %shard_map.67), channel_id=1, replica_groups=mesh['x'=4,'y'=8,'z'=8,'core'=2] {'z','core'}, dimensions={0}, use_global_device_ids=true | all-gather | bytes 696320 | tf_op jit(solution)/shard_map/all_gather | solution.py:209
  27.1 0.6 copy-done.2
  27.7 1.9 %shard_map.68 = (f32[512,256]{1,0:T(8,128)S(1)}, f32[512,512]{1,0:T(8,128)S(1)}, f32[32,8,128]{2,1,0:T(8,128)S(1)}) custom-call(s32[3]{0:T(128)S(1)} %pad_add_fusion.place, f32[512,256]{1,0:T(8,128)S(1)} %copy-done, f32[640,256]{1,0:T(8,128)S(1)} %all_gather.3.packed, s32[1,512]{1,0:T(1,128)S(1)} %bitcast.8), custom_call_target="tpu_custom_call" | custom-call | flops 134217728 | bytes 2885644 | tf_op jit(solution)/shard_map/pallas_call | solution.py:40
  29.7 20.1 %all_to_all.15.stats = f32[32,8,128]{2,1,0:T(8,128)S(1)} all-to-all(f32[32,8,128]{2,1,0:T(8,128)S(1)} %get-tuple-element.19), channel_id=1, replica_groups=mesh['x'=4,'y'=8,'z'=8,'core'=2] {'y','x'}, dimensions={0} | all-to-all | bytes 262144 | tf_op jit(solution)/shard_map/all_to_all | solution.py:190
  49.8 2.3 %shard_map.69 = (f32[4,128]{1,0:T(4,128)}, f32[512,512]{1,0:T(8,128)S(1)}, f32[512,256]{1,0:T(8,128)}) custom-call(s32[3]{0:T(128)S(1)} %pad_add_fusion.place, f32[512,256]{1,0:T(8,128)S(1)} %get-tuple-element.17.items, s32[1,512]{1,0:T(1,128)S(1)} %bitcast.9, f32[512,512]{1,0:T(8,128)S(1)} %get-tuple-element.18.scores, f32[32,8,128]{2,1,0:T(8,128)S(1)} %all_to_all.15.stats), custom_call_target="tpu_custom_call" | custom-call | flops 134217728 | bytes 3280908 | tf_op jit(solution)/shard_map/pallas_call | solution.py:40
  52.0 4.6 %all-to-all-start.1 = ((f32[32,16,256]{2,1,0:T(8,128)}), f32[32,16,256]{2,1,0:T(8,128)S(1)}, u32[]{:S(2)}, u32[]{:S(2)}) async-start(f32[32,16,256]{2,1,0:T(8,128)} %bitcast.6), calls=%async_computation.1 | async-start | bytes 1048576 | tf_op jit(solution)/shard_map/all_to_all | solution.py:190
  56.7 0.6 shard_map.70
  57.3 1.9 %collective-permute-start = (f32[256,256]{1,0:T(8,128)S(1)}, f32[256,256]{1,0:T(8,128)S(1)}, u32[]{:S(2)}, u32[]{:S(2)}) collective-permute-start(f32[256,256]{1,0:T(8,128)S(1)} %get-tuple-element.24), channel_id=1, source_target_pairs={{0,1},{1,0},{2,3},{3,2},{4,5},{5,4},{6,7},{7,6},{8,9},{9,8},{10,11... | collective-permute-start | bytes 786440 | tf_op jit(solution)/shard_map/ppermute | solution.py:199
  59.2 1.5 %collective-permute-done.b = f32[256,256]{1,0:T(8,128)S(1)} collective-permute-done((f32[256,256]{1,0:T(8,128)S(1)}, f32[256,256]{1,0:T(8,128)S(1)}, u32[]{:S(2)}, u32[]{:S(2)}) %collective-permute-start) | collective-permute-done | bytes 262176 | tf_op jit(solution)/shard_map/ppermute | solution.py:199
  60.7 0.6 shard_map.71
  61.3 1.9 %collective-permute-start.1 = (f32[128,256]{1,0:T(8,128)S(1)}, f32[128,256]{1,0:T(8,128)S(1)}, u32[]{:S(2)}, u32[]{:S(2)}) collective-permute-start(f32[128,256]{1,0:T(8,128)S(1)} %get-tuple-element.26), channel_id=1, source_target_pairs={{0,2},{1,3},{2,0},{3,1},{4,6},{5,7},{6,4},{7,5},{8,10},{9,11},{10,... | collective-permute-start | bytes 393224 | tf_op jit(solution)/shard_map/ppermute | solution.py:199
  63.2 5.5 %collective-permute-done.1.b = f32[128,256]{1,0:T(8,128)S(1)} collective-permute-done((f32[128,256]{1,0:T(8,128)S(1)}, f32[128,256]{1,0:T(8,128)S(1)}, u32[]{:S(2)}, u32[]{:S(2)}) %collective-permute-start.1) | collective-permute-done | bytes 131104 | tf_op jit(solution)/shard_map/ppermute | solution.py:199
  69.3 4.1 %all-to-all-done.1.refs_0_ = f32[32,16,256]{2,1,0:T(8,128)S(1)} async-done(((f32[32,16,256]{2,1,0:T(8,128)}), f32[32,16,256]{2,1,0:T(8,128)S(1)}, u32[]{:S(2)}, u32[]{:S(2)}) %all-to-all-start.1) | async-done | bytes 524320 | tf_op jit(solution)/shard_map/all_to_all | solution.py:190
  73.4 0.9 shard_map.73
  74.3 5.8 %all-to-all-start.2 = ((f32[32,16,256]{2,1,0:T(8,128)}), f32[32,16,256]{2,1,0:T(8,128)S(1)}, u32[]{:S(2)}, u32[]{:S(2)}) async-start(f32[32,16,256]{2,1,0:T(8,128)} %shard_map.73), calls=%async_computation.2 | async-start | bytes 1048576 | tf_op jit(solution)/shard_map/all_to_all | solution.py:190
  80.1 3.4 %collective-permute-start.2 = (f32[32,256]{1,0:T(8,128)S(1)}, f32[32,256]{1,0:T(8,128)S(1)}, u32[]{:S(2)}, u32[]{:S(2)}) collective-permute-start(f32[32,256]{1,0:T(8,128)S(1)} %get-tuple-element.28), channel_id=1, source_target_pairs={{0,8},{1,9},{2,10},{3,11},{4,12},{5,13},{6,14},{7,15},{8,0},{9,1},... | collective-permute-start | bytes 98312 | tf_op jit(solution)/shard_map/ppermute | solution.py:199
  83.4 3.1 %collective-permute-start.3 = (f32[32,256]{1,0:T(8,128)S(1)}, f32[32,256]{1,0:T(8,128)S(1)}, u32[]{:S(2)}, u32[]{:S(2)}) collective-permute-start(f32[32,256]{1,0:T(8,128)S(1)} %get-tuple-element.29), channel_id=1, source_target_pairs={{0,4},{1,5},{2,6},{3,7},{4,8},{5,9},{6,10},{7,11},{8,12},{9,13},{1... | collective-permute-start | bytes 98312 | tf_op jit(solution)/shard_map/ppermute | solution.py:199
  86.5 4.9 %collective-permute-start.4 = (f32[32,256]{1,0:T(8,128)S(1)}, f32[32,256]{1,0:T(8,128)S(1)}, u32[]{:S(2)}, u32[]{:S(2)}) collective-permute-start(f32[32,256]{1,0:T(8,128)S(1)} %get-tuple-element.30), channel_id=1, source_target_pairs={{0,12},{1,13},{2,14},{3,15},{4,0},{5,1},{6,2},{7,3},{8,4},{9,5},{1... | collective-permute-start | bytes 98312 | tf_op jit(solution)/shard_map/ppermute | solution.py:199
  91.4 2.9 %collective-permute-done.4.refs_3_ = f32[32,256]{1,0:T(8,128)S(1)} collective-permute-done((f32[32,256]{1,0:T(8,128)S(1)}, f32[32,256]{1,0:T(8,128)S(1)}, u32[]{:S(2)}, u32[]{:S(2)}) %collective-permute-start.4) | collective-permute-done | bytes 32800 | tf_op jit(solution)/shard_map/ppermute | solution.py:199
  94.3 0.6 shard_map.74
  94.9 1.9 %all-to-all-done.2 = f32[32,16,256]{2,1,0:T(8,128)S(1)} async-done(((f32[32,16,256]{2,1,0:T(8,128)}), f32[32,16,256]{2,1,0:T(8,128)S(1)}, u32[]{:S(2)}, u32[]{:S(2)}) %all-to-all-start.2) | async-done | bytes 524320 | tf_op jit(solution)/shard_map/all_to_all | solution.py:190
  96.8 0.8 copy.8
  (10 shorter events, 0.7 us)
Async XLA Ops:
  0.6 26.5 %copy-start = (f32[512,256]{1,0:T(8,128)S(1)}, f32[512,256]{1,0:T(8,128)}, u32[]{:S(2)}) copy-start(f32[512,256]{1,0:T(8,128)} %users.3) | copy-start | bytes 1572868
  0.6 0.8 copy-start.1
  1.5 0.7 copy-start.3
  27.1 0.7 copy-start.2
  52.0 21.3 %all-to-all-start.1 = ((f32[32,16,256]{2,1,0:T(8,128)}), f32[32,16,256]{2,1,0:T(8,128)S(1)}, u32[]{:S(2)}, u32[]{:S(2)}) async-start(f32[32,16,256]{2,1,0:T(8,128)} %bitcast.6), calls=%async_computation.1 | async-start | bytes 1048576 | tf_op jit(solution)/shard_map/all_to_all | solution.py:190
  57.3 3.4 %collective-permute-start = (f32[256,256]{1,0:T(8,128)S(1)}, f32[256,256]{1,0:T(8,128)S(1)}, u32[]{:S(2)}, u32[]{:S(2)}) collective-permute-start(f32[256,256]{1,0:T(8,128)S(1)} %get-tuple-element.24), channel_id=1, source_target_pairs={{0,1},{1,0},{2,3},{3,2},{4,5},{5,4},{6,7},{7,6},{8,9},{9,8},{10,11... | collective-permute-start | bytes 786440 | tf_op jit(solution)/shard_map/ppermute | solution.py:199
  61.3 7.4 %collective-permute-start.1 = (f32[128,256]{1,0:T(8,128)S(1)}, f32[128,256]{1,0:T(8,128)S(1)}, u32[]{:S(2)}, u32[]{:S(2)}) collective-permute-start(f32[128,256]{1,0:T(8,128)S(1)} %get-tuple-element.26), channel_id=1, source_target_pairs={{0,2},{1,3},{2,0},{3,1},{4,6},{5,7},{6,4},{7,5},{8,10},{9,11},{10,... | collective-permute-start | bytes 393224 | tf_op jit(solution)/shard_map/ppermute | solution.py:199
  74.3 22.5 %all-to-all-start.2 = ((f32[32,16,256]{2,1,0:T(8,128)}), f32[32,16,256]{2,1,0:T(8,128)S(1)}, u32[]{:S(2)}, u32[]{:S(2)}) async-start(f32[32,16,256]{2,1,0:T(8,128)} %shard_map.73), calls=%async_computation.2 | async-start | bytes 1048576 | tf_op jit(solution)/shard_map/all_to_all | solution.py:190
  80.1 11.3 %collective-permute-start.2 = (f32[32,256]{1,0:T(8,128)S(1)}, f32[32,256]{1,0:T(8,128)S(1)}, u32[]{:S(2)}, u32[]{:S(2)}) collective-permute-start(f32[32,256]{1,0:T(8,128)S(1)} %get-tuple-element.28), channel_id=1, source_target_pairs={{0,8},{1,9},{2,10},{3,11},{4,12},{5,13},{6,14},{7,15},{8,0},{9,1},... | collective-permute-start | bytes 98312 | tf_op jit(solution)/shard_map/ppermute | solution.py:199
  83.4 8.0 %collective-permute-start.3 = (f32[32,256]{1,0:T(8,128)S(1)}, f32[32,256]{1,0:T(8,128)S(1)}, u32[]{:S(2)}, u32[]{:S(2)}) collective-permute-start(f32[32,256]{1,0:T(8,128)S(1)} %get-tuple-element.29), channel_id=1, source_target_pairs={{0,4},{1,5},{2,6},{3,7},{4,8},{5,9},{6,10},{7,11},{8,12},{9,13},{1... | collective-permute-start | bytes 98312 | tf_op jit(solution)/shard_map/ppermute | solution.py:199
  86.5 7.8 %collective-permute-start.4 = (f32[32,256]{1,0:T(8,128)S(1)}, f32[32,256]{1,0:T(8,128)S(1)}, u32[]{:S(2)}, u32[]{:S(2)}) collective-permute-start(f32[32,256]{1,0:T(8,128)S(1)} %get-tuple-element.30), channel_id=1, source_target_pairs={{0,12},{1,13},{2,14},{3,15},{4,0},{5,1},{6,2},{7,3},{8,4},{9,5},{1... | collective-permute-start | bytes 98312 | tf_op jit(solution)/shard_map/ppermute | solution.py:199

commit v6 on v5

--- a/solution.py
+++ b/solution.py
@@ -179,11 +179,15 @@
         out[...] = a[rows, :] + b[rows, :]
 
 
-def sum_body(*refs):
-    total = refs[0][...]
-    for ref in refs[1:-1]:
+def finish_body(user_rows, *refs):
+    terms, (item_grad, user_grad, sent) = refs[:-3], refs[-3:]
+    copy = pltpu.make_async_copy(user_rows, user_grad, sent.at[0])
+    copy.start()
+    total = terms[0][...]
+    for ref in terms[1:]:
         total = total + ref[...]
-    refs[-1][...] = total
+    item_grad[...] = total
+    copy.wait()
 
 
 def exchange(value, axis):
@@ -227,11 +231,18 @@
         deal_body, [f32(OWN, E)] * (Z // 2), (place, mine, arrived), scalars=1,
     )
     spread = call(add_spread_body, f32(GROUPS, SHARE, E), (parts,), after=(pieces[0],))
-    user_grad = exchange(spread, PEERS).reshape(ROWS, E)
+    user_rows = exchange(spread, PEERS).reshape(ROWS, E)
     terms = [pieces[0]]
     for r in (2, 1, 3):
         terms.append(move(pieces[r], lambda z, c, r=r: (z + 2 * r, c)))
-    item_grad = call(sum_body, f32(OWN, E), terms)
+    item_grad, user_grad = pl.pallas_call(
+        finish_body,
+        out_shape=(f32(OWN, E), f32(ROWS, E)),
+        in_specs=[pl.BlockSpec(memory_space=pl.ANY)] + [vmem()] * len(terms),
+        out_specs=(vmem(), pl.BlockSpec(memory_space=pl.ANY)),
+        scratch_shapes=[pltpu.SemaphoreType.DMA((1,))],
+        compiler_params=pltpu.CompilerParams(vmem_limit_bytes=VMEM_LIMIT),
+    )(user_rows, *terms)
     return (loss.reshape(ROWS), user_grad, item_grad)
 
 

time: 98.2 us -> 98.8 us (level)
    pallas_call x0 -> x1, Pallas kernels: none -> 1.41 us  [per_device(): pl.pallas_call(finish_body, out_shape=(f32(OWN, E), f32(ROWS, E)), in_spe...]
    unnamed x9 -> x8, local copies, waits for them, and re-layouts: 2.86 us -> 2.07 us
    pallas_call x8 -> x7, Pallas kernels: 7.45 us -> 6.83 us  [call(): pl.pallas_call((lambda *refs: body(*refs[:last], *refs[last + len(after):...]
where the time goes in v6:
time: 98.8 us; the launch traced here: 98.2 us
  blocking collectives  45 us (46%)
  starting transfers between devices  25.6 us (26%)
  waiting for transfers between devices  16.5 us (17%)
  Pallas kernels  8.24 us (8%)
  local copies, waits for them, and re-layouts  2.07 us (2%)
    all_gather x1, blocking collectives, per_device(): packed = lax.all_gather(packed, USER_AXES, axis=0, tiled=True)  24.9 us
    all_to_all x1, blocking collectives, exchange(): return lax.all_to_all(value, axis, split_axis=0, concat_axis=0, tiled=True)  20.1 us
    ppermute x5, starting transfers between devices, move(): return lax.ppermute(value, USER_AXES, pairs)  15.1 us
    all_to_all x2, starting transfers between devices, exchange(): return lax.all_to_all(value, axis, split_axis=0, concat_axis=0, tiled=True)  10.4 us
    ppermute x5, waiting for transfers between devices, move(): return lax.ppermute(value, USER_AXES, pairs)  9.87 us
    pallas_call x7, Pallas kernels, call(): pl.pallas_call((lambda *refs: body(*refs[:last], *refs[last + len(after):...  6.83 us
    all_to_all x2, waiting for transfers between devices, exchange(): return lax.all_to_all(value, axis, split_axis=0, concat_axis=0, tiled=True)  6.62 us
    unnamed x8, local copies, waits for them, and re-layouts  2.07 us
  transfers between devices with their start and end apart: 7, of which 5 were waited for; matrix products, arithmetic and copies ran while one was open for 0% of the time, Pallas kernels for 2%

profile of v6, /device:TPU:8, one launch (start us, length us, event | category | flops | bytes accessed | tf_op | source)
XLA Modules:
  0.0 98.2 jit_solution(11894097847801353330)
XLA Ops:
  0.7 0.8 copy-done.1
  1.5 0.7 copy-done.3
  2.1 24.9 %all_gather.3.packed = f32[640,256]{1,0:T(8,128)S(1)} all-gather(f32[40,256]{1,0:T(8,128)S(1)} %shard_map.67), channel_id=1, replica_groups=mesh['x'=4,'y'=8,'z'=8,'core'=2] {'z','core'}, dimensions={0}, use_global_device_ids=true | all-gather | bytes 696320 | tf_op jit(solution)/shard_map/all_gather | solution.py:213
  27.1 0.6 copy-done.2
  27.7 1.9 %shard_map.68 = (f32[512,256]{1,0:T(8,128)S(1)}, f32[512,512]{1,0:T(8,128)S(1)}, f32[32,8,128]{2,1,0:T(8,128)S(1)}) custom-call(s32[3]{0:T(128)S(1)} %pad_add_fusion.place, f32[512,256]{1,0:T(8,128)S(1)} %copy-done, f32[640,256]{1,0:T(8,128)S(1)} %all_gather.3.packed, s32[1,512]{1,0:T(1,128)S(1)} %bitcast.9), custom_call_target="tpu_custom_call" | custom-call | flops 134217728 | bytes 2885644 | tf_op jit(solution)/shard_map/pallas_call | solution.py:40
  29.7 20.1 %all_to_all.15.stats = f32[32,8,128]{2,1,0:T(8,128)S(1)} all-to-all(f32[32,8,128]{2,1,0:T(8,128)S(1)} %get-tuple-element.21), channel_id=1, replica_groups=mesh['x'=4,'y'=8,'z'=8,'core'=2] {'y','x'}, dimensions={0} | all-to-all | bytes 262144 | tf_op jit(solution)/shard_map/all_to_all | solution.py:194
  49.8 2.3 %shard_map.69 = (f32[4,128]{1,0:T(4,128)}, f32[512,512]{1,0:T(8,128)S(1)}, f32[512,256]{1,0:T(8,128)}) custom-call(s32[3]{0:T(128)S(1)} %pad_add_fusion.place, f32[512,256]{1,0:T(8,128)S(1)} %get-tuple-element.19.items, s32[1,512]{1,0:T(1,128)S(1)} %bitcast.10, f32[512,512]{1,0:T(8,128)S(1)} %get-tuple-element.20.scores, f32[32,8,128]{2,1,0:T(8,128)S(1)} %all_to_all.15.stats), custom_call_target="tpu_custom_call" | custom-call | flops 134217728 | bytes 3280908 | tf_op jit(solution)/shard_map/pallas_call | solution.py:40
  52.0 4.6 %all-to-all-start.1 = ((f32[32,16,256]{2,1,0:T(8,128)}), f32[32,16,256]{2,1,0:T(8,128)S(1)}, u32[]{:S(2)}, u32[]{:S(2)}) async-start(f32[32,16,256]{2,1,0:T(8,128)} %bitcast.6), calls=%async_computation.1 | async-start | bytes 1048576 | tf_op jit(solution)/shard_map/all_to_all | solution.py:194
  56.7 0.6 shard_map.70
  57.3 1.9 %collective-permute-start = (f32[256,256]{1,0:T(8,128)S(1)}, f32[256,256]{1,0:T(8,128)S(1)}, u32[]{:S(2)}, u32[]{:S(2)}) collective-permute-start(f32[256,256]{1,0:T(8,128)S(1)} %get-tuple-element.26), channel_id=1, source_target_pairs={{0,1},{1,0},{2,3},{3,2},{4,5},{5,4},{6,7},{7,6},{8,9},{9,8},{10,11... | collective-permute-start | bytes 786440 | tf_op jit(solution)/shard_map/ppermute | solution.py:203
  59.2 1.5 %collective-permute-done.b = f32[256,256]{1,0:T(8,128)S(1)} collective-permute-done((f32[256,256]{1,0:T(8,128)S(1)}, f32[256,256]{1,0:T(8,128)S(1)}, u32[]{:S(2)}, u32[]{:S(2)}) %collective-permute-start) | collective-permute-done | bytes 262176 | tf_op jit(solution)/shard_map/ppermute | solution.py:203
  60.7 0.6 shard_map.71
  61.3 1.9 %collective-permute-start.1 = (f32[128,256]{1,0:T(8,128)S(1)}, f32[128,256]{1,0:T(8,128)S(1)}, u32[]{:S(2)}, u32[]{:S(2)}) collective-permute-start(f32[128,256]{1,0:T(8,128)S(1)} %get-tuple-element.28), channel_id=1, source_target_pairs={{0,2},{1,3},{2,0},{3,1},{4,6},{5,7},{6,4},{7,5},{8,10},{9,11},{10,... | collective-permute-start | bytes 393224 | tf_op jit(solution)/shard_map/ppermute | solution.py:203
  63.2 5.5 %collective-permute-done.1.b = f32[128,256]{1,0:T(8,128)S(1)} collective-permute-done((f32[128,256]{1,0:T(8,128)S(1)}, f32[128,256]{1,0:T(8,128)S(1)}, u32[]{:S(2)}, u32[]{:S(2)}) %collective-permute-start.1) | collective-permute-done | bytes 131104 | tf_op jit(solution)/shard_map/ppermute | solution.py:203
  68.7 0.6 shard_map.72
  69.3 4.1 %all-to-all-done.1.refs_0_ = f32[32,16,256]{2,1,0:T(8,128)S(1)} async-done(((f32[32,16,256]{2,1,0:T(8,128)}), f32[32,16,256]{2,1,0:T(8,128)S(1)}, u32[]{:S(2)}, u32[]{:S(2)}) %all-to-all-start.1) | async-done | bytes 524320 | tf_op jit(solution)/shard_map/all_to_all | solution.py:194
  73.4 0.9 shard_map.73
  74.3 5.8 %all-to-all-start.2 = ((f32[32,16,256]{2,1,0:T(8,128)}), f32[32,16,256]{2,1,0:T(8,128)S(1)}, u32[]{:S(2)}, u32[]{:S(2)}) async-start(f32[32,16,256]{2,1,0:T(8,128)} %shard_map.73), calls=%async_computation.2 | async-start | bytes 1048576 | tf_op jit(solution)/shard_map/all_to_all | solution.py:194
  80.1 3.4 %collective-permute-start.2 = (f32[32,256]{1,0:T(8,128)S(1)}, f32[32,256]{1,0:T(8,128)S(1)}, u32[]{:S(2)}, u32[]{:S(2)}) collective-permute-start(f32[32,256]{1,0:T(8,128)S(1)} %get-tuple-element.30), channel_id=1, source_target_pairs={{0,8},{1,9},{2,10},{3,11},{4,12},{5,13},{6,14},{7,15},{8,0},{9,1},... | collective-permute-start | bytes 98312 | tf_op jit(solution)/shard_map/ppermute | solution.py:203
  83.4 3.1 %collective-permute-start.3 = (f32[32,256]{1,0:T(8,128)S(1)}, f32[32,256]{1,0:T(8,128)S(1)}, u32[]{:S(2)}, u32[]{:S(2)}) collective-permute-start(f32[32,256]{1,0:T(8,128)S(1)} %get-tuple-element.31), channel_id=1, source_target_pairs={{0,4},{1,5},{2,6},{3,7},{4,8},{5,9},{6,10},{7,11},{8,12},{9,13},{1... | collective-permute-start | bytes 98312 | tf_op jit(solution)/shard_map/ppermute | solution.py:203
  86.5 4.9 %collective-permute-start.4 = (f32[32,256]{1,0:T(8,128)S(1)}, f32[32,256]{1,0:T(8,128)S(1)}, u32[]{:S(2)}, u32[]{:S(2)}) collective-permute-start(f32[32,256]{1,0:T(8,128)S(1)} %get-tuple-element.32), channel_id=1, source_target_pairs={{0,12},{1,13},{2,14},{3,15},{4,0},{5,1},{6,2},{7,3},{8,4},{9,5},{1... | collective-permute-start | bytes 98312 | tf_op jit(solution)/shard_map/ppermute | solution.py:203
  91.4 2.9 %collective-permute-done.4.refs_3_ = f32[32,256]{1,0:T(8,128)S(1)} collective-permute-done((f32[32,256]{1,0:T(8,128)S(1)}, f32[32,256]{1,0:T(8,128)S(1)}, u32[]{:S(2)}, u32[]{:S(2)}) %collective-permute-start.4) | collective-permute-done | bytes 32800 | tf_op jit(solution)/shard_map/ppermute | solution.py:203
  94.3 2.5 %all-to-all-done.2 = f32[32,16,256]{2,1,0:T(8,128)S(1)} async-done(((f32[32,16,256]{2,1,0:T(8,128)}), f32[32,16,256]{2,1,0:T(8,128)S(1)}, u32[]{:S(2)}, u32[]{:S(2)}) %all-to-all-start.2) | async-done | bytes 524320 | tf_op jit(solution)/shard_map/all_to_all | solution.py:194
  96.8 1.4 %shard_map.74 = (f32[32,256]{1,0:T(8,128)}, f32[512,256]{1,0:T(8,128)}) custom-call(f32[512,256]{1,0:T(8,128)S(1)} %bitcast.8, f32[32,256]{1,0:T(8,128)S(1)} %get-tuple-element.29.refs_1_.refs_0_, f32[32,256]{1,0:T(8,128)S(1)} %collective-permute-done.2.refs_1_, f32[32,256]{1,0:T(8,128)S(1)} %collective-permute-done.3.refs_2_, ...), custom_call_target="tpu_custom_call" | custom-call | tf_op jit(solution)/shard_map/pallas_call | solution.py:238
  (9 shorter events, 0.1 us)
Async XLA Ops:
  0.6 26.5 %copy-start = (f32[512,256]{1,0:T(8,128)S(1)}, f32[512,256]{1,0:T(8,128)}, u32[]{:S(2)}) copy-start(f32[512,256]{1,0:T(8,128)} %users.3) | copy-start | bytes 1572868
  0.6 0.8 copy-start.1
  1.5 0.7 copy-start.3
  27.1 0.7 copy-start.2
  52.0 21.3 %all-to-all-start.1 = ((f32[32,16,256]{2,1,0:T(8,128)}), f32[32,16,256]{2,1,0:T(8,128)S(1)}, u32[]{:S(2)}, u32[]{:S(2)}) async-start(f32[32,16,256]{2,1,0:T(8,128)} %bitcast.6), calls=%async_computation.1 | async-start | bytes 1048576 | tf_op jit(solution)/shard_map/all_to_all | solution.py:194
  57.3 3.4 %collective-permute-start = (f32[256,256]{1,0:T(8,128)S(1)}, f32[256,256]{1,0:T(8,128)S(1)}, u32[]{:S(2)}, u32[]{:S(2)}) collective-permute-start(f32[256,256]{1,0:T(8,128)S(1)} %get-tuple-element.26), channel_id=1, source_target_pairs={{0,1},{1,0},{2,3},{3,2},{4,5},{5,4},{6,7},{7,6},{8,9},{9,8},{10,11... | collective-permute-start | bytes 786440 | tf_op jit(solution)/shard_map/ppermute | solution.py:203
  61.3 7.4 %collective-permute-start.1 = (f32[128,256]{1,0:T(8,128)S(1)}, f32[128,256]{1,0:T(8,128)S(1)}, u32[]{:S(2)}, u32[]{:S(2)}) collective-permute-start(f32[128,256]{1,0:T(8,128)S(1)} %get-tuple-element.28), channel_id=1, source_target_pairs={{0,2},{1,3},{2,0},{3,1},{4,6},{5,7},{6,4},{7,5},{8,10},{9,11},{10,... | collective-permute-start | bytes 393224 | tf_op jit(solution)/shard_map/ppermute | solution.py:203
  74.3 22.5 %all-to-all-start.2 = ((f32[32,16,256]{2,1,0:T(8,128)}), f32[32,16,256]{2,1,0:T(8,128)S(1)}, u32[]{:S(2)}, u32[]{:S(2)}) async-start(f32[32,16,256]{2,1,0:T(8,128)} %shard_map.73), calls=%async_computation.2 | async-start | bytes 1048576 | tf_op jit(solution)/shard_map/all_to_all | solution.py:194
  80.1 11.3 %collective-permute-start.2 = (f32[32,256]{1,0:T(8,128)S(1)}, f32[32,256]{1,0:T(8,128)S(1)}, u32[]{:S(2)}, u32[]{:S(2)}) collective-permute-start(f32[32,256]{1,0:T(8,128)S(1)} %get-tuple-element.30), channel_id=1, source_target_pairs={{0,8},{1,9},{2,10},{3,11},{4,12},{5,13},{6,14},{7,15},{8,0},{9,1},... | collective-permute-start | bytes 98312 | tf_op jit(solution)/shard_map/ppermute | solution.py:203
  83.4 8.0 %collective-permute-start.3 = (f32[32,256]{1,0:T(8,128)S(1)}, f32[32,256]{1,0:T(8,128)S(1)}, u32[]{:S(2)}, u32[]{:S(2)}) collective-permute-start(f32[32,256]{1,0:T(8,128)S(1)} %get-tuple-element.31), channel_id=1, source_target_pairs={{0,4},{1,5},{2,6},{3,7},{4,8},{5,9},{6,10},{7,11},{8,12},{9,13},{1... | collective-permute-start | bytes 98312 | tf_op jit(solution)/shard_map/ppermute | solution.py:203
  86.5 7.8 %collective-permute-start.4 = (f32[32,256]{1,0:T(8,128)S(1)}, f32[32,256]{1,0:T(8,128)S(1)}, u32[]{:S(2)}, u32[]{:S(2)}) collective-permute-start(f32[32,256]{1,0:T(8,128)S(1)} %get-tuple-element.32), channel_id=1, source_target_pairs={{0,12},{1,13},{2,14},{3,15},{4,0},{5,1},{6,2},{7,3},{8,4},{9,5},{1... | collective-permute-start | bytes 98312 | tf_op jit(solution)/shard_map/ppermute | solution.py:203

commit v7 on v6

--- a/solution.py
+++ b/solution.py
@@ -24,6 +24,10 @@
     return pl.BlockSpec(memory_space=pltpu.VMEM)
 
 
+def anywhere():
+    return pl.BlockSpec(memory_space=pl.ANY)
+
+
 def smem():
     return pl.BlockSpec(memory_space=pltpu.SMEM)
 
@@ -32,7 +36,7 @@
     return jax.ShapeDtypeStruct(shape, jnp.float32)
 
 
-def call(body, out_shape, operands, scalars=0, scratch=(), flops=0, after=()):
+def call(body, out_shape, operands, scalars=0, scratch=(), flops=0, after=(), far=()):
     single = not isinstance(out_shape, (tuple, list))
     outs = [out_shape] if single else list(out_shape)
     size = sum(o.size * 4 for o in operands) + sum(4 * s.size for s in outs)
@@ -41,8 +45,8 @@
         (lambda *refs: body(*refs[:last], *refs[last + len(after):])) if after else body,
         out_shape=outs,
         in_specs=[smem()] * scalars + [vmem()] * (len(operands) - scalars)
-        + [pl.BlockSpec(memory_space=pl.ANY)] * len(after),
-        out_specs=[vmem()] * len(outs),
+        + [anywhere()] * len(after),
+        out_specs=[anywhere() if k in far else vmem() for k in range(len(outs))],
         scratch_shapes=list(scratch),
         compiler_params=pltpu.CompilerParams(vmem_limit_bytes=VMEM_LIMIT),
         cost_estimate=pl.CostEstimate(flops=flops, bytes_accessed=size, transcendentals=0),
@@ -128,7 +132,7 @@
         stats[d, :, :] = one
 
 
-def user_body(place, items, positive, scores, stats, loss, grad, user_part):
+def user_body(place, items, positive, scores, stats, loss, grad, user_part, block, sent):
     highest = stats[0, 0:4, :]
     for d in range(1, GROUPS):
         highest = jnp.maximum(highest, stats[d, 0:4, :])
@@ -137,15 +141,24 @@
     for d in range(GROUPS):
         total = total + jnp.exp(stats[d, 0:4, :] - highest)
         picked = picked + stats[d, 4:8, :]
-    log_total = highest + jnp.log(total)
-    loss[...] = log_total - picked
-    level = jnp.concatenate([log_total[k:k + 1, :] for k in range(4)], axis=1)
+    above = jnp.log(total)
+    loss[...] = (highest + above) - picked
+    base = jnp.concatenate([highest[k:k + 1, :] for k in range(4)], axis=1)
+    above = jnp.concatenate([above[k:k + 1, :] for k in range(4)], axis=1)
     wanted = positive[...]
     for k in range(MEMBERS):
         at = slice(OWN * k, OWN * (k + 1))
         hit = hits(place, wanted, k)
-        grad[at, :] = jnp.exp(scores[at, :] - level) - jnp.where(hit, 1.0, 0.0)
-    user_part[...] = dot_split(split(grad[...]), split(items[...]), 0, 0)
+        grad[at, :] = jnp.exp((scores[at, :] - base) - above) - jnp.where(hit, 1.0, 0.0)
+    right = split(items[...])
+    copies = []
+    for k in range(4):
+        at = pl.ds(128 * k, 128)
+        block[at, :] = dot_split(split(grad[:, 128 * k:128 * (k + 1)]), right, 0, 0)
+        copies.append(pltpu.make_async_copy(block.at[at, :], user_part.at[at, :], sent.at[k]))
+        copies[-1].start()
+    for copy in copies:
+        copy.wait()
 
 
 def item_body(users, grad, mine, theirs):
@@ -154,12 +167,16 @@
     mine[...] = dot_split(split(grad[0:HALF, :]), right, 1, 0)
 
 
-def add_spread_body(parts, out):
+def add_spread_body(parts, out, block, sent):
     total = parts[0]
     for r in range(1, parts.shape[0]):
         total = total + parts[r]
-    for r in range(out.shape[0]):
-        out[r] = total
+    block[...] = total
+    copies = [pltpu.make_async_copy(block, out.at[d], sent.at[d]) for d in range(GROUPS)]
+    for copy in copies:
+        copy.start()
+    for copy in copies:
+        copy.wait()
 
 
 def halve_body(place, a, b, keep, send):
@@ -181,13 +198,17 @@
 
 def finish_body(user_rows, *refs):
     terms, (item_grad, user_grad, sent) = refs[:-3], refs[-3:]
-    copy = pltpu.make_async_copy(user_rows, user_grad, sent.at[0])
-    copy.start()
+    copies = []
+    for k in range(8):
+        at = pl.ds(ROWS // 8 * k, ROWS // 8)
+        copies.append(pltpu.make_async_copy(user_rows.at[at, :], user_grad.at[at, :], sent.at[k]))
+        copies[-1].start()
     total = terms[0][...]
     for ref in terms[1:]:
         total = total + ref[...]
     item_grad[...] = total
-    copy.wait()
+    for copy in copies:
+        copy.wait()
 
 
 def exchange(value, axis):
@@ -218,7 +239,8 @@
     stats = exchange(stats, PEERS)
     loss, grad, user_part = call(
         user_body, (f32(4, 128), f32(SLAB, ROWS), f32(ROWS, E)),
-        (place, items, positive, scores, stats), scalars=1, flops=product,
+        (place, items, positive, scores, stats), scalars=1, flops=product, far=(2,),
+        scratch=[pltpu.VMEM((ROWS, E), jnp.float32), pltpu.SemaphoreType.DMA((4,))],
     )
     parts = exchange(user_part.reshape(GROUPS, SHARE, E), PEERS)
     mine, theirs = call(item_body, (f32(HALF, E), f32(HALF, E)), (user_vectors, grad), flops=product)
@@ -230,7 +252,10 @@
     pieces = call(
         deal_body, [f32(OWN, E)] * (Z // 2), (place, mine, arrived), scalars=1,
     )
-    spread = call(add_spread_body, f32(GROUPS, SHARE, E), (parts,), after=(pieces[0],))
+    spread = call(
+        add_spread_body, f32(GROUPS, SHARE, E), (parts,), after=(pieces[0],), far=(0,),
+        scratch=[pltpu.VMEM((SHARE, E), jnp.float32), pltpu.SemaphoreType.DMA((GROUPS,))],
+    )
     user_rows = exchange(spread, PEERS).reshape(ROWS, E)
     terms = [pieces[0]]
     for r in (2, 1, 3):
@@ -240,7 +265,7 @@
         out_shape=(f32(OWN, E), f32(ROWS, E)),
         in_specs=[pl.BlockSpec(memory_space=pl.ANY)] + [vmem()] * len(terms),
         out_specs=(vmem(), pl.BlockSpec(memory_space=pl.ANY)),
-        scratch_shapes=[pltpu.SemaphoreType.DMA((1,))],
+        scratch_shapes=[pltpu.SemaphoreType.DMA((8,))],
         compiler_params=pltpu.CompilerParams(vmem_limit_bytes=VMEM_LIMIT),
     )(user_rows, *terms)
     return (loss.reshape(ROWS), user_grad, item_grad)

time: 98.8 us -> 99.5 us (level)
  no operation moved by 1% of the time
where the time goes in v7:
time: 99.5 us; the launch traced here: 99 us
  blocking collectives  45 us (45%)
  starting transfers between devices  25.6 us (26%)
  waiting for transfers between devices  16.5 us (17%)
  Pallas kernels  8.98 us (9%)
  local copies, waits for them, and re-layouts  2.07 us (2%)
    all_gather x1, blocking collectives, per_device(): packed = lax.all_gather(packed, USER_AXES, axis=0, tiled=True)  24.9 us
    all_to_all x1, blocking collectives, exchange(): return lax.all_to_all(value, axis, split_axis=0, concat_axis=0, tiled=True)  20.1 us
    ppermute x5, starting transfers between devices, move(): return lax.ppermute(value, USER_AXES, pairs)  15.2 us
    all_to_all x2, starting transfers between devices, exchange(): return lax.all_to_all(value, axis, split_axis=0, concat_axis=0, tiled=True)  10.4 us
    ppermute x5, waiting for transfers between devices, move(): return lax.ppermute(value, USER_AXES, pairs)  9.86 us
    pallas_call x7, Pallas kernels, call(): pl.pallas_call((lambda *refs: body(*refs[:last], *refs[last + len(after):...  7.52 us
    all_to_all x2, waiting for transfers between devices, exchange(): return lax.all_to_all(value, axis, split_axis=0, concat_axis=0, tiled=True)  6.62 us
    unnamed x8, local copies, waits for them, and re-layouts  2.07 us
  transfers between devices with their start and end apart: 7, of which 5 were waited for; matrix products, arithmetic and copies ran while one was open for 0% of the time, Pallas kernels for 2%

profile of v7, /device:TPU:8, one launch (start us, length us, event | category | flops | bytes accessed | tf_op | source)
XLA Modules:
  0.0 99.0 jit_solution(2955470620278837379)
XLA Ops:
  0.7 0.8 copy-done.1
  1.5 0.7 copy-done.3
  2.1 24.9 %all_gather.3.packed = f32[640,256]{1,0:T(8,128)S(1)} all-gather(f32[40,256]{1,0:T(8,128)S(1)} %shard_map.67), channel_id=1, replica_groups=mesh['x'=4,'y'=8,'z'=8,'core'=2] {'z','core'}, dimensions={0}, use_global_device_ids=true | all-gather | bytes 696320 | tf_op jit(solution)/shard_map/all_gather | solution.py:234
  27.1 0.6 copy-done.2
  27.7 1.9 %shard_map.68 = (f32[512,256]{1,0:T(8,128)S(1)}, f32[512,512]{1,0:T(8,128)S(1)}, f32[32,8,128]{2,1,0:T(8,128)S(1)}) custom-call(s32[3]{0:T(128)S(1)} %pad_add_fusion.place, f32[512,256]{1,0:T(8,128)S(1)} %copy-done, f32[640,256]{1,0:T(8,128)S(1)} %all_gather.3.packed, s32[1,512]{1,0:T(1,128)S(1)} %bitcast.9), custom_call_target="tpu_custom_call" | custom-call | flops 134217728 | bytes 2885644 | tf_op jit(solution)/shard_map/pallas_call | solution.py:44
  29.7 20.1 %all_to_all.15.stats = f32[32,8,128]{2,1,0:T(8,128)S(1)} all-to-all(f32[32,8,128]{2,1,0:T(8,128)S(1)} %get-tuple-element.21), channel_id=1, replica_groups=mesh['x'=4,'y'=8,'z'=8,'core'=2] {'y','x'}, dimensions={0} | all-to-all | bytes 262144 | tf_op jit(solution)/shard_map/all_to_all | solution.py:215
  49.8 2.8 %shard_map.69 = (f32[4,128]{1,0:T(4,128)}, f32[512,512]{1,0:T(8,128)S(1)}, f32[512,256]{1,0:T(8,128)}) custom-call(s32[3]{0:T(128)S(1)} %pad_add_fusion.place, f32[512,256]{1,0:T(8,128)S(1)} %get-tuple-element.19.items, s32[1,512]{1,0:T(1,128)S(1)} %bitcast.10, f32[512,512]{1,0:T(8,128)S(1)} %get-tuple-element.20.scores, f32[32,8,128]{2,1,0:T(8,128)S(1)} %all_to_all.15.stats), custom_call_target="tpu_custom_call" | custom-call | flops 134217728 | bytes 3280908 | tf_op jit(solution)/shard_map/pallas_call | solution.py:44
  52.5 4.6 %all-to-all-start.1 = ((f32[32,16,256]{2,1,0:T(8,128)}), f32[32,16,256]{2,1,0:T(8,128)S(1)}, u32[]{:S(2)}, u32[]{:S(2)}) async-start(f32[32,16,256]{2,1,0:T(8,128)} %bitcast.6), calls=%async_computation.1 | async-start | bytes 1048576 | tf_op jit(solution)/shard_map/all_to_all | solution.py:215
  57.2 0.6 shard_map.70
  57.8 1.9 %collective-permute-start = (f32[256,256]{1,0:T(8,128)S(1)}, f32[256,256]{1,0:T(8,128)S(1)}, u32[]{:S(2)}, u32[]{:S(2)}) collective-permute-start(f32[256,256]{1,0:T(8,128)S(1)} %get-tuple-element.26), channel_id=1, source_target_pairs={{0,1},{1,0},{2,3},{3,2},{4,5},{5,4},{6,7},{7,6},{8,9},{9,8},{10,11... | collective-permute-start | bytes 786440 | tf_op jit(solution)/shard_map/ppermute | solution.py:224
  59.7 1.5 %collective-permute-done.b = f32[256,256]{1,0:T(8,128)S(1)} collective-permute-done((f32[256,256]{1,0:T(8,128)S(1)}, f32[256,256]{1,0:T(8,128)S(1)}, u32[]{:S(2)}, u32[]{:S(2)}) %collective-permute-start) | collective-permute-done | bytes 262176 | tf_op jit(solution)/shard_map/ppermute | solution.py:224
  61.2 0.6 shard_map.71
  61.8 1.9 %collective-permute-start.1 = (f32[128,256]{1,0:T(8,128)S(1)}, f32[128,256]{1,0:T(8,128)S(1)}, u32[]{:S(2)}, u32[]{:S(2)}) collective-permute-start(f32[128,256]{1,0:T(8,128)S(1)} %get-tuple-element.28), channel_id=1, source_target_pairs={{0,2},{1,3},{2,0},{3,1},{4,6},{5,7},{6,4},{7,5},{8,10},{9,11},{10,... | collective-permute-start | bytes 393224 | tf_op jit(solution)/shard_map/ppermute | solution.py:224
  63.7 5.5 %collective-permute-done.1.b = f32[128,256]{1,0:T(8,128)S(1)} collective-permute-done((f32[128,256]{1,0:T(8,128)S(1)}, f32[128,256]{1,0:T(8,128)S(1)}, u32[]{:S(2)}, u32[]{:S(2)}) %collective-permute-start.1) | collective-permute-done | bytes 131104 | tf_op jit(solution)/shard_map/ppermute | solution.py:224
  69.2 0.6 shard_map.72
  69.8 4.1 %all-to-all-done.1.refs_0_ = f32[32,16,256]{2,1,0:T(8,128)S(1)} async-done(((f32[32,16,256]{2,1,0:T(8,128)}), f32[32,16,256]{2,1,0:T(8,128)S(1)}, u32[]{:S(2)}, u32[]{:S(2)}) %all-to-all-start.1) | async-done | bytes 524320 | tf_op jit(solution)/shard_map/all_to_all | solution.py:215
  73.9 1.1 %shard_map.73 = f32[32,16,256]{2,1,0:T(8,128)} custom-call(f32[32,16,256]{2,1,0:T(8,128)S(1)} %all-to-all-done.1.refs_0_, f32[32,256]{1,0:T(8,128)S(1)} %get-tuple-element.29.refs_1_.refs_0_), custom_call_target="tpu_custom_call" | custom-call | bytes 1048576 | tf_op jit(solution)/shard_map/pallas_call | solution.py:44
  75.0 5.8 %all-to-all-start.2 = ((f32[32,16,256]{2,1,0:T(8,128)}), f32[32,16,256]{2,1,0:T(8,128)S(1)}, u32[]{:S(2)}, u32[]{:S(2)}) async-start(f32[32,16,256]{2,1,0:T(8,128)} %shard_map.73), calls=%async_computation.2 | async-start | bytes 1048576 | tf_op jit(solution)/shard_map/all_to_all | solution.py:215
  80.8 3.4 %collective-permute-start.2 = (f32[32,256]{1,0:T(8,128)S(1)}, f32[32,256]{1,0:T(8,128)S(1)}, u32[]{:S(2)}, u32[]{:S(2)}) collective-permute-start(f32[32,256]{1,0:T(8,128)S(1)} %get-tuple-element.30), channel_id=1, source_target_pairs={{0,8},{1,9},{2,10},{3,11},{4,12},{5,13},{6,14},{7,15},{8,0},{9,1},... | collective-permute-start | bytes 98312 | tf_op jit(solution)/shard_map/ppermute | solution.py:224
  84.2 3.1 %collective-permute-start.3 = (f32[32,256]{1,0:T(8,128)S(1)}, f32[32,256]{1,0:T(8,128)S(1)}, u32[]{:S(2)}, u32[]{:S(2)}) collective-permute-start(f32[32,256]{1,0:T(8,128)S(1)} %get-tuple-element.31), channel_id=1, source_target_pairs={{0,4},{1,5},{2,6},{3,7},{4,8},{5,9},{6,10},{7,11},{8,12},{9,13},{1... | collective-permute-start | bytes 98312 | tf_op jit(solution)/shard_map/ppermute | solution.py:224
  87.2 4.9 %collective-permute-start.4 = (f32[32,256]{1,0:T(8,128)S(1)}, f32[32,256]{1,0:T(8,128)S(1)}, u32[]{:S(2)}, u32[]{:S(2)}) collective-permute-start(f32[32,256]{1,0:T(8,128)S(1)} %get-tuple-element.32), channel_id=1, source_target_pairs={{0,12},{1,13},{2,14},{3,15},{4,0},{5,1},{6,2},{7,3},{8,4},{9,5},{1... | collective-permute-start | bytes 98312 | tf_op jit(solution)/shard_map/ppermute | solution.py:224
  92.2 2.8 %collective-permute-done.4.refs_3_ = f32[32,256]{1,0:T(8,128)S(1)} collective-permute-done((f32[32,256]{1,0:T(8,128)S(1)}, f32[32,256]{1,0:T(8,128)S(1)}, u32[]{:S(2)}, u32[]{:S(2)}) %collective-permute-start.4) | collective-permute-done | bytes 32800 | tf_op jit(solution)/shard_map/ppermute | solution.py:224
  95.0 2.5 %all-to-all-done.2 = f32[32,16,256]{2,1,0:T(8,128)S(1)} async-done(((f32[32,16,256]{2,1,0:T(8,128)}), f32[32,16,256]{2,1,0:T(8,128)S(1)}, u32[]{:S(2)}, u32[]{:S(2)}) %all-to-all-start.2) | async-done | bytes 524320 | tf_op jit(solution)/shard_map/all_to_all | solution.py:215
  97.5 1.5 %shard_map.74 = (f32[32,256]{1,0:T(8,128)}, f32[512,256]{1,0:T(8,128)}) custom-call(f32[512,256]{1,0:T(8,128)S(1)} %bitcast.8, f32[32,256]{1,0:T(8,128)S(1)} %get-tuple-element.29.refs_1_.refs_0_, f32[32,256]{1,0:T(8,128)S(1)} %collective-permute-done.2.refs_1_, f32[32,256]{1,0:T(8,128)S(1)} %collective-permute-done.3.refs_2_, ...), custom_call_target="tpu_custom_call" | custom-call | tf_op jit(solution)/shard_map/pallas_call | solution.py:263
  (9 shorter events, 0.1 us)
Async XLA Ops:
  0.6 26.5 %copy-start = (f32[512,256]{1,0:T(8,128)S(1)}, f32[512,256]{1,0:T(8,128)}, u32[]{:S(2)}) copy-start(f32[512,256]{1,0:T(8,128)} %users.3) | copy-start | bytes 1572868
  0.6 0.8 copy-start.1
  1.5 0.7 copy-start.3
  27.1 0.7 copy-start.2
  52.5 21.3 %all-to-all-start.1 = ((f32[32,16,256]{2,1,0:T(8,128)}), f32[32,16,256]{2,1,0:T(8,128)S(1)}, u32[]{:S(2)}, u32[]{:S(2)}) async-start(f32[32,16,256]{2,1,0:T(8,128)} %bitcast.6), calls=%async_computation.1 | async-start | bytes 1048576 | tf_op jit(solution)/shard_map/all_to_all | solution.py:215
  57.8 3.4 %collective-permute-start = (f32[256,256]{1,0:T(8,128)S(1)}, f32[256,256]{1,0:T(8,128)S(1)}, u32[]{:S(2)}, u32[]{:S(2)}) collective-permute-start(f32[256,256]{1,0:T(8,128)S(1)} %get-tuple-element.26), channel_id=1, source_target_pairs={{0,1},{1,0},{2,3},{3,2},{4,5},{5,4},{6,7},{7,6},{8,9},{9,8},{10,11... | collective-permute-start | bytes 786440 | tf_op jit(solution)/shard_map/ppermute | solution.py:224
  61.8 7.4 %collective-permute-start.1 = (f32[128,256]{1,0:T(8,128)S(1)}, f32[128,256]{1,0:T(8,128)S(1)}, u32[]{:S(2)}, u32[]{:S(2)}) collective-permute-start(f32[128,256]{1,0:T(8,128)S(1)} %get-tuple-element.28), channel_id=1, source_target_pairs={{0,2},{1,3},{2,0},{3,1},{4,6},{5,7},{6,4},{7,5},{8,10},{9,11},{10,... | collective-permute-start | bytes 393224 | tf_op jit(solution)/shard_map/ppermute | solution.py:224
  75.0 22.5 %all-to-all-start.2 = ((f32[32,16,256]{2,1,0:T(8,128)}), f32[32,16,256]{2,1,0:T(8,128)S(1)}, u32[]{:S(2)}, u32[]{:S(2)}) async-start(f32[32,16,256]{2,1,0:T(8,128)} %shard_map.73), calls=%async_computation.2 | async-start | bytes 1048576 | tf_op jit(solution)/shard_map/all_to_all | solution.py:215
  80.8 11.3 %collective-permute-start.2 = (f32[32,256]{1,0:T(8,128)S(1)}, f32[32,256]{1,0:T(8,128)S(1)}, u32[]{:S(2)}, u32[]{:S(2)}) collective-permute-start(f32[32,256]{1,0:T(8,128)S(1)} %get-tuple-element.30), channel_id=1, source_target_pairs={{0,8},{1,9},{2,10},{3,11},{4,12},{5,13},{6,14},{7,15},{8,0},{9,1},... | collective-permute-start | bytes 98312 | tf_op jit(solution)/shard_map/ppermute | solution.py:224
  84.2 8.0 %collective-permute-start.3 = (f32[32,256]{1,0:T(8,128)S(1)}, f32[32,256]{1,0:T(8,128)S(1)}, u32[]{:S(2)}, u32[]{:S(2)}) collective-permute-start(f32[32,256]{1,0:T(8,128)S(1)} %get-tuple-element.31), channel_id=1, source_target_pairs={{0,4},{1,5},{2,6},{3,7},{4,8},{5,9},{6,10},{7,11},{8,12},{9,13},{1... | collective-permute-start | bytes 98312 | tf_op jit(solution)/shard_map/ppermute | solution.py:224
  87.2 7.8 %collective-permute-start.4 = (f32[32,256]{1,0:T(8,128)S(1)}, f32[32,256]{1,0:T(8,128)S(1)}, u32[]{:S(2)}, u32[]{:S(2)}) collective-permute-start(f32[32,256]{1,0:T(8,128)S(1)} %get-tuple-element.32), channel_id=1, source_target_pairs={{0,12},{1,13},{2,14},{3,15},{4,0},{5,1},{6,2},{7,3},{8,4},{9,5},{1... | collective-permute-start | bytes 98312 | tf_op jit(solution)/shard_map/ppermute | solution.py:224

commit v8 on v5

--- a/solution.py
+++ b/solution.py
@@ -137,14 +137,15 @@
     for d in range(GROUPS):
         total = total + jnp.exp(stats[d, 0:4, :] - highest)
         picked = picked + stats[d, 4:8, :]
-    log_total = highest + jnp.log(total)
-    loss[...] = log_total - picked
-    level = jnp.concatenate([log_total[k:k + 1, :] for k in range(4)], axis=1)
+    above = jnp.log(total)
+    loss[...] = (highest - picked) + above
+    base = jnp.concatenate([highest[k:k + 1, :] for k in range(4)], axis=1)
+    above = jnp.concatenate([above[k:k + 1, :] for k in range(4)], axis=1)
     wanted = positive[...]
     for k in range(MEMBERS):
         at = slice(OWN * k, OWN * (k + 1))
         hit = hits(place, wanted, k)
-        grad[at, :] = jnp.exp(scores[at, :] - level) - jnp.where(hit, 1.0, 0.0)
+        grad[at, :] = jnp.exp((scores[at, :] - base) - above) - jnp.where(hit, 1.0, 0.0)
     user_part[...] = dot_split(split(grad[...]), split(items[...]), 0, 0)
 
 

time: 98.2 us -> 98.2 us (level)
  no operation moved by 1% of the time
where the time goes in v8:
time: 98.2 us; the launch traced here: 97.6 us
  blocking collectives  45 us (46%)
  starting transfers between devices  25.6 us (26%)
  waiting for transfers between devices  15.9 us (16%)
  Pallas kernels  7.48 us (8%)
  local copies, waits for them, and re-layouts  2.86 us (3%)
    all_gather x1, blocking collectives, per_device(): packed = lax.all_gather(packed, USER_AXES, axis=0, tiled=True)  24.9 us
    all_to_all x1, blocking collectives, exchange(): return lax.all_to_all(value, axis, split_axis=0, concat_axis=0, tiled=True)  20.1 us
    ppermute x5, starting transfers between devices, move(): return lax.ppermute(value, USER_AXES, pairs)  15.1 us
    all_to_all x2, starting transfers between devices, exchange(): return lax.all_to_all(value, axis, split_axis=0, concat_axis=0, tiled=True)  10.4 us
    ppermute x5, waiting for transfers between devices, move(): return lax.ppermute(value, USER_AXES, pairs)  9.87 us
    pallas_call x8, Pallas kernels, call(): pl.pallas_call((lambda *refs: body(*refs[:last], *refs[last + len(after):...  7.48 us
    all_to_all x2, waiting for transfers between devices, exchange(): return lax.all_to_all(value, axis, split_axis=0, concat_axis=0, tiled=True)  5.99 us
    unnamed x9, local copies, waits for them, and re-layouts  2.86 us
  transfers between devices with their start and end apart: 7, of which 5 were waited for; matrix products, arithmetic and copies ran while one was open for 0% of the time, Pallas kernels for 2%

profile of v8, /device:TPU:8, one launch (start us, length us, event | category | flops | bytes accessed | tf_op | source)
XLA Modules:
  0.0 97.6 jit_solution(9809654197184289496)
XLA Ops:
  0.7 0.8 copy-done.1
  1.5 0.7 copy-done.3
  2.1 24.9 %all_gather.3.packed = f32[640,256]{1,0:T(8,128)S(1)} all-gather(f32[40,256]{1,0:T(8,128)S(1)} %shard_map.67), channel_id=1, replica_groups=mesh['x'=4,'y'=8,'z'=8,'core'=2] {'z','core'}, dimensions={0}, use_global_device_ids=true | all-gather | bytes 696320 | tf_op jit(solution)/shard_map/all_gather | solution.py:210
  27.1 0.6 copy-done.2
  27.7 1.9 %shard_map.68 = (f32[512,256]{1,0:T(8,128)S(1)}, f32[512,512]{1,0:T(8,128)S(1)}, f32[32,8,128]{2,1,0:T(8,128)S(1)}) custom-call(s32[3]{0:T(128)S(1)} %pad_add_fusion.place, f32[512,256]{1,0:T(8,128)S(1)} %copy-done, f32[640,256]{1,0:T(8,128)S(1)} %all_gather.3.packed, s32[1,512]{1,0:T(1,128)S(1)} %bitcast.8), custom_call_target="tpu_custom_call" | custom-call | flops 134217728 | bytes 2885644 | tf_op jit(solution)/shard_map/pallas_call | solution.py:40
  29.7 20.1 %all_to_all.15.stats = f32[32,8,128]{2,1,0:T(8,128)S(1)} all-to-all(f32[32,8,128]{2,1,0:T(8,128)S(1)} %get-tuple-element.19), channel_id=1, replica_groups=mesh['x'=4,'y'=8,'z'=8,'core'=2] {'y','x'}, dimensions={0} | all-to-all | bytes 262144 | tf_op jit(solution)/shard_map/all_to_all | solution.py:191
  49.8 2.3 %shard_map.69 = (f32[4,128]{1,0:T(4,128)}, f32[512,512]{1,0:T(8,128)S(1)}, f32[512,256]{1,0:T(8,128)}) custom-call(s32[3]{0:T(128)S(1)} %pad_add_fusion.place, f32[512,256]{1,0:T(8,128)S(1)} %get-tuple-element.17.items, s32[1,512]{1,0:T(1,128)S(1)} %bitcast.9, f32[512,512]{1,0:T(8,128)S(1)} %get-tuple-element.18.scores, f32[32,8,128]{2,1,0:T(8,128)S(1)} %all_to_all.15.stats), custom_call_target="tpu_custom_call" | custom-call | flops 134217728 | bytes 3280908 | tf_op jit(solution)/shard_map/pallas_call | solution.py:40
  52.1 4.6 %all-to-all-start.1 = ((f32[32,16,256]{2,1,0:T(8,128)}), f32[32,16,256]{2,1,0:T(8,128)S(1)}, u32[]{:S(2)}, u32[]{:S(2)}) async-start(f32[32,16,256]{2,1,0:T(8,128)} %bitcast.6), calls=%async_computation.1 | async-start | bytes 1048576 | tf_op jit(solution)/shard_map/all_to_all | solution.py:191
  56.7 0.6 shard_map.70
  57.3 1.9 %collective-permute-start = (f32[256,256]{1,0:T(8,128)S(1)}, f32[256,256]{1,0:T(8,128)S(1)}, u32[]{:S(2)}, u32[]{:S(2)}) collective-permute-start(f32[256,256]{1,0:T(8,128)S(1)} %get-tuple-element.24), channel_id=1, source_target_pairs={{0,1},{1,0},{2,3},{3,2},{4,5},{5,4},{6,7},{7,6},{8,9},{9,8},{10,11... | collective-permute-start | bytes 786440 | tf_op jit(solution)/shard_map/ppermute | solution.py:200
  59.2 1.5 %collective-permute-done.b = f32[256,256]{1,0:T(8,128)S(1)} collective-permute-done((f32[256,256]{1,0:T(8,128)S(1)}, f32[256,256]{1,0:T(8,128)S(1)}, u32[]{:S(2)}, u32[]{:S(2)}) %collective-permute-start) | collective-permute-done | bytes 262176 | tf_op jit(solution)/shard_map/ppermute | solution.py:200
  60.7 0.6 shard_map.71
  61.3 1.9 %collective-permute-start.1 = (f32[128,256]{1,0:T(8,128)S(1)}, f32[128,256]{1,0:T(8,128)S(1)}, u32[]{:S(2)}, u32[]{:S(2)}) collective-permute-start(f32[128,256]{1,0:T(8,128)S(1)} %get-tuple-element.26), channel_id=1, source_target_pairs={{0,2},{1,3},{2,0},{3,1},{4,6},{5,7},{6,4},{7,5},{8,10},{9,11},{10,... | collective-permute-start | bytes 393224 | tf_op jit(solution)/shard_map/ppermute | solution.py:200
  63.3 5.5 %collective-permute-done.1.b = f32[128,256]{1,0:T(8,128)S(1)} collective-permute-done((f32[128,256]{1,0:T(8,128)S(1)}, f32[128,256]{1,0:T(8,128)S(1)}, u32[]{:S(2)}, u32[]{:S(2)}) %collective-permute-start.1) | collective-permute-done | bytes 131104 | tf_op jit(solution)/shard_map/ppermute | solution.py:200
  69.3 4.1 %all-to-all-done.1.refs_0_ = f32[32,16,256]{2,1,0:T(8,128)S(1)} async-done(((f32[32,16,256]{2,1,0:T(8,128)}), f32[32,16,256]{2,1,0:T(8,128)S(1)}, u32[]{:S(2)}, u32[]{:S(2)}) %all-to-all-start.1) | async-done | bytes 524320 | tf_op jit(solution)/shard_map/all_to_all | solution.py:191
  73.4 0.9 shard_map.73
  74.3 5.8 %all-to-all-start.2 = ((f32[32,16,256]{2,1,0:T(8,128)}), f32[32,16,256]{2,1,0:T(8,128)S(1)}, u32[]{:S(2)}, u32[]{:S(2)}) async-start(f32[32,16,256]{2,1,0:T(8,128)} %shard_map.73), calls=%async_computation.2 | async-start | bytes 1048576 | tf_op jit(solution)/shard_map/all_to_all | solution.py:191
  80.1 3.4 %collective-permute-start.2 = (f32[32,256]{1,0:T(8,128)S(1)}, f32[32,256]{1,0:T(8,128)S(1)}, u32[]{:S(2)}, u32[]{:S(2)}) collective-permute-start(f32[32,256]{1,0:T(8,128)S(1)} %get-tuple-element.28), channel_id=1, source_target_pairs={{0,8},{1,9},{2,10},{3,11},{4,12},{5,13},{6,14},{7,15},{8,0},{9,1},... | collective-permute-start | bytes 98312 | tf_op jit(solution)/shard_map/ppermute | solution.py:200
  83.5 3.1 %collective-permute-start.3 = (f32[32,256]{1,0:T(8,128)S(1)}, f32[32,256]{1,0:T(8,128)S(1)}, u32[]{:S(2)}, u32[]{:S(2)}) collective-permute-start(f32[32,256]{1,0:T(8,128)S(1)} %get-tuple-element.29), channel_id=1, source_target_pairs={{0,4},{1,5},{2,6},{3,7},{4,8},{5,9},{6,10},{7,11},{8,12},{9,13},{1... | collective-permute-start | bytes 98312 | tf_op jit(solution)/shard_map/ppermute | solution.py:200
  86.5 4.9 %collective-permute-start.4 = (f32[32,256]{1,0:T(8,128)S(1)}, f32[32,256]{1,0:T(8,128)S(1)}, u32[]{:S(2)}, u32[]{:S(2)}) collective-permute-start(f32[32,256]{1,0:T(8,128)S(1)} %get-tuple-element.30), channel_id=1, source_target_pairs={{0,12},{1,13},{2,14},{3,15},{4,0},{5,1},{6,2},{7,3},{8,4},{9,5},{1... | collective-permute-start | bytes 98312 | tf_op jit(solution)/shard_map/ppermute | solution.py:200
  91.4 2.9 %collective-permute-done.4.refs_3_ = f32[32,256]{1,0:T(8,128)S(1)} collective-permute-done((f32[32,256]{1,0:T(8,128)S(1)}, f32[32,256]{1,0:T(8,128)S(1)}, u32[]{:S(2)}, u32[]{:S(2)}) %collective-permute-start.4) | collective-permute-done | bytes 32800 | tf_op jit(solution)/shard_map/ppermute | solution.py:200
  94.3 0.6 shard_map.74
  94.9 1.9 %all-to-all-done.2 = f32[32,16,256]{2,1,0:T(8,128)S(1)} async-done(((f32[32,16,256]{2,1,0:T(8,128)}), f32[32,16,256]{2,1,0:T(8,128)S(1)}, u32[]{:S(2)}, u32[]{:S(2)}) %all-to-all-start.2) | async-done | bytes 524320 | tf_op jit(solution)/shard_map/all_to_all | solution.py:191
  96.8 0.8 copy.8
  (10 shorter events, 0.7 us)
Async XLA Ops:
  0.6 26.5 %copy-start = (f32[512,256]{1,0:T(8,128)S(1)}, f32[512,256]{1,0:T(8,128)}, u32[]{:S(2)}) copy-start(f32[512,256]{1,0:T(8,128)} %users.3) | copy-start | bytes 1572868
  0.6 0.8 copy-start.1
  1.5 0.7 copy-start.3
  27.1 0.7 copy-start.2
  52.1 21.3 %all-to-all-start.1 = ((f32[32,16,256]{2,1,0:T(8,128)}), f32[32,16,256]{2,1,0:T(8,128)S(1)}, u32[]{:S(2)}, u32[]{:S(2)}) async-start(f32[32,16,256]{2,1,0:T(8,128)} %bitcast.6), calls=%async_computation.1 | async-start | bytes 1048576 | tf_op jit(solution)/shard_map/all_to_all | solution.py:191
  57.3 3.4 %collective-permute-start = (f32[256,256]{1,0:T(8,128)S(1)}, f32[256,256]{1,0:T(8,128)S(1)}, u32[]{:S(2)}, u32[]{:S(2)}) collective-permute-start(f32[256,256]{1,0:T(8,128)S(1)} %get-tuple-element.24), channel_id=1, source_target_pairs={{0,1},{1,0},{2,3},{3,2},{4,5},{5,4},{6,7},{7,6},{8,9},{9,8},{10,11... | collective-permute-start | bytes 786440 | tf_op jit(solution)/shard_map/ppermute | solution.py:200
  61.3 7.4 %collective-permute-start.1 = (f32[128,256]{1,0:T(8,128)S(1)}, f32[128,256]{1,0:T(8,128)S(1)}, u32[]{:S(2)}, u32[]{:S(2)}) collective-permute-start(f32[128,256]{1,0:T(8,128)S(1)} %get-tuple-element.26), channel_id=1, source_target_pairs={{0,2},{1,3},{2,0},{3,1},{4,6},{5,7},{6,4},{7,5},{8,10},{9,11},{10,... | collective-permute-start | bytes 393224 | tf_op jit(solution)/shard_map/ppermute | solution.py:200
  74.3 22.5 %all-to-all-start.2 = ((f32[32,16,256]{2,1,0:T(8,128)}), f32[32,16,256]{2,1,0:T(8,128)S(1)}, u32[]{:S(2)}, u32[]{:S(2)}) async-start(f32[32,16,256]{2,1,0:T(8,128)} %shard_map.73), calls=%async_computation.2 | async-start | bytes 1048576 | tf_op jit(solution)/shard_map/all_to_all | solution.py:191
  80.1 11.3 %collective-permute-start.2 = (f32[32,256]{1,0:T(8,128)S(1)}, f32[32,256]{1,0:T(8,128)S(1)}, u32[]{:S(2)}, u32[]{:S(2)}) collective-permute-start(f32[32,256]{1,0:T(8,128)S(1)} %get-tuple-element.28), channel_id=1, source_target_pairs={{0,8},{1,9},{2,10},{3,11},{4,12},{5,13},{6,14},{7,15},{8,0},{9,1},... | collective-permute-start | bytes 98312 | tf_op jit(solution)/shard_map/ppermute | solution.py:200
  83.5 8.0 %collective-permute-start.3 = (f32[32,256]{1,0:T(8,128)S(1)}, f32[32,256]{1,0:T(8,128)S(1)}, u32[]{:S(2)}, u32[]{:S(2)}) collective-permute-start(f32[32,256]{1,0:T(8,128)S(1)} %get-tuple-element.29), channel_id=1, source_target_pairs={{0,4},{1,5},{2,6},{3,7},{4,8},{5,9},{6,10},{7,11},{8,12},{9,13},{1... | collective-permute-start | bytes 98312 | tf_op jit(solution)/shard_map/ppermute | solution.py:200
  86.5 7.8 %collective-permute-start.4 = (f32[32,256]{1,0:T(8,128)S(1)}, f32[32,256]{1,0:T(8,128)S(1)}, u32[]{:S(2)}, u32[]{:S(2)}) collective-permute-start(f32[32,256]{1,0:T(8,128)S(1)} %get-tuple-element.30), channel_id=1, source_target_pairs={{0,12},{1,13},{2,14},{3,15},{4,0},{5,1},{6,2},{7,3},{8,4},{9,5},{1... | collective-permute-start | bytes 98312 | tf_op jit(solution)/shard_map/ppermute | solution.py:200

commit v9 on v8

--- a/solution.py
+++ b/solution.py
@@ -1,3 +1,5 @@
+import functools
+
 import jax
 import jax.numpy as jnp
 from jax import lax
@@ -149,10 +151,9 @@
     user_part[...] = dot_split(split(grad[...]), split(items[...]), 0, 0)
 
 
-def item_body(users, grad, mine, theirs):
-    right = split(users[...])
-    theirs[...] = dot_split(split(grad[HALF:SLAB, :]), right, 1, 0)
-    mine[...] = dot_split(split(grad[0:HALF, :]), right, 1, 0)
+def item_body(part, users, grad, out):
+    rows = grad[HALF * part:HALF * (part + 1), :]
+    out[...] = dot_split(split(rows), split(users[...]), 1, 0)
 
 
 def add_spread_body(parts, out):
@@ -218,7 +219,10 @@
         (place, items, positive, scores, stats), scalars=1, flops=product,
     )
     parts = exchange(user_part.reshape(GROUPS, SHARE, E), PEERS)
-    mine, theirs = call(item_body, (f32(HALF, E), f32(HALF, E)), (user_vectors, grad), flops=product)
+    mine, theirs = (
+        call(functools.partial(item_body, part), f32(HALF, E), (user_vectors, grad), flops=product // 2)
+        for part in range(2)
+    )
     arrived = move(theirs, lambda z, c: (z, 1 - c))
     mine, theirs = call(
         halve_body, [f32(HALF // 2, E)] * 2, (place, mine, arrived), scalars=1,

time: 98.2 us -> 97.9 us (level)
    pallas_call x8 -> x9, Pallas kernels: 7.48 us -> 7.64 us  [call(): pl.pallas_call((lambda *refs: body(*refs[:last], *refs[last + len(after):...]
  transfers between devices with their start and end apart: 7 -> 7, of which waited for: 5 -> 5; matrix products, arithmetic and copies ran while one was open for 0% -> 0% of each run, Pallas kernels for 2% -> 3%
where the time goes in v9:
time: 97.9 us; the launch traced here: 97.4 us
  blocking collectives  45 us (46%)
  starting transfers between devices  25.3 us (26%)
  waiting for transfers between devices  15.7 us (16%)
  Pallas kernels  7.64 us (8%)
  local copies, waits for them, and re-layouts  2.86 us (3%)
    all_gather x1, blocking collectives, per_device(): packed = lax.all_gather(packed, USER_AXES, axis=0, tiled=True)  24.9 us
    all_to_all x1, blocking collectives, exchange(): return lax.all_to_all(value, axis, split_axis=0, concat_axis=0, tiled=True)  20.1 us
    ppermute x5, starting transfers between devices, move(): return lax.ppermute(value, USER_AXES, pairs)  15.1 us
    all_to_all x2, starting transfers between devices, exchange(): return lax.all_to_all(value, axis, split_axis=0, concat_axis=0, tiled=True)  10.2 us
    ppermute x5, waiting for transfers between devices, move(): return lax.ppermute(value, USER_AXES, pairs)  9.48 us
    pallas_call x9, Pallas kernels, call(): pl.pallas_call((lambda *refs: body(*refs[:last], *refs[last + len(after):...  7.64 us
    all_to_all x2, waiting for transfers between devices, exchange(): return lax.all_to_all(value, axis, split_axis=0, concat_axis=0, tiled=True)  6.21 us
    unnamed x9, local copies, waits for them, and re-layouts  2.86 us
  transfers between devices with their start and end apart: 7, of which 5 were waited for; matrix products, arithmetic and copies ran while one was open for 0% of the time, Pallas kernels for 3%

profile of v9, /device:TPU:8, one launch (start us, length us, event | category | flops | bytes accessed | tf_op | source)
XLA Modules:
  0.0 97.4 jit_solution(1087134742703450374)
XLA Ops:
  0.7 0.8 copy-done.1
  1.5 0.7 copy-done.3
  2.1 24.9 %all_gather.3.packed = f32[640,256]{1,0:T(8,128)S(1)} all-gather(f32[40,256]{1,0:T(8,128)S(1)} %shard_map.67), channel_id=1, replica_groups=mesh['x'=4,'y'=8,'z'=8,'core'=2] {'z','core'}, dimensions={0}, use_global_device_ids=true | all-gather | bytes 696320 | tf_op jit(solution)/shard_map/all_gather | solution.py:211
  27.1 0.6 copy-done.2
  27.7 1.9 %shard_map.68 = (f32[512,256]{1,0:T(8,128)S(1)}, f32[512,512]{1,0:T(8,128)S(1)}, f32[32,8,128]{2,1,0:T(8,128)S(1)}) custom-call(s32[3]{0:T(128)S(1)} %pad_add_fusion.place, f32[512,256]{1,0:T(8,128)S(1)} %copy-done, f32[640,256]{1,0:T(8,128)S(1)} %all_gather.3.packed, s32[1,512]{1,0:T(1,128)S(1)} %bitcast.8), custom_call_target="tpu_custom_call" | custom-call | flops 134217728 | bytes 2885644 | tf_op jit(solution)/shard_map/pallas_call | solution.py:42
  29.7 20.1 %all_to_all.15.stats = f32[32,8,128]{2,1,0:T(8,128)S(1)} all-to-all(f32[32,8,128]{2,1,0:T(8,128)S(1)} %get-tuple-element.17), channel_id=1, replica_groups=mesh['x'=4,'y'=8,'z'=8,'core'=2] {'y','x'}, dimensions={0} | all-to-all | bytes 262144 | tf_op jit(solution)/shard_map/all_to_all | solution.py:192
  49.8 2.3 %shard_map.69 = (f32[4,128]{1,0:T(4,128)}, f32[512,512]{1,0:T(8,128)S(1)}, f32[512,256]{1,0:T(8,128)}) custom-call(s32[3]{0:T(128)S(1)} %pad_add_fusion.place, f32[512,256]{1,0:T(8,128)S(1)} %get-tuple-element.15.items, s32[1,512]{1,0:T(1,128)S(1)} %bitcast.9, f32[512,512]{1,0:T(8,128)S(1)} %get-tuple-element.16.scores, f32[32,8,128]{2,1,0:T(8,128)S(1)} %all_to_all.15.stats), custom_call_target="tpu_custom_call" | custom-call | flops 134217728 | bytes 3280908 | tf_op jit(solution)/shard_map/pallas_call | solution.py:42
  52.1 4.6 %all-to-all-start.1 = ((f32[32,16,256]{2,1,0:T(8,128)}), f32[32,16,256]{2,1,0:T(8,128)S(1)}, u32[]{:S(2)}, u32[]{:S(2)}) async-start(f32[32,16,256]{2,1,0:T(8,128)} %bitcast.6), calls=%async_computation.1 | async-start | bytes 1048576 | tf_op jit(solution)/shard_map/all_to_all | solution.py:192
  57.1 1.9 %collective-permute-start = (f32[256,256]{1,0:T(8,128)S(1)}, f32[256,256]{1,0:T(8,128)S(1)}, u32[]{:S(2)}, u32[]{:S(2)}) collective-permute-start(f32[256,256]{1,0:T(8,128)S(1)} %shard_map.71), channel_id=1, source_target_pairs={{0,1},{1,0},{2,3},{3,2},{4,5},{5,4},{6,7},{7,6},{8,9},{9,8},{10,11... | collective-permute-start | bytes 786440 | tf_op jit(solution)/shard_map/ppermute | solution.py:201
  59.4 1.1 %collective-permute-done.b = f32[256,256]{1,0:T(8,128)S(1)} collective-permute-done((f32[256,256]{1,0:T(8,128)S(1)}, f32[256,256]{1,0:T(8,128)S(1)}, u32[]{:S(2)}, u32[]{:S(2)}) %collective-permute-start) | collective-permute-done | bytes 262176 | tf_op jit(solution)/shard_map/ppermute | solution.py:201
  60.5 0.6 shard_map.72
  61.1 1.9 %collective-permute-start.1 = (f32[128,256]{1,0:T(8,128)S(1)}, f32[128,256]{1,0:T(8,128)S(1)}, u32[]{:S(2)}, u32[]{:S(2)}) collective-permute-start(f32[128,256]{1,0:T(8,128)S(1)} %get-tuple-element.22), channel_id=1, source_target_pairs={{0,2},{1,3},{2,0},{3,1},{4,6},{5,7},{6,4},{7,5},{8,10},{9,11},{10,... | collective-permute-start | bytes 393224 | tf_op jit(solution)/shard_map/ppermute | solution.py:201
  63.0 5.5 %collective-permute-done.1.b = f32[128,256]{1,0:T(8,128)S(1)} collective-permute-done((f32[128,256]{1,0:T(8,128)S(1)}, f32[128,256]{1,0:T(8,128)S(1)}, u32[]{:S(2)}, u32[]{:S(2)}) %collective-permute-start.1) | collective-permute-done | bytes 131104 | tf_op jit(solution)/shard_map/ppermute | solution.py:201
  68.5 0.6 shard_map.73
  69.1 4.3 %all-to-all-done.1.refs_0_ = f32[32,16,256]{2,1,0:T(8,128)S(1)} async-done(((f32[32,16,256]{2,1,0:T(8,128)}), f32[32,16,256]{2,1,0:T(8,128)S(1)}, u32[]{:S(2)}, u32[]{:S(2)}) %all-to-all-start.1) | async-done | bytes 524320 | tf_op jit(solution)/shard_map/all_to_all | solution.py:192
  73.4 0.9 shard_map.74
  74.3 5.6 %all-to-all-start.2 = ((f32[32,16,256]{2,1,0:T(8,128)}), f32[32,16,256]{2,1,0:T(8,128)S(1)}, u32[]{:S(2)}, u32[]{:S(2)}) async-start(f32[32,16,256]{2,1,0:T(8,128)} %shard_map.74), calls=%async_computation.2 | async-start | bytes 1048576 | tf_op jit(solution)/shard_map/all_to_all | solution.py:192
  79.9 3.4 %collective-permute-start.2 = (f32[32,256]{1,0:T(8,128)S(1)}, f32[32,256]{1,0:T(8,128)S(1)}, u32[]{:S(2)}, u32[]{:S(2)}) collective-permute-start(f32[32,256]{1,0:T(8,128)S(1)} %get-tuple-element.24), channel_id=1, source_target_pairs={{0,8},{1,9},{2,10},{3,11},{4,12},{5,13},{6,14},{7,15},{8,0},{9,1},... | collective-permute-start | bytes 98312 | tf_op jit(solution)/shard_map/ppermute | solution.py:201
  83.2 3.1 %collective-permute-start.3 = (f32[32,256]{1,0:T(8,128)S(1)}, f32[32,256]{1,0:T(8,128)S(1)}, u32[]{:S(2)}, u32[]{:S(2)}) collective-permute-start(f32[32,256]{1,0:T(8,128)S(1)} %get-tuple-element.25), channel_id=1, source_target_pairs={{0,4},{1,5},{2,6},{3,7},{4,8},{5,9},{6,10},{7,11},{8,12},{9,13},{1... | collective-permute-start | bytes 98312 | tf_op jit(solution)/shard_map/ppermute | solution.py:201
  86.3 4.9 %collective-permute-start.4 = (f32[32,256]{1,0:T(8,128)S(1)}, f32[32,256]{1,0:T(8,128)S(1)}, u32[]{:S(2)}, u32[]{:S(2)}) collective-permute-start(f32[32,256]{1,0:T(8,128)S(1)} %get-tuple-element.26), channel_id=1, source_target_pairs={{0,12},{1,13},{2,14},{3,15},{4,0},{5,1},{6,2},{7,3},{8,4},{9,5},{1... | collective-permute-start | bytes 98312 | tf_op jit(solution)/shard_map/ppermute | solution.py:201
  91.2 2.9 %collective-permute-done.4.refs_3_ = f32[32,256]{1,0:T(8,128)S(1)} collective-permute-done((f32[32,256]{1,0:T(8,128)S(1)}, f32[32,256]{1,0:T(8,128)S(1)}, u32[]{:S(2)}, u32[]{:S(2)}) %collective-permute-start.4) | collective-permute-done | bytes 32800 | tf_op jit(solution)/shard_map/ppermute | solution.py:201
  94.1 0.6 shard_map.75
  94.7 1.9 %all-to-all-done.2 = f32[32,16,256]{2,1,0:T(8,128)S(1)} async-done(((f32[32,16,256]{2,1,0:T(8,128)}), f32[32,16,256]{2,1,0:T(8,128)S(1)}, u32[]{:S(2)}, u32[]{:S(2)}) %all-to-all-start.2) | async-done | bytes 524320 | tf_op jit(solution)/shard_map/all_to_all | solution.py:192
  96.6 0.8 copy.8
  (11 shorter events, 0.9 us)
Async XLA Ops:
  0.6 26.5 %copy-start = (f32[512,256]{1,0:T(8,128)S(1)}, f32[512,256]{1,0:T(8,128)}, u32[]{:S(2)}) copy-start(f32[512,256]{1,0:T(8,128)} %users.5) | copy-start | bytes 1572868
  0.6 0.8 copy-start.1
  1.5 0.7 copy-start.3
  27.1 0.7 copy-start.2
  52.1 21.3 %all-to-all-start.1 = ((f32[32,16,256]{2,1,0:T(8,128)}), f32[32,16,256]{2,1,0:T(8,128)S(1)}, u32[]{:S(2)}, u32[]{:S(2)}) async-start(f32[32,16,256]{2,1,0:T(8,128)} %bitcast.6), calls=%async_computation.1 | async-start | bytes 1048576 | tf_op jit(solution)/shard_map/all_to_all | solution.py:192
  57.1 3.4 %collective-permute-start = (f32[256,256]{1,0:T(8,128)S(1)}, f32[256,256]{1,0:T(8,128)S(1)}, u32[]{:S(2)}, u32[]{:S(2)}) collective-permute-start(f32[256,256]{1,0:T(8,128)S(1)} %shard_map.71), channel_id=1, source_target_pairs={{0,1},{1,0},{2,3},{3,2},{4,5},{5,4},{6,7},{7,6},{8,9},{9,8},{10,11... | collective-permute-start | bytes 786440 | tf_op jit(solution)/shard_map/ppermute | solution.py:201
  61.1 7.4 %collective-permute-start.1 = (f32[128,256]{1,0:T(8,128)S(1)}, f32[128,256]{1,0:T(8,128)S(1)}, u32[]{:S(2)}, u32[]{:S(2)}) collective-permute-start(f32[128,256]{1,0:T(8,128)S(1)} %get-tuple-element.22), channel_id=1, source_target_pairs={{0,2},{1,3},{2,0},{3,1},{4,6},{5,7},{6,4},{7,5},{8,10},{9,11},{10,... | collective-permute-start | bytes 393224 | tf_op jit(solution)/shard_map/ppermute | solution.py:201
  74.3 22.3 %all-to-all-start.2 = ((f32[32,16,256]{2,1,0:T(8,128)}), f32[32,16,256]{2,1,0:T(8,128)S(1)}, u32[]{:S(2)}, u32[]{:S(2)}) async-start(f32[32,16,256]{2,1,0:T(8,128)} %shard_map.74), calls=%async_computation.2 | async-start | bytes 1048576 | tf_op jit(solution)/shard_map/all_to_all | solution.py:192
  79.9 11.3 %collective-permute-start.2 = (f32[32,256]{1,0:T(8,128)S(1)}, f32[32,256]{1,0:T(8,128)S(1)}, u32[]{:S(2)}, u32[]{:S(2)}) collective-permute-start(f32[32,256]{1,0:T(8,128)S(1)} %get-tuple-element.24), channel_id=1, source_target_pairs={{0,8},{1,9},{2,10},{3,11},{4,12},{5,13},{6,14},{7,15},{8,0},{9,1},... | collective-permute-start | bytes 98312 | tf_op jit(solution)/shard_map/ppermute | solution.py:201
  83.2 8.0 %collective-permute-start.3 = (f32[32,256]{1,0:T(8,128)S(1)}, f32[32,256]{1,0:T(8,128)S(1)}, u32[]{:S(2)}, u32[]{:S(2)}) collective-permute-start(f32[32,256]{1,0:T(8,128)S(1)} %get-tuple-element.25), channel_id=1, source_target_pairs={{0,4},{1,5},{2,6},{3,7},{4,8},{5,9},{6,10},{7,11},{8,12},{9,13},{1... | collective-permute-start | bytes 98312 | tf_op jit(solution)/shard_map/ppermute | solution.py:201
  86.3 7.8 %collective-permute-start.4 = (f32[32,256]{1,0:T(8,128)S(1)}, f32[32,256]{1,0:T(8,128)S(1)}, u32[]{:S(2)}, u32[]{:S(2)}) collective-permute-start(f32[32,256]{1,0:T(8,128)S(1)} %get-tuple-element.26), channel_id=1, source_target_pairs={{0,12},{1,13},{2,14},{3,15},{4,0},{5,1},{6,2},{7,3},{8,4},{9,5},{1... | collective-permute-start | bytes 98312 | tf_op jit(solution)/shard_map/ppermute | solution.py:201

commit v10 on v8

--- a/solution.py
+++ b/solution.py
@@ -227,7 +227,7 @@
     pieces = call(
         deal_body, [f32(OWN, E)] * (Z // 2), (place, mine, arrived), scalars=1,
     )
-    spread = call(add_spread_body, f32(GROUPS, SHARE, E), (parts,), after=(pieces[0],))
+    spread = call(add_spread_body, f32(GROUPS, SHARE, E), (parts,), after=(arrived,))
     user_grad = exchange(spread, PEERS).reshape(ROWS, E)
     terms = [pieces[0]]
     for r in (2, 1, 3):

time: 98.2 us -> 97.6 us (level)
  no operation moved by 1% of the time
where the time goes in v10:
time: 97.6 us; the launch traced here: 97 us
  blocking collectives  45 us (46%)
  starting transfers between devices  25 us (26%)
  waiting for transfers between devices  15.9 us (16%)
  Pallas kernels  7.48 us (8%)
  local copies, waits for them, and re-layouts  2.86 us (3%)
    all_gather x1, blocking collectives, per_device(): packed = lax.all_gather(packed, USER_AXES, axis=0, tiled=True)  24.9 us
    all_to_all x1, blocking collectives, exchange(): return lax.all_to_all(value, axis, split_axis=0, concat_axis=0, tiled=True)  20.1 us
    ppermute x5, starting transfers between devices, move(): return lax.ppermute(value, USER_AXES, pairs)  15.1 us
    ppermute x5, waiting for transfers between devices, move(): return lax.ppermute(value, USER_AXES, pairs)  9.87 us
    all_to_all x2, starting transfers between devices, exchange(): return lax.all_to_all(value, axis, split_axis=0, concat_axis=0, tiled=True)  9.84 us
    pallas_call x8, Pallas kernels, call(): pl.pallas_call((lambda *refs: body(*refs[:last], *refs[last + len(after):...  7.48 us
    all_to_all x2, waiting for transfers between devices, exchange(): return lax.all_to_all(value, axis, split_axis=0, concat_axis=0, tiled=True)  5.99 us
    unnamed x9, local copies, waits for them, and re-layouts  2.86 us
  transfers between devices with their start and end apart: 7, of which 5 were waited for; matrix products, arithmetic and copies ran while one was open for 0% of the time, Pallas kernels for 2%

profile of v10, /device:TPU:8, one launch (start us, length us, event | category | flops | bytes accessed | tf_op | source)
XLA Modules:
  0.0 97.0 jit_solution(449795390455977274)
XLA Ops:
  0.7 0.8 copy-done.1
  1.5 0.7 copy-done.3
  2.1 24.9 %all_gather.3.packed = f32[640,256]{1,0:T(8,128)S(1)} all-gather(f32[40,256]{1,0:T(8,128)S(1)} %shard_map.67), channel_id=1, replica_groups=mesh['x'=4,'y'=8,'z'=8,'core'=2] {'z','core'}, dimensions={0}, use_global_device_ids=true | all-gather | bytes 696320 | tf_op jit(solution)/shard_map/all_gather | solution.py:210
  27.1 0.6 copy-done.2
  27.7 1.9 %shard_map.68 = (f32[512,256]{1,0:T(8,128)S(1)}, f32[512,512]{1,0:T(8,128)S(1)}, f32[32,8,128]{2,1,0:T(8,128)S(1)}) custom-call(s32[3]{0:T(128)S(1)} %pad_add_fusion.place, f32[512,256]{1,0:T(8,128)S(1)} %copy-done, f32[640,256]{1,0:T(8,128)S(1)} %all_gather.3.packed, s32[1,512]{1,0:T(1,128)S(1)} %bitcast.8), custom_call_target="tpu_custom_call" | custom-call | flops 134217728 | bytes 2885644 | tf_op jit(solution)/shard_map/pallas_call | solution.py:40
  29.7 20.1 %all_to_all.15.stats = f32[32,8,128]{2,1,0:T(8,128)S(1)} all-to-all(f32[32,8,128]{2,1,0:T(8,128)S(1)} %get-tuple-element.19), channel_id=1, replica_groups=mesh['x'=4,'y'=8,'z'=8,'core'=2] {'y','x'}, dimensions={0} | all-to-all | bytes 262144 | tf_op jit(solution)/shard_map/all_to_all | solution.py:191
  49.8 2.3 %shard_map.69 = (f32[4,128]{1,0:T(4,128)}, f32[512,512]{1,0:T(8,128)S(1)}, f32[512,256]{1,0:T(8,128)}) custom-call(s32[3]{0:T(128)S(1)} %pad_add_fusion.place, f32[512,256]{1,0:T(8,128)S(1)} %get-tuple-element.17.items, s32[1,512]{1,0:T(1,128)S(1)} %bitcast.9, f32[512,512]{1,0:T(8,128)S(1)} %get-tuple-element.18.scores, f32[32,8,128]{2,1,0:T(8,128)S(1)} %all_to_all.15.stats), custom_call_target="tpu_custom_call" | custom-call | flops 134217728 | bytes 3280908 | tf_op jit(solution)/shard_map/pallas_call | solution.py:40
  52.1 4.6 %all-to-all-start.1 = ((f32[32,16,256]{2,1,0:T(8,128)}), f32[32,16,256]{2,1,0:T(8,128)S(1)}, u32[]{:S(2)}, u32[]{:S(2)}) async-start(f32[32,16,256]{2,1,0:T(8,128)} %bitcast.6), calls=%async_computation.1 | async-start | bytes 1048576 | tf_op jit(solution)/shard_map/all_to_all | solution.py:191
  56.7 0.6 shard_map.70
  57.3 1.9 %collective-permute-start = (f32[256,256]{1,0:T(8,128)S(1)}, f32[256,256]{1,0:T(8,128)S(1)}, u32[]{:S(2)}, u32[]{:S(2)}) collective-permute-start(f32[256,256]{1,0:T(8,128)S(1)} %get-tuple-element.24), channel_id=1, source_target_pairs={{0,1},{1,0},{2,3},{3,2},{4,5},{5,4},{6,7},{7,6},{8,9},{9,8},{10,11... | collective-permute-start | bytes 786440 | tf_op jit(solution)/shard_map/ppermute | solution.py:200
  59.2 1.5 %collective-permute-done.b = f32[256,256]{1,0:T(8,128)S(1)} collective-permute-done((f32[256,256]{1,0:T(8,128)S(1)}, f32[256,256]{1,0:T(8,128)S(1)}, u32[]{:S(2)}, u32[]{:S(2)}) %collective-permute-start) | collective-permute-done | bytes 262176 | tf_op jit(solution)/shard_map/ppermute | solution.py:200
  60.7 0.6 shard_map.71
  61.3 1.9 %collective-permute-start.1 = (f32[128,256]{1,0:T(8,128)S(1)}, f32[128,256]{1,0:T(8,128)S(1)}, u32[]{:S(2)}, u32[]{:S(2)}) collective-permute-start(f32[128,256]{1,0:T(8,128)S(1)} %get-tuple-element.25), channel_id=1, source_target_pairs={{0,2},{1,3},{2,0},{3,1},{4,6},{5,7},{6,4},{7,5},{8,10},{9,11},{10,... | collective-permute-start | bytes 393224 | tf_op jit(solution)/shard_map/ppermute | solution.py:200
  63.3 5.5 %collective-permute-done.1.refs_1_.b = f32[128,256]{1,0:T(8,128)S(1)} collective-permute-done((f32[128,256]{1,0:T(8,128)S(1)}, f32[128,256]{1,0:T(8,128)S(1)}, u32[]{:S(2)}, u32[]{:S(2)}) %collective-permute-start.1) | collective-permute-done | bytes 131104 | tf_op jit(solution)/shard_map/ppermute | solution.py:200
  68.8 4.7 %all-to-all-done.1.refs_0_ = f32[32,16,256]{2,1,0:T(8,128)S(1)} async-done(((f32[32,16,256]{2,1,0:T(8,128)}), f32[32,16,256]{2,1,0:T(8,128)S(1)}, u32[]{:S(2)}, u32[]{:S(2)}) %all-to-all-start.1) | async-done | bytes 524320 | tf_op jit(solution)/shard_map/all_to_all | solution.py:191
  73.4 0.9 shard_map.72
  74.3 5.2 %all-to-all-start.2 = ((f32[32,16,256]{2,1,0:T(8,128)}), f32[32,16,256]{2,1,0:T(8,128)S(1)}, u32[]{:S(2)}, u32[]{:S(2)}) async-start(f32[32,16,256]{2,1,0:T(8,128)} %shard_map.72), calls=%async_computation.2 | async-start | bytes 1048576 | tf_op jit(solution)/shard_map/all_to_all | solution.py:191
  80.1 3.4 %collective-permute-start.2 = (f32[32,256]{1,0:T(8,128)S(1)}, f32[32,256]{1,0:T(8,128)S(1)}, u32[]{:S(2)}, u32[]{:S(2)}) collective-permute-start(f32[32,256]{1,0:T(8,128)S(1)} %get-tuple-element.28), channel_id=1, source_target_pairs={{0,8},{1,9},{2,10},{3,11},{4,12},{5,13},{6,14},{7,15},{8,0},{9,1},... | collective-permute-start | bytes 98312 | tf_op jit(solution)/shard_map/ppermute | solution.py:200
  83.4 3.1 %collective-permute-start.3 = (f32[32,256]{1,0:T(8,128)S(1)}, f32[32,256]{1,0:T(8,128)S(1)}, u32[]{:S(2)}, u32[]{:S(2)}) collective-permute-start(f32[32,256]{1,0:T(8,128)S(1)} %get-tuple-element.29), channel_id=1, source_target_pairs={{0,4},{1,5},{2,6},{3,7},{4,8},{5,9},{6,10},{7,11},{8,12},{9,13},{1... | collective-permute-start | bytes 98312 | tf_op jit(solution)/shard_map/ppermute | solution.py:200
  86.5 4.9 %collective-permute-start.4 = (f32[32,256]{1,0:T(8,128)S(1)}, f32[32,256]{1,0:T(8,128)S(1)}, u32[]{:S(2)}, u32[]{:S(2)}) collective-permute-start(f32[32,256]{1,0:T(8,128)S(1)} %get-tuple-element.30), channel_id=1, source_target_pairs={{0,12},{1,13},{2,14},{3,15},{4,0},{5,1},{6,2},{7,3},{8,4},{9,5},{1... | collective-permute-start | bytes 98312 | tf_op jit(solution)/shard_map/ppermute | solution.py:200
  91.4 2.9 %collective-permute-done.4.refs_3_ = f32[32,256]{1,0:T(8,128)S(1)} collective-permute-done((f32[32,256]{1,0:T(8,128)S(1)}, f32[32,256]{1,0:T(8,128)S(1)}, u32[]{:S(2)}, u32[]{:S(2)}) %collective-permute-start.4) | collective-permute-done | bytes 32800 | tf_op jit(solution)/shard_map/ppermute | solution.py:200
  94.3 0.6 shard_map.74
  94.9 1.3 %all-to-all-done.2 = f32[32,16,256]{2,1,0:T(8,128)S(1)} async-done(((f32[32,16,256]{2,1,0:T(8,128)}), f32[32,16,256]{2,1,0:T(8,128)S(1)}, u32[]{:S(2)}, u32[]{:S(2)}) %all-to-all-start.2) | async-done | bytes 524320 | tf_op jit(solution)/shard_map/all_to_all | solution.py:191
  96.2 0.8 copy.8
  (10 shorter events, 0.7 us)
Async XLA Ops:
  0.6 26.5 %copy-start = (f32[512,256]{1,0:T(8,128)S(1)}, f32[512,256]{1,0:T(8,128)}, u32[]{:S(2)}) copy-start(f32[512,256]{1,0:T(8,128)} %users.3) | copy-start | bytes 1572868
  0.6 0.8 copy-start.1
  1.5 0.7 copy-start.3
  27.1 0.7 copy-start.2
  52.1 21.3 %all-to-all-start.1 = ((f32[32,16,256]{2,1,0:T(8,128)}), f32[32,16,256]{2,1,0:T(8,128)S(1)}, u32[]{:S(2)}, u32[]{:S(2)}) async-start(f32[32,16,256]{2,1,0:T(8,128)} %bitcast.6), calls=%async_computation.1 | async-start | bytes 1048576 | tf_op jit(solution)/shard_map/all_to_all | solution.py:191
  57.3 3.4 %collective-permute-start = (f32[256,256]{1,0:T(8,128)S(1)}, f32[256,256]{1,0:T(8,128)S(1)}, u32[]{:S(2)}, u32[]{:S(2)}) collective-permute-start(f32[256,256]{1,0:T(8,128)S(1)} %get-tuple-element.24), channel_id=1, source_target_pairs={{0,1},{1,0},{2,3},{3,2},{4,5},{5,4},{6,7},{7,6},{8,9},{9,8},{10,11... | collective-permute-start | bytes 786440 | tf_op jit(solution)/shard_map/ppermute | solution.py:200
  61.3 7.4 %collective-permute-start.1 = (f32[128,256]{1,0:T(8,128)S(1)}, f32[128,256]{1,0:T(8,128)S(1)}, u32[]{:S(2)}, u32[]{:S(2)}) collective-permute-start(f32[128,256]{1,0:T(8,128)S(1)} %get-tuple-element.25), channel_id=1, source_target_pairs={{0,2},{1,3},{2,0},{3,1},{4,6},{5,7},{6,4},{7,5},{8,10},{9,11},{10,... | collective-permute-start | bytes 393224 | tf_op jit(solution)/shard_map/ppermute | solution.py:200
  74.3 21.9 %all-to-all-start.2 = ((f32[32,16,256]{2,1,0:T(8,128)}), f32[32,16,256]{2,1,0:T(8,128)S(1)}, u32[]{:S(2)}, u32[]{:S(2)}) async-start(f32[32,16,256]{2,1,0:T(8,128)} %shard_map.72), calls=%async_computation.2 | async-start | bytes 1048576 | tf_op jit(solution)/shard_map/all_to_all | solution.py:191
  80.1 11.3 %collective-permute-start.2 = (f32[32,256]{1,0:T(8,128)S(1)}, f32[32,256]{1,0:T(8,128)S(1)}, u32[]{:S(2)}, u32[]{:S(2)}) collective-permute-start(f32[32,256]{1,0:T(8,128)S(1)} %get-tuple-element.28), channel_id=1, source_target_pairs={{0,8},{1,9},{2,10},{3,11},{4,12},{5,13},{6,14},{7,15},{8,0},{9,1},... | collective-permute-start | bytes 98312 | tf_op jit(solution)/shard_map/ppermute | solution.py:200
  83.4 8.0 %collective-permute-start.3 = (f32[32,256]{1,0:T(8,128)S(1)}, f32[32,256]{1,0:T(8,128)S(1)}, u32[]{:S(2)}, u32[]{:S(2)}) collective-permute-start(f32[32,256]{1,0:T(8,128)S(1)} %get-tuple-element.29), channel_id=1, source_target_pairs={{0,4},{1,5},{2,6},{3,7},{4,8},{5,9},{6,10},{7,11},{8,12},{9,13},{1... | collective-permute-start | bytes 98312 | tf_op jit(solution)/shard_map/ppermute | solution.py:200
  86.5 7.8 %collective-permute-start.4 = (f32[32,256]{1,0:T(8,128)S(1)}, f32[32,256]{1,0:T(8,128)S(1)}, u32[]{:S(2)}, u32[]{:S(2)}) collective-permute-start(f32[32,256]{1,0:T(8,128)S(1)} %get-tuple-element.30), channel_id=1, source_target_pairs={{0,12},{1,13},{2,14},{3,15},{4,0},{5,1},{6,2},{7,3},{8,4},{9,5},{1... | collective-permute-start | bytes 98312 | tf_op jit(solution)/shard_map/ppermute | solution.py:200
